TPU v7x, 32 devices: a whole 2x2x4 slice. The times are simulated.
32 devices in a mesh: lon: 8 (over z, x), lat: 4 (over y, core).
Axes of the slice: x: 2, y: 2, z: 4, core: 2. Of those that a mesh axis runs over, the one named last changes fastest.
Arguments:
- inputs: bfloat16 [64, 128, 1024], P(None, 'lon', 'lat'), may hold values from -6 to 6
- weights: bfloat16 [2, 3, 3, 64, 64], replicated, may hold values from -0.25 to 0.25
- biases: float32 [2, 64], replicated, may hold values from -0.5 to 0.5
- cotangent: bfloat16 [64, 128, 1024], P(None, 'lon', 'lat'), may hold values from -6 to 6
Outputs:
- features_out: bfloat16 [64, 128, 1024], P(None, 'lon', 'lat')
- grad_input: bfloat16 [64, 128, 1024], P(None, 'lon', 'lat')
- weight_grads: float32 [2, 3, 3, 64, 64], replicated
- bias_grads: float32 [2, 64], replicated
All inputs are finite; a program needn't handle non-finite values.
Results may differ from a plain program's by a relative error of at most 0.012.
Values may be sent and summed in bfloat16 or wider, within the bound.
No kernel may reach another device: no remote copies, remote signals or barrier semaphores. Data moves between devices by JAX's collectives and lax.ppermute only.
A program may use at most 64 MiB of HBM per device.

v0:
```python
import functools
import math

import jax
import jax.numpy as jnp
from jax import lax
from jax.experimental import pallas as pl
from jax.experimental.pallas import tpu as pltpu
from jax.sharding import PartitionSpec as P


AXES = ("lon", "lat")
LANES = 128
TAIL = 64
QUARTERS = (2, 1, 3)
BF16, F32 = jnp.bfloat16, jnp.float32
PARAMS = pltpu.CompilerParams(vmem_limit_bytes=24 * 2**20)
MIDDLE = pltpu.CompilerParams(vmem_limit_bytes=207 * 2**18)
WIDE = pltpu.CompilerParams(vmem_limit_bytes=56 * 2**20)


def lane_order(cols, lat_rows, share, inverse):
    steps = lat_rows // cols
    place = lax.broadcasted_iota(jnp.int32, (lat_rows, lat_rows), 0 if inverse else 1)
    source = lax.broadcasted_iota(jnp.int32, (lat_rows, lat_rows), 1 if inverse else 0)
    group = lax.div(source & (cols - 1), share)
    wanted = (group * steps + lax.div(source, cols)) * share + (source & (share - 1))
    return (place == wanted).astype(F32).astype(BF16)


def row_order(outer, inner):
    rows = outer * inner
    place = lax.broadcasted_iota(jnp.int32, (rows, rows), 0)
    source = lax.broadcasted_iota(jnp.int32, (rows, rows), 1)
    wanted = (source & (inner - 1)) * outer + lax.div(source, inner)
    return (place == wanted).astype(F32).astype(BF16)


def product(left, right):
    return jnp.dot(left, right, preferred_element_type=F32)


def pack_kernel(share, x_ref, cot_ref, out_ref, buf, packed, in_sems, out_sems):
    _, channels, cols, lat_rows = buf.shape
    devices, _, width = packed.shape
    groups = devices // cols
    part = min(channels, 256 // cols)
    arrivals, departures = [], []
    for at, ref in enumerate((x_ref, cot_ref)):
        arrivals.append(pltpu.make_async_copy(ref, buf.at[at], in_sems.at[at]))
        rows = (slice(None), pl.ds(at * channels, channels), slice(None))
        departures.append(
            pltpu.make_async_copy(packed.at[rows], out_ref.at[rows], out_sems.at[at])
        )
        arrivals[at].start()
    lanes = lane_order(cols, lat_rows, share, False)
    order = row_order(part, cols)
    for at in range(2):
        arrivals[at].wait()
        for first in range(0, channels, part):
            rows = buf[at, first : first + part].reshape(part * cols, lat_rows)
            rows = product(order, rows).astype(BF16)
            rows = product(rows, lanes).astype(BF16)
            start = at * channels + first
            for col in range(cols):
                for group in range(groups):
                    packed[col * groups + group, start : start + part, :] = rows[
                        col * part : (col + 1) * part, group * width : (group + 1) * width
                    ]
        departures[at].start()
    for departure in departures:
        departure.wait()


def unpack_kernel(share, parts_ref, feat_ref, grad_ref, buf, sems):
    _, channels, cols, lat_rows = buf.shape
    devices, _, width = parts_ref.shape
    groups = devices // cols
    part = min(channels, 256 // cols)
    lanes = lane_order(cols, lat_rows, share, True)
    order = row_order(cols, part)
    departures = []
    for at, out_ref in enumerate((feat_ref, grad_ref)):
        for first in range(0, channels, part):
            start = at * channels + first
            rows = [
                jnp.concatenate(
                    [
                        parts_ref[col * groups + group, start : start + part, :]
                        for group in range(groups)
                    ],
                    axis=1,
                )
                for col in range(cols)
            ]
            rows = product(jnp.concatenate(rows, axis=0), lanes).astype(BF16)
            rows = product(order, rows).astype(BF16)
            buf[at, first : first + part] = rows.reshape(part, cols, lat_rows)
            rows = pl.ds(first, part)
            departures.append(
                pltpu.make_async_copy(buf.at[at, rows], out_ref.at[rows], sems.at[len(departures)])
            )
            departures[-1].start()
    for departure in departures:
        departure.wait()


def taps(row, shift):
    edge = jnp.zeros((row.shape[0], shift), row.dtype)
    before = jnp.concatenate([edge, row[:, :-shift]], axis=1)
    after = jnp.concatenate([row[:, shift:], edge], axis=1)
    return before, row, after


def line_of(parts_ref, count, channels, field, i):
    blocks = parts_ref.shape[0] // count
    rows = slice(field * channels, (field + 1) * channels)
    return jnp.concatenate([parts_ref[i * blocks + k, rows, :] for k in range(blocks)], axis=1)


def stack_kernel(
    share,
    parts_ref,
    w_ref,
    b_ref,
    out_ref,
    kept_ref,
    h_ref,
    gz0_ref,
    gz1_ref,
    s0_ref,
    s1_ref,
    y_ref,
    fields_ref,
    sems,
):
    count = h_ref.shape[0]
    channels = w_ref.shape[-1]
    devices, _, width = parts_ref.shape
    blocks = devices // count
    copies = []

    def put(field, i, line):
        rows = slice(field * channels, (field + 1) * channels)
        for k in range(blocks):
            fields_ref[i * blocks + k, rows, :] = line[:, k * width : (k + 1) * width]

    def copy(source, target):
        copies.append(pltpu.make_async_copy(source, target, sems.at[len(copies)]))
        copies[-1].start()

    def send(field, i, lines):
        place = (pl.ds(i * blocks, lines * blocks), pl.ds(field * channels, channels))
        copy(fields_ref.at[place], out_ref.at[place])

    for layer in range(2):
        hops = 2**layer
        kernel = jnp.concatenate(
            [
                jnp.concatenate([w_ref[layer, a, b] for b in range(3)], axis=1)
                for a in range(3)
            ],
            axis=0,
        )
        for i in range(count):
            line = line_of(parts_ref, count, channels, 0, i) if layer == 0 else h_ref[i]
            stack = jnp.concatenate(taps(line, hops * share), axis=0)
            y_ref[i] = jnp.dot(kernel, stack, preferred_element_type=F32)
        bias = b_ref[layer]
        for i in range(count):
            pre = bias + y_ref[i, channels : 2 * channels]
            pre = pre + y_ref[(i - hops) % count, :channels]
            pre = pre + y_ref[(i + hops) % count, 2 * channels :]
            sigma = 1.0 / (1.0 + jnp.exp(-pre))
            state = (pre * sigma).astype(BF16)
            slope = sigma * (1.0 + pre * (1.0 - sigma))
            if layer == 0:
                h_ref[i] = state
                s0_ref[i] = slope
            else:
                s1_ref[i] = slope
                put(0, i, state)
        if layer == 0:
            copy(h_ref, kept_ref.at[0])
    send(0, 0, count)

    for layer in (1, 0):
        hops = 2**layer
        kernel = jnp.concatenate(
            [
                jnp.concatenate([w_ref[layer, a, b].astype(F32).T for b in range(3)], axis=1)
                for a in range(3)
            ],
            axis=0,
        ).astype(BF16)
        for i in range(count):
            if layer == 1:
                gated = line_of(parts_ref, count, channels, 1, i).astype(F32) * s1_ref[i]
                gated = gated.astype(BF16)
                gz1_ref[i] = gated
            else:
                gated = gz0_ref[i]
            before, here, after = taps(gated, hops * share)
            stack = jnp.concatenate([after, here, before], axis=0)
            y_ref[i] = jnp.dot(kernel, stack, preferred_element_type=F32)
        for i in range(count):
            g = y_ref[i, channels : 2 * channels]
            g = g + y_ref[(i + hops) % count, :channels]
            g = g + y_ref[(i - hops) % count, 2 * channels :]
            g = g.astype(BF16)
            if layer == 1:
                gz0_ref[i] = (g.astype(F32) * s0_ref[i]).astype(BF16)
            else:
                put(1, i, g)
                send(1, i, 1)
        if layer == 1:
            copy(gz1_ref, kept_ref.at[1])
            copy(gz0_ref, kept_ref.at[2])
    for started in copies:
        started.wait()


def quarters():
    lat = lax.axis_index("lat")
    odd, upper = lat & 1, lax.div(lat, 2) & 1
    mine = 2 * odd + upper
    other = 2 * (1 - odd) + upper
    return mine, 2 * odd + 1 - upper, other, 2 * (1 - odd) + 1 - upper


def sums_kernel(share, parts_ref, kept_ref, keep_ref, *refs):
    send_refs, (buf, total_ref, sems) = refs[:3], refs[3:]
    _, count, channels, span = buf.shape
    h_ref, gz1_ref, gz0_ref = buf.at[0], buf.at[1], buf.at[2]
    copies = [pltpu.make_async_copy(kept_ref.at[k], buf.at[k], sems.at[k]) for k in range(3)]
    for copy in copies:
        copy.start()
    copies[0].wait()
    copies[1].wait()
    ones = jnp.ones((16, span), BF16)
    high = 3 * channels
    bias_rows = [None, None]
    for layer, gz_ref in ((1, gz1_ref), (0, gz0_ref)):
        hops = 2**layer
        if layer == 0:
            copies[2].wait()
        total = jnp.zeros((high, high), F32)
        bias = jnp.zeros((16, channels), F32)
        for i in range(count):
            gated = gz_ref[i]
            bias = bias + lax.dot_general(
                ones, gated, (((1,), (1,)), ((), ())), preferred_element_type=F32
            )
            before, here, after = taps(gated, hops * share)
            stack = jnp.concatenate([after, here, before], axis=0)
            around = [(i + (a - 1) * hops) % count for a in range(3)]
            lines = [
                line_of(parts_ref, count, channels, 0, j) if layer == 0 else h_ref[j]
                for j in around
            ]
            total = total + lax.dot_general(
                stack,
                jnp.concatenate(lines, axis=0),
                (((1,), (1,)), ((), ())),
                preferred_element_type=F32,
            )
        total_ref[layer * high : (layer + 1) * high, :] = total[:, : 2 * channels]
        total_ref[2 * high : 3 * high, layer * channels : (layer + 1) * channels] = total[
            :, 2 * channels :
        ]
        bias_rows[layer] = bias[:1]
    bias = jnp.concatenate(bias_rows, axis=1)
    row = lax.broadcasted_iota(jnp.int32, (TAIL, 2 * channels), 0)
    total_ref[3 * high :, :] = jnp.where(row == 0, bias, 0.0)
    size = keep_ref.shape[0]
    for at, quarter in enumerate(quarters()):
        rows = total_ref[pl.ds(pl.multiple_of(quarter * size, 16), size), :]
        if at == 0:
            keep_ref[...] = rows
        else:
            send_refs[at - 1][...] = rows.astype(BF16)


def assemble_kernel(scale, *refs):
    quarter_refs, (out_ref, bias_ref, total_ref) = refs[:4], refs[4:]
    channels = out_ref.shape[-1]
    size = quarter_refs[0].shape[0]
    for quarter, ref in zip(quarters(), quarter_refs):
        rows = ref[...].astype(F32) * scale
        total_ref[pl.ds(pl.multiple_of(quarter * size, 16), size), :] = rows
    high = 3 * channels
    for layer in range(2):
        for b in range(3):
            first = layer * high + b * channels
            pair = total_ref[first : first + channels, :]
            out_ref[layer, 0, b] = pair[:, :channels]
            out_ref[layer, 1, b] = pair[:, channels:]
            first = 2 * high + b * channels
            third = total_ref[first : first + channels, :]
            out_ref[layer, 2, b] = third[:, layer * channels : (layer + 1) * channels]
    bias = total_ref[3 * high : 3 * high + 1, :]
    bias_ref[0:1, :] = bias[:, :channels]
    bias_ref[1:2, :] = bias[:, channels:]


def partnered(block, devices, bit):
    return lax.ppermute(block, AXES, [(i, i ^ bit) for i in range(devices)])


def added(keep, sends, devices):
    came = [partnered(send, devices, bit).astype(F32) for send, bit in zip(sends, QUARTERS)]
    mine = (keep + came[0]) + (came[1] + came[2])
    low = 4
    while low < devices:
        high = 2 * low if 2 * low < devices else 0
        rounded = mine.astype(BF16)
        mine = rounded.astype(F32)
        if high:
            far = partnered(rounded, devices, high)
            across = partnered(rounded, devices, low + high)
            mine = mine + partnered(rounded, devices, low).astype(F32)
            mine = mine + (far.astype(F32) + across.astype(F32))
        else:
            mine = mine + partnered(rounded, devices, low).astype(F32)
        low *= 4
    return mine.astype(BF16)


def exchanged(parts):
    return lax.all_to_all(parts, AXES, 0, 0, tiled=True)


def local(inputs, weights, biases, cotangent):
    channels, cols, lat_rows = inputs.shape
    lons, lats = lax.axis_size("lon"), lax.axis_size("lat")
    devices = lons * lats
    share = cols * cols // devices
    width = lat_rows // cols * share
    span = lats * width
    scale = 1.0 / math.sqrt(cols * lons * lat_rows * lats)
    blocks = lats if width % LANES == 0 else 1
    shape = jax.ShapeDtypeStruct

    chunks = 2 * channels // min(channels, 256 // cols)
    fields_shape = (devices, 2 * channels, width)
    hbm = pl.BlockSpec(memory_space=pltpu.HBM)
    vmem = pl.BlockSpec(memory_space=pltpu.VMEM)

    packed = pl.pallas_call(
        functools.partial(pack_kernel, share),
        out_shape=shape(fields_shape, BF16),
        in_specs=[hbm, hbm],
        out_specs=hbm,
        scratch_shapes=[
            pltpu.VMEM((2,) + inputs.shape, BF16),
            pltpu.VMEM(fields_shape, BF16),
            pltpu.SemaphoreType.DMA((2,)),
            pltpu.SemaphoreType.DMA((2,)),
        ],
        compiler_params=WIDE,
    )(inputs, cotangent)
    parts = exchanged(packed)
    if blocks == 1:
        parts = parts.reshape(lons, lats, 2 * channels, width).transpose(0, 2, 1, 3)
        parts = parts.reshape(lons, 2 * channels, span)

    cells = (lons, channels, span)
    fields, kept = pl.pallas_call(
        functools.partial(stack_kernel, share),
        out_shape=[shape(parts.shape, BF16), shape((3,) + cells, BF16)],
        out_specs=[hbm, hbm],
        scratch_shapes=[
            pltpu.VMEM(cells, BF16),
            pltpu.VMEM(cells, BF16),
            pltpu.VMEM(cells, BF16),
            pltpu.VMEM(cells, F32),
            pltpu.VMEM(cells, F32),
            pltpu.VMEM((lons, 3 * channels, span), F32),
            pltpu.VMEM(parts.shape, BF16),
            pltpu.SemaphoreType.DMA((lons + 4,)),
        ],
        compiler_params=MIDDLE,
    )(parts, weights, biases[:, :, None])
    if blocks == 1:
        fields = fields.reshape(lons, 2 * channels, lats, width).transpose(0, 2, 1, 3)
        fields = fields.reshape(fields_shape)
    home = exchanged(fields)

    rows = 9 * channels + TAIL
    quarter_shape = (rows // 4, 2 * channels)
    flops = 2 * 2 * 9 * channels * parts.size // 2
    keep, *sends = pl.pallas_call(
        functools.partial(sums_kernel, share),
        out_shape=[shape(quarter_shape, F32)] + [shape(quarter_shape, BF16)] * 3,
        in_specs=[vmem, hbm],
        scratch_shapes=[
            pltpu.VMEM((3,) + cells, BF16),
            pltpu.VMEM((rows, 2 * channels), F32),
            pltpu.SemaphoreType.DMA((3,)),
        ],
        compiler_params=PARAMS,
        cost_estimate=pl.CostEstimate(flops=flops, bytes_accessed=5 * parts.size, transcendentals=0),
    )(parts, kept)
    mine = added(keep, sends, devices)
    home, mine = lax.optimization_barrier((home, mine))
    others = [partnered(mine, devices, bit) for bit in QUARTERS]
    features_out, grad_input = pl.pallas_call(
        functools.partial(unpack_kernel, share),
        out_shape=[shape(inputs.shape, BF16), shape(inputs.shape, BF16)],
        out_specs=[hbm, hbm],
        scratch_shapes=[
            pltpu.VMEM((2,) + inputs.shape, BF16),
            pltpu.SemaphoreType.DMA((chunks,)),
        ],
        compiler_params=PARAMS,
        cost_estimate=pl.CostEstimate(
            flops=4 * inputs.size * lat_rows, bytes_accessed=8 * inputs.size, transcendentals=0
        ),
    )(home)
    weight_grads, bias_grads = pl.pallas_call(
        functools.partial(assemble_kernel, scale),
        out_shape=[shape(weights.shape, F32), shape(biases.shape, F32)],
        scratch_shapes=[pltpu.VMEM((rows, 2 * channels), F32)],
        compiler_params=PARAMS,
    )(mine, *others)
    return features_out, grad_input, weight_grads, bias_grads


def solution(mesh):
    in_specs = (P(None, "lon", "lat"), P(), P(), P(None, "lon", "lat"))
    out_specs = (P(None, "lon", "lat"), P(None, "lon", "lat"), P(), P())
    return jax.shard_map(local, mesh=mesh, in_specs=in_specs, out_specs=out_specs, check_vma=False)
```

profile of v0, /device:TPU:0, one launch (start us, length us, event | category | flops | bytes accessed | tf_op | source)
XLA Modules:
  0.0 82.0 jit_solution(16088404659450754572)
XLA Ops:
  0.6 3.0 %shard_map.75 = bf16[32,128,128]{2,1,0:T(8,128)(2,1)} custom-call(bf16[64,16,256]{2,1,0:T(8,128)(2,1)} %x_ref.1, bf16[64,16,256]{2,1,0:T(8,128)(2,1)} %cot_ref.1), custom_call_target="tpu_custom_call" | custom-call | tf_op jit(solution)/shard_map/pallas_call | solution.py:349
  3.6 0.0 copy-start.4
  3.6 0.0 copy-start.3
  3.6 7.3 %all-to-all-start = ((bf16[32,128,128]{2,1,0:T(8,128)(2,1)}), bf16[32,128,128]{2,1,0:T(8,128)(2,1)S(1)}, u32[]{:S(2)}, u32[]{:S(2)}) async-start(bf16[32,128,128]{2,1,0:T(8,128)(2,1)} %shard_map.75), calls=%async_computation | async-start | bytes 2097152 | tf_op jit(solution)/shard_map/all_to_all | solution.py:330
  10.9 0.0 copy-done.4
  11.0 0.1 copy.8.b_ref
  11.1 26.1 %all-to-all-done.parts_ref = bf16[32,128,128]{2,1,0:T(8,128)(2,1)S(1)} async-done(((bf16[32,128,128]{2,1,0:T(8,128)(2,1)}), bf16[32,128,128]{2,1,0:T(8,128)(2,1)S(1)}, u32[]{:S(2)}, u32[]{:S(2)}) %all-to-all-start) | async-done | bytes 1048608 | tf_op jit(solution)/shard_map/all_to_all | solution.py:330
  37.2 0.0 copy-start
  37.2 1.0 %copy-done = bf16[32,128,128]{2,1,0:T(8,128)(2,1)} copy-done((bf16[32,128,128]{2,1,0:T(8,128)(2,1)}, bf16[32,128,128]{2,1,0:T(8,128)(2,1)S(1)}, u32[]{:S(2)}) %copy-start) | copy-done | bytes 1048600
  38.2 0.0 copy-done.3
  38.2 5.4 %shard_map.76 = (bf16[32,128,128]{2,1,0:T(8,128)(2,1)}, bf16[3,8,64,512]{3,2,1,0:T(8,128)(2,1)}) custom-call(bf16[32,128,128]{2,1,0:T(8,128)(2,1)} %copy-done, bf16[2,3,3,64,64]{4,3,2,1,0:T(8,128)(2,1)S(1)} %copy-done.3, f32[2,64,1]{2,1,0:T(8,128)S(1)} %copy.8.b_ref), custom_call_target="tpu_custom_call" | custom-call | tf_op jit(solution)/shard_map/pallas_call | solution.py:368
  43.6 0.0 copy-start.1
  43.6 3.6 %all-to-all-start.1 = ((bf16[32,128,128]{2,1,0:T(8,128)(2,1)}), bf16[32,128,128]{2,1,0:T(8,128)(2,1)S(1)}, u32[]{:S(2)}, u32[]{:S(2)}) async-start(bf16[32,128,128]{2,1,0:T(8,128)(2,1)} %get-tuple-element.16), calls=%async_computation.1 | async-start | bytes 2097152 | tf_op jit(solution)/shard_map/all_to_all | solution.py:330
  47.2 0.0 copy-done.1
  47.2 0.0 copy-start.2
  47.2 1.4 %copy-done.2 = bf16[3,8,64,512]{3,2,1,0:T(8,128)(2,1)S(1)} copy-done((bf16[3,8,64,512]{3,2,1,0:T(8,128)(2,1)S(1)}, bf16[3,8,64,512]{3,2,1,0:T(8,128)(2,1)}, u32[]{:S(2)}) %copy-start.2) | copy-done | bytes 1572888
  48.6 2.3 %shard_map.77 = (f32[160,128]{1,0:T(8,128)S(1)}, bf16[160,128]{1,0:T(8,128)(2,1)S(1)}, bf16[160,128]{1,0:T(8,128)(2,1)S(1)}, bf16[160,128]{1,0:T(8,128)(2,1)S(1)}) custom-call(bf16[32,128,128]{2,1,0:T(8,128)(2,1)S(1)} %copy-done.1, bf16[3,8,64,512]{3,2,1,0:T(8,128)(2,1)S(1)} %copy-done.2), custom_call_target="tpu_custom_call" | custom-call | flops 603979776 | bytes 2621440 | tf_op jit(solution)/shard_map/pallas_call | solution.py:392
  50.9 1.8 %collective-permute-start = (bf16[160,128]{1,0:T(8,128)(2,1)S(1)}, bf16[160,128]{1,0:T(8,128)(2,1)S(1)}, u32[]{:S(2)}, u32[]{:S(2)}) collective-permute-start(bf16[160,128]{1,0:T(8,128)(2,1)S(1)} %get-tuple-element.19), channel_id=1, source_target_pairs={{0,2},{1,3},{2,0},{3,1},{4,6},{5,7},{6,4},{7,5},{8,10},{9,11},{10,... | collective-permute-start | bytes 122888 | tf_op jit(solution)/shard_map/ppermute | solution.py:307
  52.8 0.0 collective-permute-start.1
  52.8 0.4 collective-permute-start.2
  53.2 4.9 %collective-permute-done = bf16[160,128]{1,0:T(8,128)(2,1)S(1)} collective-permute-done((bf16[160,128]{1,0:T(8,128)(2,1)S(1)}, bf16[160,128]{1,0:T(8,128)(2,1)S(1)}, u32[]{:S(2)}, u32[]{:S(2)}) %collective-permute-start) | collective-permute-done | bytes 40992 | tf_op jit(solution)/shard_map/ppermute | solution.py:307
  58.0 0.0 collective-permute-done.1
  58.0 1.6 %collective-permute-done.2 = bf16[160,128]{1,0:T(8,128)(2,1)S(1)} collective-permute-done((bf16[160,128]{1,0:T(8,128)(2,1)S(1)}, bf16[160,128]{1,0:T(8,128)(2,1)S(1)}, u32[]{:S(2)}, u32[]{:S(2)}) %collective-permute-start.2) | collective-permute-done | bytes 40992 | tf_op jit(solution)/shard_map/ppermute | solution.py:307
  59.7 0.1 collective-permute-start.5
  59.7 3.9 %collective-permute-start.4 = (bf16[160,128]{1,0:T(8,128)(2,1)S(1)}, bf16[160,128]{1,0:T(8,128)(2,1)S(1)}, u32[]{:S(2)}, u32[]{:S(2)}) collective-permute-start(bf16[160,128]{1,0:T(8,128)(2,1)S(1)} %add_convert_fusion.2), channel_id=1, source_target_pairs={{0,8},{1,9},{2,10},{3,11},{4,12},{5,13},{6,14},{7,15},{8,0},{9,1},... | collective-permute-start | bytes 122888 | tf_op jit(solution)/shard_map/ppermute | solution.py:307
  63.7 0.0 collective-permute-start.3
  63.7 2.4 %collective-permute-done.5 = bf16[160,128]{1,0:T(8,128)(2,1)S(1)} collective-permute-done((bf16[160,128]{1,0:T(8,128)(2,1)S(1)}, bf16[160,128]{1,0:T(8,128)(2,1)S(1)}, u32[]{:S(2)}, u32[]{:S(2)}) %collective-permute-start.5) | collective-permute-done | bytes 40992 | tf_op jit(solution)/shard_map/ppermute | solution.py:307
  66.0 2.2 %collective-permute-done.4 = bf16[160,128]{1,0:T(8,128)(2,1)S(1)} collective-permute-done((bf16[160,128]{1,0:T(8,128)(2,1)S(1)}, bf16[160,128]{1,0:T(8,128)(2,1)S(1)}, u32[]{:S(2)}, u32[]{:S(2)}) %collective-permute-start.4) | collective-permute-done | bytes 40992 | tf_op jit(solution)/shard_map/ppermute | solution.py:307
  68.3 0.0 collective-permute-done.3
  68.3 3.4 %collective-permute-start.6 = (bf16[160,128]{1,0:T(8,128)(2,1)S(1)}, bf16[160,128]{1,0:T(8,128)(2,1)S(1)}, u32[]{:S(2)}, u32[]{:S(2)}) collective-permute-start(bf16[160,128]{1,0:T(8,128)(2,1)S(1)} %add_convert_fusion.1), channel_id=1, source_target_pairs={{0,16},{1,17},{2,18},{3,19},{4,20},{5,21},{6,22},{7,23},{8,24},{9,... | collective-permute-start | bytes 122888 | tf_op jit(solution)/shard_map/ppermute | solution.py:307
  71.7 3.5 %collective-permute-done.6 = bf16[160,128]{1,0:T(8,128)(2,1)S(1)} collective-permute-done((bf16[160,128]{1,0:T(8,128)(2,1)S(1)}, bf16[160,128]{1,0:T(8,128)(2,1)S(1)}, u32[]{:S(2)}, u32[]{:S(2)}) %collective-permute-start.6) | collective-permute-done | bytes 40992 | tf_op jit(solution)/shard_map/ppermute | solution.py:307
  75.2 0.0 all-to-all-done.1.parts_ref
  75.2 0.8 %collective-permute-start.9 = (bf16[160,128]{1,0:T(8,128)(2,1)S(1)}, bf16[160,128]{1,0:T(8,128)(2,1)S(1)}, u32[]{:S(2)}, u32[]{:S(2)}) collective-permute-start(bf16[160,128]{1,0:T(8,128)(2,1)S(1)} %add_convert_fusion.refs_0_), channel_id=1, source_target_pairs={{0,3},{1,2},{2,1},{3,0},{4,7},{5,6},{6,5},{7,4},{8,11},{9,10},{10,... | collective-permute-start | bytes 122888 | tf_op jit(solution)/shard_map/ppermute | solution.py:307
  76.1 0.9 %collective-permute-start.8 = (bf16[160,128]{1,0:T(8,128)(2,1)S(1)}, bf16[160,128]{1,0:T(8,128)(2,1)S(1)}, u32[]{:S(2)}, u32[]{:S(2)}) collective-permute-start(bf16[160,128]{1,0:T(8,128)(2,1)S(1)} %add_convert_fusion.refs_0_), channel_id=1, source_target_pairs={{0,1},{1,0},{2,3},{3,2},{4,5},{5,4},{6,7},{7,6},{8,9},{9,8},{10,11... | collective-permute-start | bytes 122888 | tf_op jit(solution)/shard_map/ppermute | solution.py:307
  76.9 0.5 collective-permute-start.7
  77.4 1.6 %shard_map.78 = (bf16[64,16,256]{2,1,0:T(8,128)(2,1)}, bf16[64,16,256]{2,1,0:T(8,128)(2,1)}) custom-call(bf16[32,128,128]{2,1,0:T(8,128)(2,1)S(1)} %all-to-all-done.1.parts_ref), custom_call_target="tpu_custom_call" | custom-call | flops 268435456 | bytes 2097152 | tf_op jit(solution)/shard_map/pallas_call | solution.py:407
  79.1 0.0 collective-permute-done.9.refs_3_
  79.1 0.0 collective-permute-done.8.refs_2_
  79.1 1.9 %collective-permute-done.7.refs_1_ = bf16[160,128]{1,0:T(8,128)(2,1)S(1)} collective-permute-done((bf16[160,128]{1,0:T(8,128)(2,1)S(1)}, bf16[160,128]{1,0:T(8,128)(2,1)S(1)}, u32[]{:S(2)}, u32[]{:S(2)}) %collective-permute-start.7) | collective-permute-done | bytes 40992 | tf_op jit(solution)/shard_map/ppermute | solution.py:307
  80.9 1.0 %shard_map.79 = (f32[2,3,3,64,64]{4,3,2,1,0:T(8,128)}, f32[2,64]{1,0:T(2,128)}) custom-call(bf16[160,128]{1,0:T(8,128)(2,1)S(1)} %add_convert_fusion.refs_0_, bf16[160,128]{1,0:T(8,128)(2,1)S(1)} %collective-permute-done.7.refs_1_, bf16[160,128]{1,0:T(8,128)(2,1)S(1)} %collective-permute-done.8.refs_2_, bf16[160,128]{1,0:T(8,128)(2,1)S(1)} %collective-permute-done.9.refs_3_), custom_call_target="tpu_custom_call" | custom-call | tf_op jit(solution)/shard_map/pallas_call | solution.py:420
  (3 shorter events, 0.1 us)
Async XLA Ops:
  3.6 7.3 %copy-start.4 = (f32[2,64]{1,0:T(2,128)S(1)}, f32[2,64]{1,0:T(2,128)}, u32[]{:S(2)}) copy-start(f32[2,64]{1,0:T(2,128)} %param.6) | copy-start | bytes 1540
  3.6 34.5 %copy-start.3 = (bf16[2,3,3,64,64]{4,3,2,1,0:T(8,128)(2,1)S(1)}, bf16[2,3,3,64,64]{4,3,2,1,0:T(8,128)(2,1)}, u32[]{:S(2)}) copy-start(bf16[2,3,3,64,64]{4,3,2,1,0:T(8,128)(2,1)} %w_ref.1) | copy-start | bytes 442372
  3.6 33.5 %all-to-all-start = ((bf16[32,128,128]{2,1,0:T(8,128)(2,1)}), bf16[32,128,128]{2,1,0:T(8,128)(2,1)S(1)}, u32[]{:S(2)}, u32[]{:S(2)}) async-start(bf16[32,128,128]{2,1,0:T(8,128)(2,1)} %shard_map.75), calls=%async_computation | async-start | bytes 2097152 | tf_op jit(solution)/shard_map/all_to_all | solution.py:330
  37.2 1.0 %copy-start = (bf16[32,128,128]{2,1,0:T(8,128)(2,1)}, bf16[32,128,128]{2,1,0:T(8,128)(2,1)S(1)}, u32[]{:S(2)}) copy-start(bf16[32,128,128]{2,1,0:T(8,128)(2,1)S(1)} %all-to-all-done.parts_ref) | copy-start | bytes 3145732
  43.6 3.6 %copy-start.1 = (bf16[32,128,128]{2,1,0:T(8,128)(2,1)S(1)}, bf16[32,128,128]{2,1,0:T(8,128)(2,1)}, u32[]{:S(2)}) copy-start(bf16[32,128,128]{2,1,0:T(8,128)(2,1)} %copy-done) | copy-start | bytes 3145732
  43.6 31.7 %all-to-all-start.1 = ((bf16[32,128,128]{2,1,0:T(8,128)(2,1)}), bf16[32,128,128]{2,1,0:T(8,128)(2,1)S(1)}, u32[]{:S(2)}, u32[]{:S(2)}) async-start(bf16[32,128,128]{2,1,0:T(8,128)(2,1)} %get-tuple-element.16), calls=%async_computation.1 | async-start | bytes 2097152 | tf_op jit(solution)/shard_map/all_to_all | solution.py:330
  47.2 1.4 %copy-start.2 = (bf16[3,8,64,512]{3,2,1,0:T(8,128)(2,1)S(1)}, bf16[3,8,64,512]{3,2,1,0:T(8,128)(2,1)}, u32[]{:S(2)}) copy-start(bf16[3,8,64,512]{3,2,1,0:T(8,128)(2,1)} %get-tuple-element.17.kept_ref) | copy-start | bytes 4718596
  50.9 7.1 %collective-permute-start = (bf16[160,128]{1,0:T(8,128)(2,1)S(1)}, bf16[160,128]{1,0:T(8,128)(2,1)S(1)}, u32[]{:S(2)}, u32[]{:S(2)}) collective-permute-start(bf16[160,128]{1,0:T(8,128)(2,1)S(1)} %get-tuple-element.19), channel_id=1, source_target_pairs={{0,2},{1,3},{2,0},{3,1},{4,6},{5,7},{6,4},{7,5},{8,10},{9,11},{10,... | collective-permute-start | bytes 122888 | tf_op jit(solution)/shard_map/ppermute | solution.py:307
  52.8 5.3 %collective-permute-start.1 = (bf16[160,128]{1,0:T(8,128)(2,1)S(1)}, bf16[160,128]{1,0:T(8,128)(2,1)S(1)}, u32[]{:S(2)}, u32[]{:S(2)}) collective-permute-start(bf16[160,128]{1,0:T(8,128)(2,1)S(1)} %get-tuple-element.20), channel_id=1, source_target_pairs={{0,1},{1,0},{2,3},{3,2},{4,5},{5,4},{6,7},{7,6},{8,9},{9,8},{10,11... | collective-permute-start | bytes 122888 | tf_op jit(solution)/shard_map/ppermute | solution.py:307
  52.8 6.8 %collective-permute-start.2 = (bf16[160,128]{1,0:T(8,128)(2,1)S(1)}, bf16[160,128]{1,0:T(8,128)(2,1)S(1)}, u32[]{:S(2)}, u32[]{:S(2)}) collective-permute-start(bf16[160,128]{1,0:T(8,128)(2,1)S(1)} %get-tuple-element.21), channel_id=1, source_target_pairs={{0,3},{1,2},{2,1},{3,0},{4,7},{5,6},{6,5},{7,4},{8,11},{9,10},{10,... | collective-permute-start | bytes 122888 | tf_op jit(solution)/shard_map/ppermute | solution.py:307
  59.7 6.4 %collective-permute-start.5 = (bf16[160,128]{1,0:T(8,128)(2,1)S(1)}, bf16[160,128]{1,0:T(8,128)(2,1)S(1)}, u32[]{:S(2)}, u32[]{:S(2)}) collective-permute-start(bf16[160,128]{1,0:T(8,128)(2,1)S(1)} %add_convert_fusion.2), channel_id=1, source_target_pairs={{0,12},{1,13},{2,14},{3,15},{4,8},{5,9},{6,10},{7,11},{8,4},{9,5},... | collective-permute-start | bytes 122888 | tf_op jit(solution)/shard_map/ppermute | solution.py:307
  59.7 8.5 %collective-permute-start.4 = (bf16[160,128]{1,0:T(8,128)(2,1)S(1)}, bf16[160,128]{1,0:T(8,128)(2,1)S(1)}, u32[]{:S(2)}, u32[]{:S(2)}) collective-permute-start(bf16[160,128]{1,0:T(8,128)(2,1)S(1)} %add_convert_fusion.2), channel_id=1, source_target_pairs={{0,8},{1,9},{2,10},{3,11},{4,12},{5,13},{6,14},{7,15},{8,0},{9,1},... | collective-permute-start | bytes 122888 | tf_op jit(solution)/shard_map/ppermute | solution.py:307
  63.7 4.6 %collective-permute-start.3 = (bf16[160,128]{1,0:T(8,128)(2,1)S(1)}, bf16[160,128]{1,0:T(8,128)(2,1)S(1)}, u32[]{:S(2)}, u32[]{:S(2)}) collective-permute-start(bf16[160,128]{1,0:T(8,128)(2,1)S(1)} %add_convert_fusion.2), channel_id=1, source_target_pairs={{0,4},{1,5},{2,6},{3,7},{4,0},{5,1},{6,2},{7,3},{8,12},{9,13},{10,... | collective-permute-start | bytes 122888 | tf_op jit(solution)/shard_map/ppermute | solution.py:307
  68.3 6.9 %collective-permute-start.6 = (bf16[160,128]{1,0:T(8,128)(2,1)S(1)}, bf16[160,128]{1,0:T(8,128)(2,1)S(1)}, u32[]{:S(2)}, u32[]{:S(2)}) collective-permute-start(bf16[160,128]{1,0:T(8,128)(2,1)S(1)} %add_convert_fusion.1), channel_id=1, source_target_pairs={{0,16},{1,17},{2,18},{3,19},{4,20},{5,21},{6,22},{7,23},{8,24},{9,... | collective-permute-start | bytes 122888 | tf_op jit(solution)/shard_map/ppermute | solution.py:307
  75.2 3.8 %collective-permute-start.9 = (bf16[160,128]{1,0:T(8,128)(2,1)S(1)}, bf16[160,128]{1,0:T(8,128)(2,1)S(1)}, u32[]{:S(2)}, u32[]{:S(2)}) collective-permute-start(bf16[160,128]{1,0:T(8,128)(2,1)S(1)} %add_convert_fusion.refs_0_), channel_id=1, source_target_pairs={{0,3},{1,2},{2,1},{3,0},{4,7},{5,6},{6,5},{7,4},{8,11},{9,10},{10,... | collective-permute-start | bytes 122888 | tf_op jit(solution)/shard_map/ppermute | solution.py:307
  76.1 3.0 %collective-permute-start.8 = (bf16[160,128]{1,0:T(8,128)(2,1)S(1)}, bf16[160,128]{1,0:T(8,128)(2,1)S(1)}, u32[]{:S(2)}, u32[]{:S(2)}) collective-permute-start(bf16[160,128]{1,0:T(8,128)(2,1)S(1)} %add_convert_fusion.refs_0_), channel_id=1, source_target_pairs={{0,1},{1,0},{2,3},{3,2},{4,5},{5,4},{6,7},{7,6},{8,9},{9,8},{10,11... | collective-permute-start | bytes 122888 | tf_op jit(solution)/shard_map/ppermute | solution.py:307
  76.9 4.0 %collective-permute-start.7 = (bf16[160,128]{1,0:T(8,128)(2,1)S(1)}, bf16[160,128]{1,0:T(8,128)(2,1)S(1)}, u32[]{:S(2)}, u32[]{:S(2)}) collective-permute-start(bf16[160,128]{1,0:T(8,128)(2,1)S(1)} %add_convert_fusion.refs_0_), channel_id=1, source_target_pairs={{0,2},{1,3},{2,0},{3,1},{4,6},{5,7},{6,4},{7,5},{8,10},{9,11},{10,... | collective-permute-start | bytes 122888 | tf_op jit(solution)/shard_map/ppermute | solution.py:307
where the time goes:
time: 82.3 us; the launch traced here: 82 us
  waiting for transfers between devices  42.6 us (52%)
  starting transfers between devices  22.7 us (28%)
  Pallas kernels  13.3 us (16%)
  local copies, waits for them, and re-layouts  2.49 us (3%)
    all_to_all x2, waiting for transfers between devices, exchanged(): return lax.all_to_all(parts, AXES, 0, 0, tiled=True)  26.1 us
    ppermute x10, waiting for transfers between devices, partnered(): return lax.ppermute(block, AXES, [(i, i ^ bit) for i in range(devices)])  16.5 us
    ppermute x10, starting transfers between devices, partnered(): return lax.ppermute(block, AXES, [(i, i ^ bit) for i in range(devices)])  11.8 us
    all_to_all x2, starting transfers between devices, exchanged(): return lax.all_to_all(parts, AXES, 0, 0, tiled=True)  10.9 us
    pallas_call x1, Pallas kernels, local(): pl.pallas_call(functools.partial(stack_kernel, share), out_shape=[shape(p...  5.4 us
    pallas_call x1, Pallas kernels, local(): pl.pallas_call(functools.partial(pack_kernel, share), out_shape=shape(fie...  2.97 us
    unnamed x10, local copies, waits for them, and re-layouts  2.39 us
    pallas_call x1, Pallas kernels, local(): pl.pallas_call(functools.partial(sums_kernel, share), out_shape=[shape(qu...  2.31 us
  transfers between devices with their start and end apart: 12, of which 7 were waited for; matrix products, arithmetic and copies ran while one was open for 0% of the time, Pallas kernels for 5%

commit v1 on v0

--- a/solution.py
+++ b/solution.py
@@ -15,7 +15,6 @@
 QUARTERS = (2, 1, 3)
 BF16, F32 = jnp.bfloat16, jnp.float32
 PARAMS = pltpu.CompilerParams(vmem_limit_bytes=24 * 2**20)
-MIDDLE = pltpu.CompilerParams(vmem_limit_bytes=207 * 2**18)
 WIDE = pltpu.CompilerParams(vmem_limit_bytes=56 * 2**20)
 
 
@@ -112,10 +111,35 @@
     return before, row, after
 
 
+def kernels_kernel(w_ref, out_ref):
+    for layer in range(2):
+        for back in range(2):
+            rows = []
+            for a in range(3):
+                row = [w_ref[layer, a, b] for b in range(3)]
+                if back:
+                    row = [tap.astype(F32).T.astype(BF16) for tap in row]
+                rows.append(jnp.concatenate(row, axis=1))
+            out_ref[2 * layer + back] = jnp.concatenate(rows, axis=0)
+
+
 def line_of(parts_ref, count, channels, field, i):
     blocks = parts_ref.shape[0] // count
     rows = slice(field * channels, (field + 1) * channels)
     return jnp.concatenate([parts_ref[i * blocks + k, rows, :] for k in range(blocks)], axis=1)
+
+
+def weight_product(gated, stack, lines):
+    ones = jnp.ones((16, gated.shape[1]), BF16)
+    across = (((1,), (1,)), ((), ()))
+    bias = lax.dot_general(ones, gated, across, preferred_element_type=F32)
+    lines = jnp.concatenate(lines, axis=0)
+    return lax.dot_general(stack, lines, across, preferred_element_type=F32), bias
+
+
+def back_taps(gated, shift):
+    before, here, after = taps(gated, shift)
+    return jnp.concatenate([after, here, before], axis=0)
 
 
 def stack_kernel(
@@ -124,18 +148,17 @@
     w_ref,
     b_ref,
     out_ref,
-    kept_ref,
+    gz_ref,
+    total_ref,
+    bias_ref,
     h_ref,
-    gz0_ref,
-    gz1_ref,
     s0_ref,
     s1_ref,
     y_ref,
     fields_ref,
     sems,
 ):
-    count = h_ref.shape[0]
-    channels = w_ref.shape[-1]
+    count, channels, _ = h_ref.shape
     devices, _, width = parts_ref.shape
     blocks = devices // count
     copies = []
@@ -145,77 +168,65 @@
         for k in range(blocks):
             fields_ref[i * blocks + k, rows, :] = line[:, k * width : (k + 1) * width]
 
-    def copy(source, target):
-        copies.append(pltpu.make_async_copy(source, target, sems.at[len(copies)]))
-        copies[-1].start()
-
     def send(field, i, lines):
         place = (pl.ds(i * blocks, lines * blocks), pl.ds(field * channels, channels))
-        copy(fields_ref.at[place], out_ref.at[place])
+        copies.append(
+            pltpu.make_async_copy(fields_ref.at[place], out_ref.at[place], sems.at[len(copies)])
+        )
+        copies[-1].start()
 
     for layer in range(2):
         hops = 2**layer
-        kernel = jnp.concatenate(
-            [
-                jnp.concatenate([w_ref[layer, a, b] for b in range(3)], axis=1)
-                for a in range(3)
-            ],
-            axis=0,
-        )
+        kernel = w_ref[2 * layer]
         for i in range(count):
             line = line_of(parts_ref, count, channels, 0, i) if layer == 0 else h_ref[i]
             stack = jnp.concatenate(taps(line, hops * share), axis=0)
-            y_ref[i] = jnp.dot(kernel, stack, preferred_element_type=F32)
+            y_ref[i] = product(kernel, stack)
         bias = b_ref[layer]
         for i in range(count):
             pre = bias + y_ref[i, channels : 2 * channels]
             pre = pre + y_ref[(i - hops) % count, :channels]
             pre = pre + y_ref[(i + hops) % count, 2 * channels :]
-            sigma = 1.0 / (1.0 + jnp.exp(-pre))
-            state = (pre * sigma).astype(BF16)
-            slope = sigma * (1.0 + pre * (1.0 - sigma))
+            sigma = 0.5 * jnp.tanh(0.5 * pre) + 0.5
+            state = pre * sigma
+            slope = sigma + state * (1.0 - sigma)
             if layer == 0:
-                h_ref[i] = state
+                h_ref[i] = state.astype(BF16)
                 s0_ref[i] = slope
             else:
                 s1_ref[i] = slope
-                put(0, i, state)
-        if layer == 0:
-            copy(h_ref, kept_ref.at[0])
+                put(0, i, state.astype(BF16))
     send(0, 0, count)
 
+    total, bias = 0.0, 0.0
     for layer in (1, 0):
         hops = 2**layer
-        kernel = jnp.concatenate(
-            [
-                jnp.concatenate([w_ref[layer, a, b].astype(F32).T for b in range(3)], axis=1)
-                for a in range(3)
-            ],
-            axis=0,
-        ).astype(BF16)
+        kernel = w_ref[2 * layer + 1]
         for i in range(count):
             if layer == 1:
                 gated = line_of(parts_ref, count, channels, 1, i).astype(F32) * s1_ref[i]
                 gated = gated.astype(BF16)
-                gz1_ref[i] = gated
             else:
-                gated = gz0_ref[i]
-            before, here, after = taps(gated, hops * share)
-            stack = jnp.concatenate([after, here, before], axis=0)
-            y_ref[i] = jnp.dot(kernel, stack, preferred_element_type=F32)
+                gated = gz_ref[i]
+            stack = back_taps(gated, hops * share)
+            y_ref[i] = product(kernel, stack)
+            if layer == 1:
+                around = [h_ref[(i + (a - 1) * hops) % count] for a in range(3)]
+                term, bias_term = weight_product(gated, stack, around)
+                total, bias = total + term, bias + bias_term
         for i in range(count):
             g = y_ref[i, channels : 2 * channels]
             g = g + y_ref[(i + hops) % count, :channels]
             g = g + y_ref[(i - hops) % count, 2 * channels :]
             g = g.astype(BF16)
             if layer == 1:
-                gz0_ref[i] = (g.astype(F32) * s0_ref[i]).astype(BF16)
+                gz_ref[i] = (g.astype(F32) * s0_ref[i]).astype(BF16)
             else:
                 put(1, i, g)
                 send(1, i, 1)
         if layer == 1:
-            copy(gz1_ref, kept_ref.at[1])
-            copy(gz0_ref, kept_ref.at[2])
+            total_ref[...] = total
+            bias_ref[...] = bias
     for started in copies:
         started.wait()
 
@@ -228,53 +239,29 @@
     return mine, 2 * odd + 1 - upper, other, 2 * (1 - odd) + 1 - upper
 
 
-def sums_kernel(share, parts_ref, kept_ref, keep_ref, *refs):
-    send_refs, (buf, total_ref, sems) = refs[:3], refs[3:]
-    _, count, channels, span = buf.shape
-    h_ref, gz1_ref, gz0_ref = buf.at[0], buf.at[1], buf.at[2]
-    copies = [pltpu.make_async_copy(kept_ref.at[k], buf.at[k], sems.at[k]) for k in range(3)]
-    for copy in copies:
-        copy.start()
-    copies[0].wait()
-    copies[1].wait()
-    ones = jnp.ones((16, span), BF16)
+def sums_kernel(share, parts_ref, gz_ref, total_ref, bias_ref, keep_ref, *refs):
+    send_refs, (rows_ref,) = refs[:3], refs[3:]
+    count, channels, _ = gz_ref.shape
     high = 3 * channels
-    bias_rows = [None, None]
-    for layer, gz_ref in ((1, gz1_ref), (0, gz0_ref)):
-        hops = 2**layer
-        if layer == 0:
-            copies[2].wait()
-        total = jnp.zeros((high, high), F32)
-        bias = jnp.zeros((16, channels), F32)
-        for i in range(count):
-            gated = gz_ref[i]
-            bias = bias + lax.dot_general(
-                ones, gated, (((1,), (1,)), ((), ())), preferred_element_type=F32
-            )
-            before, here, after = taps(gated, hops * share)
-            stack = jnp.concatenate([after, here, before], axis=0)
-            around = [(i + (a - 1) * hops) % count for a in range(3)]
-            lines = [
-                line_of(parts_ref, count, channels, 0, j) if layer == 0 else h_ref[j]
-                for j in around
-            ]
-            total = total + lax.dot_general(
-                stack,
-                jnp.concatenate(lines, axis=0),
-                (((1,), (1,)), ((), ())),
-                preferred_element_type=F32,
-            )
-        total_ref[layer * high : (layer + 1) * high, :] = total[:, : 2 * channels]
-        total_ref[2 * high : 3 * high, layer * channels : (layer + 1) * channels] = total[
+    total, bias = 0.0, 0.0
+    for i in range(count):
+        gated = gz_ref[i]
+        around = [
+            line_of(parts_ref, count, channels, 0, (i + a - 1) % count) for a in range(3)
+        ]
+        term, bias_term = weight_product(gated, back_taps(gated, share), around)
+        total, bias = total + term, bias + bias_term
+    for layer, sums in enumerate((total, total_ref[...])):
+        rows_ref[layer * high : (layer + 1) * high, :] = sums[:, : 2 * channels]
+        rows_ref[2 * high : 3 * high, layer * channels : (layer + 1) * channels] = sums[
             :, 2 * channels :
         ]
-        bias_rows[layer] = bias[:1]
-    bias = jnp.concatenate(bias_rows, axis=1)
+    bias = jnp.concatenate([bias[:1], bias_ref[:1]], axis=1)
     row = lax.broadcasted_iota(jnp.int32, (TAIL, 2 * channels), 0)
-    total_ref[3 * high :, :] = jnp.where(row == 0, bias, 0.0)
+    rows_ref[3 * high :, :] = jnp.where(row == 0, bias, 0.0)
     size = keep_ref.shape[0]
     for at, quarter in enumerate(quarters()):
-        rows = total_ref[pl.ds(pl.multiple_of(quarter * size, 16), size), :]
+        rows = rows_ref[pl.ds(pl.multiple_of(quarter * size, 16), size), :]
         if at == 0:
             keep_ref[...] = rows
         else:
@@ -359,28 +346,38 @@
         ],
         compiler_params=WIDE,
     )(inputs, cotangent)
+    packed, weights = lax.optimization_barrier((packed, weights))
+    kernels = pl.pallas_call(
+        kernels_kernel,
+        out_shape=shape((4, 3 * channels, 3 * channels), BF16),
+        compiler_params=PARAMS,
+    )(weights)
     parts = exchanged(packed)
     if blocks == 1:
         parts = parts.reshape(lons, lats, 2 * channels, width).transpose(0, 2, 1, 3)
         parts = parts.reshape(lons, 2 * channels, span)
 
     cells = (lons, channels, span)
-    fields, kept = pl.pallas_call(
+    high = 3 * channels
+    fields, gated, total, bias_sums = pl.pallas_call(
         functools.partial(stack_kernel, share),
-        out_shape=[shape(parts.shape, BF16), shape((3,) + cells, BF16)],
-        out_specs=[hbm, hbm],
+        out_shape=[
+            shape(parts.shape, BF16),
+            shape(cells, BF16),
+            shape((high, high), F32),
+            shape((16, channels), F32),
+        ],
+        out_specs=[hbm, vmem, vmem, vmem],
         scratch_shapes=[
-            pltpu.VMEM(cells, BF16),
-            pltpu.VMEM(cells, BF16),
             pltpu.VMEM(cells, BF16),
             pltpu.VMEM(cells, F32),
             pltpu.VMEM(cells, F32),
             pltpu.VMEM((lons, 3 * channels, span), F32),
             pltpu.VMEM(parts.shape, BF16),
-            pltpu.SemaphoreType.DMA((lons + 4,)),
+            pltpu.SemaphoreType.DMA((lons + 1,)),
         ],
-        compiler_params=MIDDLE,
-    )(parts, weights, biases[:, :, None])
+        compiler_params=PARAMS,
+    )(parts, kernels, biases[:, :, None])
     if blocks == 1:
         fields = fields.reshape(lons, 2 * channels, lats, width).transpose(0, 2, 1, 3)
         fields = fields.reshape(fields_shape)
@@ -388,19 +385,14 @@
 
     rows = 9 * channels + TAIL
     quarter_shape = (rows // 4, 2 * channels)
-    flops = 2 * 2 * 9 * channels * parts.size // 2
+    flops = 9 * channels * parts.size
     keep, *sends = pl.pallas_call(
         functools.partial(sums_kernel, share),
         out_shape=[shape(quarter_shape, F32)] + [shape(quarter_shape, BF16)] * 3,
-        in_specs=[vmem, hbm],
-        scratch_shapes=[
-            pltpu.VMEM((3,) + cells, BF16),
-            pltpu.VMEM((rows, 2 * channels), F32),
-            pltpu.SemaphoreType.DMA((3,)),
-        ],
+        scratch_shapes=[pltpu.VMEM((rows, 2 * channels), F32)],
         compiler_params=PARAMS,
-        cost_estimate=pl.CostEstimate(flops=flops, bytes_accessed=5 * parts.size, transcendentals=0),
-    )(parts, kept)
+        cost_estimate=pl.CostEstimate(flops=flops, bytes_accessed=3 * parts.size, transcendentals=0),
+    )(parts, gated, total, bias_sums)
     mine = added(keep, sends, devices)
     home, mine = lax.optimization_barrier((home, mine))
     others = [partnered(mine, devices, bit) for bit in QUARTERS]

time: 82.3 us -> 80.6 us (0.979)
  Pallas kernels: 13.3 us -> 11.3 us
  local copies, waits for them, and re-layouts: 2.49 us -> 0.78 us
  starting transfers between devices: 22.7 us -> 24.1 us
    unnamed x10 -> x4, local copies, waits for them, and re-layouts: 2.39 us -> 0.68 us
    ppermute x10, waiting for transfers between devices: 16.5 us -> 18.1 us  [partnered(): return lax.ppermute(block, AXES, [(i, i ^ bit) for i in range(devices)])]
    pallas_call x1, Pallas kernels: 2.31 us -> 0.8 us  [local(): pl.pallas_call(functools.partial(sums_kernel, share), out_shape=[shape(qu...]
    ppermute x10, starting transfers between devices: 11.8 us -> 13.1 us  [partnered(): return lax.ppermute(block, AXES, [(i, i ^ bit) for i in range(devices)])]
    all_to_all x2, waiting for transfers between devices: 26.1 us -> 25.2 us  [exchanged(): return lax.all_to_all(parts, AXES, 0, 0, tiled=True)]
  transfers between devices with their start and end apart: 12 -> 12, of which waited for: 7 -> 7; matrix products, arithmetic and copies ran while one was open for 0% -> 0% of each run, Pallas kernels for 5% -> 3%
where the time goes in v1:
time: 80.6 us; the launch traced here: 80.3 us
  waiting for transfers between devices  43.3 us (54%)
  starting transfers between devices  24.1 us (30%)
  Pallas kernels  11.3 us (14%)
    all_to_all x2, waiting for transfers between devices, exchanged(): return lax.all_to_all(parts, AXES, 0, 0, tiled=True)  25.2 us
    ppermute x10, waiting for transfers between devices, partnered(): return lax.ppermute(block, AXES, [(i, i ^ bit) for i in range(devices)])  18.1 us
    ppermute x10, starting transfers between devices, partnered(): return lax.ppermute(block, AXES, [(i, i ^ bit) for i in range(devices)])  13.1 us
    all_to_all x2, starting transfers between devices, exchanged(): return lax.all_to_all(parts, AXES, 0, 0, tiled=True)  10.9 us
    pallas_call x1, Pallas kernels, local(): pl.pallas_call(functools.partial(stack_kernel, share), out_shape=[shape(p...  4.71 us
    pallas_call x1, Pallas kernels, local(): pl.pallas_call(functools.partial(pack_kernel, share), out_shape=shape(fie...  2.96 us
    pallas_call x1, Pallas kernels, local(): pl.pallas_call(functools.partial(unpack_kernel, share), out_shape=[shape(...  1.61 us
  transfers between devices with their start and end apart: 12, of which 7 were waited for; matrix products, arithmetic and copies ran while one was open for 0% of the time, Pallas kernels for 3%

profile of v1, /device:TPU:0, one launch (start us, length us, event | category | flops | bytes accessed | tf_op | source)
XLA Modules:
  0.0 80.3 jit_solution(12580871396389846726)
XLA Ops:
  0.6 3.0 %shard_map.75 = bf16[32,128,128]{2,1,0:T(8,128)(2,1)} custom-call(bf16[64,16,256]{2,1,0:T(8,128)(2,1)} %x_ref.1, bf16[64,16,256]{2,1,0:T(8,128)(2,1)} %cot_ref.1), custom_call_target="tpu_custom_call" | custom-call | tf_op jit(solution)/shard_map/pallas_call | solution.py:336
  3.6 0.0 copy-start
  3.6 7.3 %all-to-all-start = ((bf16[32,128,128]{2,1,0:T(8,128)(2,1)}), bf16[32,128,128]{2,1,0:T(8,128)(2,1)S(1)}, u32[]{:S(2)}, u32[]{:S(2)}) async-start(bf16[32,128,128]{2,1,0:T(8,128)(2,1)} %shard_map.75), calls=%async_computation | async-start | bytes 2097152 | tf_op jit(solution)/shard_map/all_to_all | solution.py:317
  10.9 0.0 copy-start.1
  10.9 0.7 copy-done.1
  11.6 0.1 copy.8.b_ref
  11.7 0.0 copy-done
  11.7 0.2 shard_map.76.w_ref
  12.0 25.2 %all-to-all-done.parts_ref = bf16[32,128,128]{2,1,0:T(8,128)(2,1)S(1)} async-done(((bf16[32,128,128]{2,1,0:T(8,128)(2,1)}), bf16[32,128,128]{2,1,0:T(8,128)(2,1)S(1)}, u32[]{:S(2)}, u32[]{:S(2)}) %all-to-all-start) | async-done | bytes 1048608 | tf_op jit(solution)/shard_map/all_to_all | solution.py:317
  37.2 4.7 %shard_map.77 = (bf16[32,128,128]{2,1,0:T(8,128)(2,1)}, bf16[8,64,512]{2,1,0:T(8,128)(2,1)S(1)}, f32[192,192]{1,0:T(8,128)S(1)}, f32[16,64]{1,0:T(8,128)S(1)}) custom-call(bf16[32,128,128]{2,1,0:T(8,128)(2,1)S(1)} %all-to-all-done.parts_ref, bf16[4,192,192]{2,1,0:T(8,128)(2,1)S(1)} %shard_map.76.w_ref, f32[2,64,1]{2,1,0:T(8,128)S(1)} %copy.8.b_ref), custom_call_target="tpu_custom_call" | custom-call | tf_op jit(solution)/shard_map/pallas_call | solution.py:362
  41.9 3.6 %all-to-all-start.1 = ((bf16[32,128,128]{2,1,0:T(8,128)(2,1)}), bf16[32,128,128]{2,1,0:T(8,128)(2,1)S(1)}, u32[]{:S(2)}, u32[]{:S(2)}) async-start(bf16[32,128,128]{2,1,0:T(8,128)(2,1)} %get-tuple-element.22), calls=%async_computation.1 | async-start | bytes 2097152 | tf_op jit(solution)/shard_map/all_to_all | solution.py:317
  45.5 0.8 shard_map.78
  46.3 1.8 %collective-permute-start = (bf16[160,128]{1,0:T(8,128)(2,1)S(1)}, bf16[160,128]{1,0:T(8,128)(2,1)S(1)}, u32[]{:S(2)}, u32[]{:S(2)}) collective-permute-start(bf16[160,128]{1,0:T(8,128)(2,1)S(1)} %get-tuple-element.27), channel_id=1, source_target_pairs={{0,2},{1,3},{2,0},{3,1},{4,6},{5,7},{6,4},{7,5},{8,10},{9,11},{10,... | collective-permute-start | bytes 122888 | tf_op jit(solution)/shard_map/ppermute | solution.py:294
  48.2 0.0 collective-permute-start.1
  48.2 0.4 collective-permute-start.2
  48.5 7.0 %collective-permute-done = bf16[160,128]{1,0:T(8,128)(2,1)S(1)} collective-permute-done((bf16[160,128]{1,0:T(8,128)(2,1)S(1)}, bf16[160,128]{1,0:T(8,128)(2,1)S(1)}, u32[]{:S(2)}, u32[]{:S(2)}) %collective-permute-start) | collective-permute-done | bytes 40992 | tf_op jit(solution)/shard_map/ppermute | solution.py:294
  55.5 0.0 collective-permute-done.1
  55.5 0.4 collective-permute-done.2
  55.9 1.6 %collective-permute-start.5 = (bf16[160,128]{1,0:T(8,128)(2,1)S(1)}, bf16[160,128]{1,0:T(8,128)(2,1)S(1)}, u32[]{:S(2)}, u32[]{:S(2)}) collective-permute-start(bf16[160,128]{1,0:T(8,128)(2,1)S(1)} %add_convert_fusion.2), channel_id=1, source_target_pairs={{0,12},{1,13},{2,14},{3,15},{4,8},{5,9},{6,10},{7,11},{8,4},{9,5},... | collective-permute-start | bytes 122888 | tf_op jit(solution)/shard_map/ppermute | solution.py:294
  57.5 2.6 %collective-permute-start.4 = (bf16[160,128]{1,0:T(8,128)(2,1)S(1)}, bf16[160,128]{1,0:T(8,128)(2,1)S(1)}, u32[]{:S(2)}, u32[]{:S(2)}) collective-permute-start(bf16[160,128]{1,0:T(8,128)(2,1)S(1)} %add_convert_fusion.2), channel_id=1, source_target_pairs={{0,8},{1,9},{2,10},{3,11},{4,12},{5,13},{6,14},{7,15},{8,0},{9,1},... | collective-permute-start | bytes 122888 | tf_op jit(solution)/shard_map/ppermute | solution.py:294
  60.1 0.0 collective-permute-start.3
  60.1 4.3 %collective-permute-done.5 = bf16[160,128]{1,0:T(8,128)(2,1)S(1)} collective-permute-done((bf16[160,128]{1,0:T(8,128)(2,1)S(1)}, bf16[160,128]{1,0:T(8,128)(2,1)S(1)}, u32[]{:S(2)}, u32[]{:S(2)}) %collective-permute-start.5) | collective-permute-done | bytes 40992 | tf_op jit(solution)/shard_map/ppermute | solution.py:294
  64.3 1.1 %collective-permute-done.4 = bf16[160,128]{1,0:T(8,128)(2,1)S(1)} collective-permute-done((bf16[160,128]{1,0:T(8,128)(2,1)S(1)}, bf16[160,128]{1,0:T(8,128)(2,1)S(1)}, u32[]{:S(2)}, u32[]{:S(2)}) %collective-permute-start.4) | collective-permute-done | bytes 40992 | tf_op jit(solution)/shard_map/ppermute | solution.py:294
  65.4 0.0 collective-permute-done.3
  65.4 4.6 %collective-permute-start.6 = (bf16[160,128]{1,0:T(8,128)(2,1)S(1)}, bf16[160,128]{1,0:T(8,128)(2,1)S(1)}, u32[]{:S(2)}, u32[]{:S(2)}) collective-permute-start(bf16[160,128]{1,0:T(8,128)(2,1)S(1)} %add_convert_fusion.1), channel_id=1, source_target_pairs={{0,16},{1,17},{2,18},{3,19},{4,20},{5,21},{6,22},{7,23},{8,24},{9,... | collective-permute-start | bytes 122888 | tf_op jit(solution)/shard_map/ppermute | solution.py:294
  70.0 3.5 %collective-permute-done.6 = bf16[160,128]{1,0:T(8,128)(2,1)S(1)} collective-permute-done((bf16[160,128]{1,0:T(8,128)(2,1)S(1)}, bf16[160,128]{1,0:T(8,128)(2,1)S(1)}, u32[]{:S(2)}, u32[]{:S(2)}) %collective-permute-start.6) | collective-permute-done | bytes 40992 | tf_op jit(solution)/shard_map/ppermute | solution.py:294
  73.5 0.0 all-to-all-done.1.parts_ref
  73.5 0.8 %collective-permute-start.9 = (bf16[160,128]{1,0:T(8,128)(2,1)S(1)}, bf16[160,128]{1,0:T(8,128)(2,1)S(1)}, u32[]{:S(2)}, u32[]{:S(2)}) collective-permute-start(bf16[160,128]{1,0:T(8,128)(2,1)S(1)} %add_convert_fusion.refs_0_), channel_id=1, source_target_pairs={{0,3},{1,2},{2,1},{3,0},{4,7},{5,6},{6,5},{7,4},{8,11},{9,10},{10,... | collective-permute-start | bytes 122888 | tf_op jit(solution)/shard_map/ppermute | solution.py:294
  74.4 0.9 %collective-permute-start.8 = (bf16[160,128]{1,0:T(8,128)(2,1)S(1)}, bf16[160,128]{1,0:T(8,128)(2,1)S(1)}, u32[]{:S(2)}, u32[]{:S(2)}) collective-permute-start(bf16[160,128]{1,0:T(8,128)(2,1)S(1)} %add_convert_fusion.refs_0_), channel_id=1, source_target_pairs={{0,1},{1,0},{2,3},{3,2},{4,5},{5,4},{6,7},{7,6},{8,9},{9,8},{10,11... | collective-permute-start | bytes 122888 | tf_op jit(solution)/shard_map/ppermute | solution.py:294
  75.2 0.5 collective-permute-start.7
  75.7 1.6 %shard_map.79 = (bf16[64,16,256]{2,1,0:T(8,128)(2,1)}, bf16[64,16,256]{2,1,0:T(8,128)(2,1)}) custom-call(bf16[32,128,128]{2,1,0:T(8,128)(2,1)S(1)} %all-to-all-done.1.parts_ref), custom_call_target="tpu_custom_call" | custom-call | flops 268435456 | bytes 2097152 | tf_op jit(solution)/shard_map/pallas_call | solution.py:399
  77.4 0.0 collective-permute-done.9.refs_3_
  77.4 0.0 collective-permute-done.8.refs_2_
  77.4 1.8 %collective-permute-done.7.refs_1_ = bf16[160,128]{1,0:T(8,128)(2,1)S(1)} collective-permute-done((bf16[160,128]{1,0:T(8,128)(2,1)S(1)}, bf16[160,128]{1,0:T(8,128)(2,1)S(1)}, u32[]{:S(2)}, u32[]{:S(2)}) %collective-permute-start.7) | collective-permute-done | bytes 40992 | tf_op jit(solution)/shard_map/ppermute | solution.py:294
  79.2 1.0 %shard_map.80 = (f32[2,3,3,64,64]{4,3,2,1,0:T(8,128)}, f32[2,64]{1,0:T(2,128)}) custom-call(bf16[160,128]{1,0:T(8,128)(2,1)S(1)} %add_convert_fusion.refs_0_, bf16[160,128]{1,0:T(8,128)(2,1)S(1)} %collective-permute-done.7.refs_1_, bf16[160,128]{1,0:T(8,128)(2,1)S(1)} %collective-permute-done.8.refs_2_, bf16[160,128]{1,0:T(8,128)(2,1)S(1)} %collective-permute-done.9.refs_3_), custom_call_target="tpu_custom_call" | custom-call | tf_op jit(solution)/shard_map/pallas_call | solution.py:412
  (3 shorter events, 0.1 us)
Async XLA Ops:
  3.6 8.1 %copy-start = (bf16[2,3,3,64,64]{4,3,2,1,0:T(8,128)(2,1)S(1)}, bf16[2,3,3,64,64]{4,3,2,1,0:T(8,128)(2,1)}, u32[]{:S(2)}) copy-start(bf16[2,3,3,64,64]{4,3,2,1,0:T(8,128)(2,1)} %w_ref) | copy-start | bytes 442372
  3.6 33.5 %all-to-all-start = ((bf16[32,128,128]{2,1,0:T(8,128)(2,1)}), bf16[32,128,128]{2,1,0:T(8,128)(2,1)S(1)}, u32[]{:S(2)}, u32[]{:S(2)}) async-start(bf16[32,128,128]{2,1,0:T(8,128)(2,1)} %shard_map.75), calls=%async_computation | async-start | bytes 2097152 | tf_op jit(solution)/shard_map/all_to_all | solution.py:317
  10.9 0.7 copy-start.1
  41.9 31.6 %all-to-all-start.1 = ((bf16[32,128,128]{2,1,0:T(8,128)(2,1)}), bf16[32,128,128]{2,1,0:T(8,128)(2,1)S(1)}, u32[]{:S(2)}, u32[]{:S(2)}) async-start(bf16[32,128,128]{2,1,0:T(8,128)(2,1)} %get-tuple-element.22), calls=%async_computation.1 | async-start | bytes 2097152 | tf_op jit(solution)/shard_map/all_to_all | solution.py:317
  46.3 9.2 %collective-permute-start = (bf16[160,128]{1,0:T(8,128)(2,1)S(1)}, bf16[160,128]{1,0:T(8,128)(2,1)S(1)}, u32[]{:S(2)}, u32[]{:S(2)}) collective-permute-start(bf16[160,128]{1,0:T(8,128)(2,1)S(1)} %get-tuple-element.27), channel_id=1, source_target_pairs={{0,2},{1,3},{2,0},{3,1},{4,6},{5,7},{6,4},{7,5},{8,10},{9,11},{10,... | collective-permute-start | bytes 122888 | tf_op jit(solution)/shard_map/ppermute | solution.py:294
  48.2 7.4 %collective-permute-start.1 = (bf16[160,128]{1,0:T(8,128)(2,1)S(1)}, bf16[160,128]{1,0:T(8,128)(2,1)S(1)}, u32[]{:S(2)}, u32[]{:S(2)}) collective-permute-start(bf16[160,128]{1,0:T(8,128)(2,1)S(1)} %get-tuple-element.28), channel_id=1, source_target_pairs={{0,1},{1,0},{2,3},{3,2},{4,5},{5,4},{6,7},{7,6},{8,9},{9,8},{10,11... | collective-permute-start | bytes 122888 | tf_op jit(solution)/shard_map/ppermute | solution.py:294
  48.2 7.7 %collective-permute-start.2 = (bf16[160,128]{1,0:T(8,128)(2,1)S(1)}, bf16[160,128]{1,0:T(8,128)(2,1)S(1)}, u32[]{:S(2)}, u32[]{:S(2)}) collective-permute-start(bf16[160,128]{1,0:T(8,128)(2,1)S(1)} %get-tuple-element.29), channel_id=1, source_target_pairs={{0,3},{1,2},{2,1},{3,0},{4,7},{5,6},{6,5},{7,4},{8,11},{9,10},{10,... | collective-permute-start | bytes 122888 | tf_op jit(solution)/shard_map/ppermute | solution.py:294
  55.9 8.5 %collective-permute-start.5 = (bf16[160,128]{1,0:T(8,128)(2,1)S(1)}, bf16[160,128]{1,0:T(8,128)(2,1)S(1)}, u32[]{:S(2)}, u32[]{:S(2)}) collective-permute-start(bf16[160,128]{1,0:T(8,128)(2,1)S(1)} %add_convert_fusion.2), channel_id=1, source_target_pairs={{0,12},{1,13},{2,14},{3,15},{4,8},{5,9},{6,10},{7,11},{8,4},{9,5},... | collective-permute-start | bytes 122888 | tf_op jit(solution)/shard_map/ppermute | solution.py:294
  57.5 7.9 %collective-permute-start.4 = (bf16[160,128]{1,0:T(8,128)(2,1)S(1)}, bf16[160,128]{1,0:T(8,128)(2,1)S(1)}, u32[]{:S(2)}, u32[]{:S(2)}) collective-permute-start(bf16[160,128]{1,0:T(8,128)(2,1)S(1)} %add_convert_fusion.2), channel_id=1, source_target_pairs={{0,8},{1,9},{2,10},{3,11},{4,12},{5,13},{6,14},{7,15},{8,0},{9,1},... | collective-permute-start | bytes 122888 | tf_op jit(solution)/shard_map/ppermute | solution.py:294
  60.1 5.4 %collective-permute-start.3 = (bf16[160,128]{1,0:T(8,128)(2,1)S(1)}, bf16[160,128]{1,0:T(8,128)(2,1)S(1)}, u32[]{:S(2)}, u32[]{:S(2)}) collective-permute-start(bf16[160,128]{1,0:T(8,128)(2,1)S(1)} %add_convert_fusion.2), channel_id=1, source_target_pairs={{0,4},{1,5},{2,6},{3,7},{4,0},{5,1},{6,2},{7,3},{8,12},{9,13},{10,... | collective-permute-start | bytes 122888 | tf_op jit(solution)/shard_map/ppermute | solution.py:294
  65.4 8.1 %collective-permute-start.6 = (bf16[160,128]{1,0:T(8,128)(2,1)S(1)}, bf16[160,128]{1,0:T(8,128)(2,1)S(1)}, u32[]{:S(2)}, u32[]{:S(2)}) collective-permute-start(bf16[160,128]{1,0:T(8,128)(2,1)S(1)} %add_convert_fusion.1), channel_id=1, source_target_pairs={{0,16},{1,17},{2,18},{3,19},{4,20},{5,21},{6,22},{7,23},{8,24},{9,... | collective-permute-start | bytes 122888 | tf_op jit(solution)/shard_map/ppermute | solution.py:294
  73.5 3.9 %collective-permute-start.9 = (bf16[160,128]{1,0:T(8,128)(2,1)S(1)}, bf16[160,128]{1,0:T(8,128)(2,1)S(1)}, u32[]{:S(2)}, u32[]{:S(2)}) collective-permute-start(bf16[160,128]{1,0:T(8,128)(2,1)S(1)} %add_convert_fusion.refs_0_), channel_id=1, source_target_pairs={{0,3},{1,2},{2,1},{3,0},{4,7},{5,6},{6,5},{7,4},{8,11},{9,10},{10,... | collective-permute-start | bytes 122888 | tf_op jit(solution)/shard_map/ppermute | solution.py:294
  74.4 3.0 %collective-permute-start.8 = (bf16[160,128]{1,0:T(8,128)(2,1)S(1)}, bf16[160,128]{1,0:T(8,128)(2,1)S(1)}, u32[]{:S(2)}, u32[]{:S(2)}) collective-permute-start(bf16[160,128]{1,0:T(8,128)(2,1)S(1)} %add_convert_fusion.refs_0_), channel_id=1, source_target_pairs={{0,1},{1,0},{2,3},{3,2},{4,5},{5,4},{6,7},{7,6},{8,9},{9,8},{10,11... | collective-permute-start | bytes 122888 | tf_op jit(solution)/shard_map/ppermute | solution.py:294
  75.2 4.0 %collective-permute-start.7 = (bf16[160,128]{1,0:T(8,128)(2,1)S(1)}, bf16[160,128]{1,0:T(8,128)(2,1)S(1)}, u32[]{:S(2)}, u32[]{:S(2)}) collective-permute-start(bf16[160,128]{1,0:T(8,128)(2,1)S(1)} %add_convert_fusion.refs_0_), channel_id=1, source_target_pairs={{0,2},{1,3},{2,0},{3,1},{4,6},{5,7},{6,4},{7,5},{8,10},{9,11},{10,... | collective-permute-start | bytes 122888 | tf_op jit(solution)/shard_map/ppermute | solution.py:294

commit v2 on v1

--- a/solution.py
+++ b/solution.py
@@ -11,8 +11,7 @@
 
 AXES = ("lon", "lat")
 LANES = 128
-TAIL = 64
-QUARTERS = (2, 1, 3)
+TAIL = 32
 BF16, F32 = jnp.bfloat16, jnp.float32
 PARAMS = pltpu.CompilerParams(vmem_limit_bytes=24 * 2**20)
 WIDE = pltpu.CompilerParams(vmem_limit_bytes=56 * 2**20)
@@ -231,16 +230,7 @@
         started.wait()
 
 
-def quarters():
-    lat = lax.axis_index("lat")
-    odd, upper = lat & 1, lax.div(lat, 2) & 1
-    mine = 2 * odd + upper
-    other = 2 * (1 - odd) + upper
-    return mine, 2 * odd + 1 - upper, other, 2 * (1 - odd) + 1 - upper
-
-
-def sums_kernel(share, parts_ref, gz_ref, total_ref, bias_ref, keep_ref, *refs):
-    send_refs, (rows_ref,) = refs[:3], refs[3:]
+def sums_kernel(share, parts_ref, gz_ref, total_ref, bias_ref, keep_ref, send_ref, rows_ref):
     count, channels, _ = gz_ref.shape
     high = 3 * channels
     total, bias = 0.0, 0.0
@@ -259,22 +249,18 @@
     bias = jnp.concatenate([bias[:1], bias_ref[:1]], axis=1)
     row = lax.broadcasted_iota(jnp.int32, (TAIL, 2 * channels), 0)
     rows_ref[3 * high :, :] = jnp.where(row == 0, bias, 0.0)
-    size = keep_ref.shape[0]
-    for at, quarter in enumerate(quarters()):
-        rows = rows_ref[pl.ds(pl.multiple_of(quarter * size, 16), size), :]
-        if at == 0:
-            keep_ref[...] = rows
-        else:
-            send_refs[at - 1][...] = rows.astype(BF16)
-
-
-def assemble_kernel(scale, *refs):
-    quarter_refs, (out_ref, bias_ref, total_ref) = refs[:4], refs[4:]
+    half = keep_ref.shape[0]
+    odd = lax.axis_index("lat") & 1
+    keep_ref[...] = rows_ref[pl.ds(pl.multiple_of(odd * half, 16), half), :]
+    send_ref[...] = rows_ref[pl.ds(pl.multiple_of((1 - odd) * half, 16), half), :].astype(BF16)
+
+
+def assemble_kernel(scale, mine_ref, other_ref, out_ref, bias_ref, total_ref):
     channels = out_ref.shape[-1]
-    size = quarter_refs[0].shape[0]
-    for quarter, ref in zip(quarters(), quarter_refs):
-        rows = ref[...].astype(F32) * scale
-        total_ref[pl.ds(pl.multiple_of(quarter * size, 16), size), :] = rows
+    half = mine_ref.shape[0]
+    odd = lax.axis_index("lat") & 1
+    for side, ref in ((odd, mine_ref), (1 - odd, other_ref)):
+        total_ref[pl.ds(pl.multiple_of(side * half, 16), half), :] = ref[...].astype(F32) * scale
     high = 3 * channels
     for layer in range(2):
         for b in range(3):
@@ -294,23 +280,13 @@
     return lax.ppermute(block, AXES, [(i, i ^ bit) for i in range(devices)])
 
 
-def added(keep, sends, devices):
-    came = [partnered(send, devices, bit).astype(F32) for send, bit in zip(sends, QUARTERS)]
-    mine = (keep + came[0]) + (came[1] + came[2])
-    low = 4
-    while low < devices:
-        high = 2 * low if 2 * low < devices else 0
-        rounded = mine.astype(BF16)
-        mine = rounded.astype(F32)
-        if high:
-            far = partnered(rounded, devices, high)
-            across = partnered(rounded, devices, low + high)
-            mine = mine + partnered(rounded, devices, low).astype(F32)
-            mine = mine + (far.astype(F32) + across.astype(F32))
-        else:
-            mine = mine + partnered(rounded, devices, low).astype(F32)
-        low *= 4
-    return mine.astype(BF16)
+def added(keep, send, devices):
+    total = keep + partnered(send, devices, 1).astype(F32)
+    bits = [4 << k for k in range((devices // 4).bit_length() - 1)] + [2]
+    for bit in bits:
+        rounded = total.astype(BF16)
+        total = rounded.astype(F32) + partnered(rounded, devices, bit).astype(F32)
+    return total.astype(BF16)
 
 
 def exchanged(parts):
@@ -384,18 +360,18 @@
     home = exchanged(fields)
 
     rows = 9 * channels + TAIL
-    quarter_shape = (rows // 4, 2 * channels)
+    half_shape = (rows // 2, 2 * channels)
     flops = 9 * channels * parts.size
-    keep, *sends = pl.pallas_call(
+    keep, send = pl.pallas_call(
         functools.partial(sums_kernel, share),
-        out_shape=[shape(quarter_shape, F32)] + [shape(quarter_shape, BF16)] * 3,
+        out_shape=[shape(half_shape, F32), shape(half_shape, BF16)],
         scratch_shapes=[pltpu.VMEM((rows, 2 * channels), F32)],
         compiler_params=PARAMS,
         cost_estimate=pl.CostEstimate(flops=flops, bytes_accessed=3 * parts.size, transcendentals=0),
     )(parts, gated, total, bias_sums)
-    mine = added(keep, sends, devices)
+    mine = added(keep, send, devices)
     home, mine = lax.optimization_barrier((home, mine))
-    others = [partnered(mine, devices, bit) for bit in QUARTERS]
+    other = partnered(mine, devices, 1)
     features_out, grad_input = pl.pallas_call(
         functools.partial(unpack_kernel, share),
         out_shape=[shape(inputs.shape, BF16), shape(inputs.shape, BF16)],
@@ -414,7 +390,7 @@
         out_shape=[shape(weights.shape, F32), shape(biases.shape, F32)],
         scratch_shapes=[pltpu.VMEM((rows, 2 * channels), F32)],
         compiler_params=PARAMS,
-    )(mine, *others)
+    )(mine, other)
     return features_out, grad_input, weight_grads, bias_grads
 
 

time: 80.6 us -> 82.7 us (1.026)
  waiting for transfers between devices: 43.3 us -> 49.4 us
  starting transfers between devices: 24.1 us -> 19.9 us
    ppermute x10 -> x6, waiting for transfers between devices: 18.1 us -> 24.2 us  [partnered(): return lax.ppermute(block, AXES, [(i, i ^ bit) for i in range(devices)])]
    ppermute x10 -> x6, starting transfers between devices: 13.1 us -> 9.02 us  [partnered(): return lax.ppermute(block, AXES, [(i, i ^ bit) for i in range(devices)])]
  transfers between devices with their start and end apart: 12 -> 8, of which waited for: 7 -> 6; matrix products, arithmetic and copies ran while one was open for 0% -> 0% of each run, Pallas kernels for 3% -> 3%
where the time goes in v2:
time: 82.7 us; the launch traced here: 82.4 us
  waiting for transfers between devices  49.4 us (60%)
  starting transfers between devices  19.9 us (24%)
  Pallas kernels  11.4 us (14%)
    all_to_all x2, waiting for transfers between devices, exchanged(): return lax.all_to_all(parts, AXES, 0, 0, tiled=True)  25.2 us
    ppermute x6, waiting for transfers between devices, partnered(): return lax.ppermute(block, AXES, [(i, i ^ bit) for i in range(devices)])  24.2 us
    all_to_all x2, starting transfers between devices, exchanged(): return lax.all_to_all(parts, AXES, 0, 0, tiled=True)  10.9 us
    ppermute x6, starting transfers between devices, partnered(): return lax.ppermute(block, AXES, [(i, i ^ bit) for i in range(devices)])  9.02 us
    pallas_call x1, Pallas kernels, local(): pl.pallas_call(functools.partial(stack_kernel, share), out_shape=[shape(p...  4.72 us
    pallas_call x1, Pallas kernels, local(): pl.pallas_call(functools.partial(pack_kernel, share), out_shape=shape(fie...  2.97 us
  transfers between devices with their start and end apart: 8, of which 6 were waited for; matrix products, arithmetic and copies ran while one was open for 0% of the time, Pallas kernels for 3%

profile of v2, /device:TPU:0, one launch (start us, length us, event | category | flops | bytes accessed | tf_op | source)
XLA Modules:
  0.0 82.4 jit_solution(17801345479314813258)
XLA Ops:
  0.6 3.0 %shard_map.75 = bf16[32,128,128]{2,1,0:T(8,128)(2,1)} custom-call(bf16[64,16,256]{2,1,0:T(8,128)(2,1)} %x_ref.1, bf16[64,16,256]{2,1,0:T(8,128)(2,1)} %cot_ref.1), custom_call_target="tpu_custom_call" | custom-call | tf_op jit(solution)/shard_map/pallas_call | solution.py:312
  3.6 0.0 copy-start
  3.6 7.3 %all-to-all-start = ((bf16[32,128,128]{2,1,0:T(8,128)(2,1)}), bf16[32,128,128]{2,1,0:T(8,128)(2,1)S(1)}, u32[]{:S(2)}, u32[]{:S(2)}) async-start(bf16[32,128,128]{2,1,0:T(8,128)(2,1)} %shard_map.75), calls=%async_computation | async-start | bytes 2097152 | tf_op jit(solution)/shard_map/all_to_all | solution.py:293
  10.9 0.0 copy-start.1
  10.9 0.7 copy-done.1
  11.6 0.1 copy.8.b_ref
  11.7 0.0 copy-done
  11.7 0.2 shard_map.76.w_ref
  12.0 25.2 %all-to-all-done.parts_ref = bf16[32,128,128]{2,1,0:T(8,128)(2,1)S(1)} async-done(((bf16[32,128,128]{2,1,0:T(8,128)(2,1)}), bf16[32,128,128]{2,1,0:T(8,128)(2,1)S(1)}, u32[]{:S(2)}, u32[]{:S(2)}) %all-to-all-start) | async-done | bytes 1048608 | tf_op jit(solution)/shard_map/all_to_all | solution.py:293
  37.2 4.7 %shard_map.77 = (bf16[32,128,128]{2,1,0:T(8,128)(2,1)}, bf16[8,64,512]{2,1,0:T(8,128)(2,1)S(1)}, f32[192,192]{1,0:T(8,128)S(1)}, f32[16,64]{1,0:T(8,128)S(1)}) custom-call(bf16[32,128,128]{2,1,0:T(8,128)(2,1)S(1)} %all-to-all-done.parts_ref, bf16[4,192,192]{2,1,0:T(8,128)(2,1)S(1)} %shard_map.76.w_ref, f32[2,64,1]{2,1,0:T(8,128)S(1)} %copy.8.b_ref), custom_call_target="tpu_custom_call" | custom-call | tf_op jit(solution)/shard_map/pallas_call | solution.py:338
  41.9 3.6 %all-to-all-start.1 = ((bf16[32,128,128]{2,1,0:T(8,128)(2,1)}), bf16[32,128,128]{2,1,0:T(8,128)(2,1)S(1)}, u32[]{:S(2)}, u32[]{:S(2)}) async-start(bf16[32,128,128]{2,1,0:T(8,128)(2,1)} %get-tuple-element.20), calls=%async_computation.1 | async-start | bytes 2097152 | tf_op jit(solution)/shard_map/all_to_all | solution.py:293
  45.5 0.8 shard_map.78
  46.3 0.3 collective-permute-start
  46.7 1.0 %collective-permute-done = bf16[304,128]{1,0:T(8,128)(2,1)S(1)} collective-permute-done((bf16[304,128]{1,0:T(8,128)(2,1)S(1)}, bf16[304,128]{1,0:T(8,128)(2,1)S(1)}, u32[]{:S(2)}, u32[]{:S(2)}) %collective-permute-start) | collective-permute-done | bytes 77856 | tf_op jit(solution)/shard_map/ppermute | solution.py:280
  47.7 1.8 %collective-permute-start.1 = (bf16[304,128]{1,0:T(8,128)(2,1)S(1)}, bf16[304,128]{1,0:T(8,128)(2,1)S(1)}, u32[]{:S(2)}, u32[]{:S(2)}) collective-permute-start(bf16[304,128]{1,0:T(8,128)(2,1)S(1)} %add_convert_fusion.4), channel_id=1, source_target_pairs={{0,4},{1,5},{2,6},{3,7},{4,0},{5,1},{6,2},{7,3},{8,12},{9,13},{10,... | collective-permute-start | bytes 233480 | tf_op jit(solution)/shard_map/ppermute | solution.py:280
  49.5 7.2 %collective-permute-done.1 = bf16[304,128]{1,0:T(8,128)(2,1)S(1)} collective-permute-done((bf16[304,128]{1,0:T(8,128)(2,1)S(1)}, bf16[304,128]{1,0:T(8,128)(2,1)S(1)}, u32[]{:S(2)}, u32[]{:S(2)}) %collective-permute-start.1) | collective-permute-done | bytes 77856 | tf_op jit(solution)/shard_map/ppermute | solution.py:280
  56.8 0.7 collective-permute-start.2
  57.5 7.3 %collective-permute-done.2 = bf16[304,128]{1,0:T(8,128)(2,1)S(1)} collective-permute-done((bf16[304,128]{1,0:T(8,128)(2,1)S(1)}, bf16[304,128]{1,0:T(8,128)(2,1)S(1)}, u32[]{:S(2)}, u32[]{:S(2)}) %collective-permute-start.2) | collective-permute-done | bytes 77856 | tf_op jit(solution)/shard_map/ppermute | solution.py:280
  64.9 4.6 %collective-permute-start.3 = (bf16[304,128]{1,0:T(8,128)(2,1)S(1)}, bf16[304,128]{1,0:T(8,128)(2,1)S(1)}, u32[]{:S(2)}, u32[]{:S(2)}) collective-permute-start(bf16[304,128]{1,0:T(8,128)(2,1)S(1)} %add_convert_fusion.2), channel_id=1, source_target_pairs={{0,16},{1,17},{2,18},{3,19},{4,20},{5,21},{6,22},{7,23},{8,24},{9,... | collective-permute-start | bytes 233480 | tf_op jit(solution)/shard_map/ppermute | solution.py:280
  69.4 5.7 %collective-permute-done.3 = bf16[304,128]{1,0:T(8,128)(2,1)S(1)} collective-permute-done((bf16[304,128]{1,0:T(8,128)(2,1)S(1)}, bf16[304,128]{1,0:T(8,128)(2,1)S(1)}, u32[]{:S(2)}, u32[]{:S(2)}) %collective-permute-start.3) | collective-permute-done | bytes 77856 | tf_op jit(solution)/shard_map/ppermute | solution.py:280
  75.1 1.5 %collective-permute-start.4 = (bf16[304,128]{1,0:T(8,128)(2,1)S(1)}, bf16[304,128]{1,0:T(8,128)(2,1)S(1)}, u32[]{:S(2)}, u32[]{:S(2)}) collective-permute-start(bf16[304,128]{1,0:T(8,128)(2,1)S(1)} %add_convert_fusion.1), channel_id=1, source_target_pairs={{0,2},{1,3},{2,0},{3,1},{4,6},{5,7},{6,4},{7,5},{8,10},{9,11},{10,... | collective-permute-start | bytes 233480 | tf_op jit(solution)/shard_map/ppermute | solution.py:280
  76.7 2.9 %collective-permute-done.4 = bf16[304,128]{1,0:T(8,128)(2,1)S(1)} collective-permute-done((bf16[304,128]{1,0:T(8,128)(2,1)S(1)}, bf16[304,128]{1,0:T(8,128)(2,1)S(1)}, u32[]{:S(2)}, u32[]{:S(2)}) %collective-permute-start.4) | collective-permute-done | bytes 77856 | tf_op jit(solution)/shard_map/ppermute | solution.py:280
  79.6 0.0 all-to-all-done.1.parts_ref
  79.6 0.1 collective-permute-start.5
  79.7 1.6 %shard_map.79 = (bf16[64,16,256]{2,1,0:T(8,128)(2,1)}, bf16[64,16,256]{2,1,0:T(8,128)(2,1)}) custom-call(bf16[32,128,128]{2,1,0:T(8,128)(2,1)S(1)} %all-to-all-done.1.parts_ref), custom_call_target="tpu_custom_call" | custom-call | flops 268435456 | bytes 2097152 | tf_op jit(solution)/shard_map/pallas_call | solution.py:375
  81.3 0.0 collective-permute-done.5.other_ref
  81.3 1.0 %shard_map.80 = (f32[2,3,3,64,64]{4,3,2,1,0:T(8,128)}, f32[2,64]{1,0:T(2,128)}) custom-call(bf16[304,128]{1,0:T(8,128)(2,1)S(1)} %add_convert_fusion.mine_ref, bf16[304,128]{1,0:T(8,128)(2,1)S(1)} %collective-permute-done.5.other_ref), custom_call_target="tpu_custom_call" | custom-call | tf_op jit(solution)/shard_map/pallas_call | solution.py:388
  (5 shorter events, 0.1 us)
Async XLA Ops:
  3.6 8.1 %copy-start = (bf16[2,3,3,64,64]{4,3,2,1,0:T(8,128)(2,1)S(1)}, bf16[2,3,3,64,64]{4,3,2,1,0:T(8,128)(2,1)}, u32[]{:S(2)}) copy-start(bf16[2,3,3,64,64]{4,3,2,1,0:T(8,128)(2,1)} %w_ref) | copy-start | bytes 442372
  3.6 33.5 %all-to-all-start = ((bf16[32,128,128]{2,1,0:T(8,128)(2,1)}), bf16[32,128,128]{2,1,0:T(8,128)(2,1)S(1)}, u32[]{:S(2)}, u32[]{:S(2)}) async-start(bf16[32,128,128]{2,1,0:T(8,128)(2,1)} %shard_map.75), calls=%async_computation | async-start | bytes 2097152 | tf_op jit(solution)/shard_map/all_to_all | solution.py:293
  10.9 0.7 copy-start.1
  41.9 37.7 %all-to-all-start.1 = ((bf16[32,128,128]{2,1,0:T(8,128)(2,1)}), bf16[32,128,128]{2,1,0:T(8,128)(2,1)S(1)}, u32[]{:S(2)}, u32[]{:S(2)}) async-start(bf16[32,128,128]{2,1,0:T(8,128)(2,1)} %get-tuple-element.20), calls=%async_computation.1 | async-start | bytes 2097152 | tf_op jit(solution)/shard_map/all_to_all | solution.py:293
  46.3 1.3 %collective-permute-start = (bf16[304,128]{1,0:T(8,128)(2,1)S(1)}, bf16[304,128]{1,0:T(8,128)(2,1)S(1)}, u32[]{:S(2)}, u32[]{:S(2)}) collective-permute-start(bf16[304,128]{1,0:T(8,128)(2,1)S(1)} %get-tuple-element.25), channel_id=1, source_target_pairs={{0,1},{1,0},{2,3},{3,2},{4,5},{5,4},{6,7},{7,6},{8,9},{9,8},{10,11... | collective-permute-start | bytes 233480 | tf_op jit(solution)/shard_map/ppermute | solution.py:280
  47.7 9.1 %collective-permute-start.1 = (bf16[304,128]{1,0:T(8,128)(2,1)S(1)}, bf16[304,128]{1,0:T(8,128)(2,1)S(1)}, u32[]{:S(2)}, u32[]{:S(2)}) collective-permute-start(bf16[304,128]{1,0:T(8,128)(2,1)S(1)} %add_convert_fusion.4), channel_id=1, source_target_pairs={{0,4},{1,5},{2,6},{3,7},{4,0},{5,1},{6,2},{7,3},{8,12},{9,13},{10,... | collective-permute-start | bytes 233480 | tf_op jit(solution)/shard_map/ppermute | solution.py:280
  56.8 8.0 %collective-permute-start.2 = (bf16[304,128]{1,0:T(8,128)(2,1)S(1)}, bf16[304,128]{1,0:T(8,128)(2,1)S(1)}, u32[]{:S(2)}, u32[]{:S(2)}) collective-permute-start(bf16[304,128]{1,0:T(8,128)(2,1)S(1)} %add_convert_fusion.3), channel_id=1, source_target_pairs={{0,8},{1,9},{2,10},{3,11},{4,12},{5,13},{6,14},{7,15},{8,0},{9,1},... | collective-permute-start | bytes 233480 | tf_op jit(solution)/shard_map/ppermute | solution.py:280
  64.9 10.2 %collective-permute-start.3 = (bf16[304,128]{1,0:T(8,128)(2,1)S(1)}, bf16[304,128]{1,0:T(8,128)(2,1)S(1)}, u32[]{:S(2)}, u32[]{:S(2)}) collective-permute-start(bf16[304,128]{1,0:T(8,128)(2,1)S(1)} %add_convert_fusion.2), channel_id=1, source_target_pairs={{0,16},{1,17},{2,18},{3,19},{4,20},{5,21},{6,22},{7,23},{8,24},{9,... | collective-permute-start | bytes 233480 | tf_op jit(solution)/shard_map/ppermute | solution.py:280
  75.1 4.5 %collective-permute-start.4 = (bf16[304,128]{1,0:T(8,128)(2,1)S(1)}, bf16[304,128]{1,0:T(8,128)(2,1)S(1)}, u32[]{:S(2)}, u32[]{:S(2)}) collective-permute-start(bf16[304,128]{1,0:T(8,128)(2,1)S(1)} %add_convert_fusion.1), channel_id=1, source_target_pairs={{0,2},{1,3},{2,0},{3,1},{4,6},{5,7},{6,4},{7,5},{8,10},{9,11},{10,... | collective-permute-start | bytes 233480 | tf_op jit(solution)/shard_map/ppermute | solution.py:280
  79.6 1.7 %collective-permute-start.5 = (bf16[304,128]{1,0:T(8,128)(2,1)S(1)}, bf16[304,128]{1,0:T(8,128)(2,1)S(1)}, u32[]{:S(2)}, u32[]{:S(2)}) collective-permute-start(bf16[304,128]{1,0:T(8,128)(2,1)S(1)} %add_convert_fusion.mine_ref), channel_id=1, source_target_pairs={{0,1},{1,0},{2,3},{3,2},{4,5},{5,4},{6,7},{7,6},{8,9},{9,8},{10,11... | collective-permute-start | bytes 233480 | tf_op jit(solution)/shard_map/ppermute | solution.py:280

commit v3 on v2

--- a/solution.py
+++ b/solution.py
@@ -11,7 +11,7 @@
 
 AXES = ("lon", "lat")
 LANES = 128
-TAIL = 32
+TAIL = 64
 BF16, F32 = jnp.bfloat16, jnp.float32
 PARAMS = pltpu.CompilerParams(vmem_limit_bytes=24 * 2**20)
 WIDE = pltpu.CompilerParams(vmem_limit_bytes=56 * 2**20)
@@ -230,6 +230,12 @@
         started.wait()
 
 
+def quarters():
+    lat = lax.axis_index("lat")
+    odd, upper = lat & 1, lax.div(lat, 2) & 1
+    return 2 * odd + upper, 2 * odd + 1 - upper, 2 * (1 - odd) + upper, 3 - 2 * odd - upper
+
+
 def sums_kernel(share, parts_ref, gz_ref, total_ref, bias_ref, keep_ref, send_ref, rows_ref):
     count, channels, _ = gz_ref.shape
     high = 3 * channels
@@ -249,18 +255,23 @@
     bias = jnp.concatenate([bias[:1], bias_ref[:1]], axis=1)
     row = lax.broadcasted_iota(jnp.int32, (TAIL, 2 * channels), 0)
     rows_ref[3 * high :, :] = jnp.where(row == 0, bias, 0.0)
-    half = keep_ref.shape[0]
-    odd = lax.axis_index("lat") & 1
-    keep_ref[...] = rows_ref[pl.ds(pl.multiple_of(odd * half, 16), half), :]
-    send_ref[...] = rows_ref[pl.ds(pl.multiple_of((1 - odd) * half, 16), half), :].astype(BF16)
-
-
-def assemble_kernel(scale, mine_ref, other_ref, out_ref, bias_ref, total_ref):
+    size = keep_ref.shape[0] // 2
+    for at, quarter in enumerate(quarters()):
+        rows = rows_ref[pl.ds(pl.multiple_of(quarter * size, 16), size), :]
+        place = slice((at % 2) * size, (at % 2 + 1) * size)
+        if at < 2:
+            keep_ref[place, :] = rows
+        else:
+            send_ref[place, :] = rows.astype(BF16)
+
+
+def assemble_kernel(scale, pair_ref, other_ref, out_ref, bias_ref, total_ref):
     channels = out_ref.shape[-1]
-    half = mine_ref.shape[0]
-    odd = lax.axis_index("lat") & 1
-    for side, ref in ((odd, mine_ref), (1 - odd, other_ref)):
-        total_ref[pl.ds(pl.multiple_of(side * half, 16), half), :] = ref[...].astype(F32) * scale
+    size = pair_ref.shape[0] // 2
+    for at, quarter in enumerate(quarters()):
+        ref = pair_ref if at < 2 else other_ref
+        rows = ref[(at % 2) * size : (at % 2 + 1) * size, :].astype(F32) * scale
+        total_ref[pl.ds(pl.multiple_of(quarter * size, 16), size), :] = rows
     high = 3 * channels
     for layer in range(2):
         for b in range(3):
@@ -281,11 +292,14 @@
 
 
 def added(keep, send, devices):
-    total = keep + partnered(send, devices, 1).astype(F32)
-    bits = [4 << k for k in range((devices // 4).bit_length() - 1)] + [2]
-    for bit in bits:
+    size = keep.shape[0] // 2
+    keep = keep + partnered(send, devices, 1).astype(F32)
+    total = keep[:size] + partnered(keep[size:].astype(BF16), devices, 2).astype(F32)
+    bit = 4
+    while bit < devices:
         rounded = total.astype(BF16)
         total = rounded.astype(F32) + partnered(rounded, devices, bit).astype(F32)
+        bit *= 2
     return total.astype(BF16)
 
 
@@ -371,7 +385,8 @@
     )(parts, gated, total, bias_sums)
     mine = added(keep, send, devices)
     home, mine = lax.optimization_barrier((home, mine))
-    other = partnered(mine, devices, 1)
+    pair = jnp.concatenate([mine, partnered(mine, devices, 2)], axis=0)
+    other = partnered(pair, devices, 1)
     features_out, grad_input = pl.pallas_call(
         functools.partial(unpack_kernel, share),
         out_shape=[shape(inputs.shape, BF16), shape(inputs.shape, BF16)],
@@ -390,7 +405,7 @@
         out_shape=[shape(weights.shape, F32), shape(biases.shape, F32)],
         scratch_shapes=[pltpu.VMEM((rows, 2 * channels), F32)],
         compiler_params=PARAMS,
-    )(mine, other)
+    )(pair, other)
     return features_out, grad_input, weight_grads, bias_grads
 
 

time: 82.7 us -> 80.7 us (0.976)
  waiting for transfers between devices: 49.4 us -> 47.5 us
    ppermute x6 -> x7, waiting for transfers between devices: 24.2 us -> 22.3 us  [partnered(): return lax.ppermute(block, AXES, [(i, i ^ bit) for i in range(devices)])]
    ppermute x6 -> x7, starting transfers between devices: 9.02 us -> 8.87 us  [partnered(): return lax.ppermute(block, AXES, [(i, i ^ bit) for i in range(devices)])]
  transfers between devices with their start and end apart: 8 -> 9, of which waited for: 6 -> 7; matrix products, arithmetic and copies ran while one was open for 0% -> 0% of each run, Pallas kernels for 3% -> 3%
where the time goes in v3:
time: 80.7 us; the launch traced here: 80.4 us
  waiting for transfers between devices  47.5 us (59%)
  starting transfers between devices  19.8 us (25%)
  Pallas kernels  11.4 us (14%)
    all_to_all x2, waiting for transfers between devices, exchanged(): return lax.all_to_all(parts, AXES, 0, 0, tiled=True)  25.2 us
    ppermute x7, waiting for transfers between devices, partnered(): return lax.ppermute(block, AXES, [(i, i ^ bit) for i in range(devices)])  22.3 us
    all_to_all x2, starting transfers between devices, exchanged(): return lax.all_to_all(parts, AXES, 0, 0, tiled=True)  10.9 us
    ppermute x7, starting transfers between devices, partnered(): return lax.ppermute(block, AXES, [(i, i ^ bit) for i in range(devices)])  8.87 us
    pallas_call x1, Pallas kernels, local(): pl.pallas_call(functools.partial(stack_kernel, share), out_shape=[shape(p...  4.73 us
    pallas_call x1, Pallas kernels, local(): pl.pallas_call(functools.partial(pack_kernel, share), out_shape=shape(fie...  2.99 us
    pallas_call x1, Pallas kernels, local(): pl.pallas_call(functools.partial(unpack_kernel, share), out_shape=[shape(...  1.62 us
  transfers between devices with their start and end apart: 9, of which 7 were waited for; matrix products, arithmetic and copies ran while one was open for 0% of the time, Pallas kernels for 3%

profile of v3, /device:TPU:0, one launch (start us, length us, event | category | flops | bytes accessed | tf_op | source)
XLA Modules:
  0.0 80.4 jit_solution(6879888663236107062)
XLA Ops:
  0.6 3.0 %shard_map.75 = bf16[32,128,128]{2,1,0:T(8,128)(2,1)} custom-call(bf16[64,16,256]{2,1,0:T(8,128)(2,1)} %x_ref.1, bf16[64,16,256]{2,1,0:T(8,128)(2,1)} %cot_ref.1), custom_call_target="tpu_custom_call" | custom-call | tf_op jit(solution)/shard_map/pallas_call | solution.py:326
  3.6 0.0 copy-start
  3.6 7.3 %all-to-all-start = ((bf16[32,128,128]{2,1,0:T(8,128)(2,1)}), bf16[32,128,128]{2,1,0:T(8,128)(2,1)S(1)}, u32[]{:S(2)}, u32[]{:S(2)}) async-start(bf16[32,128,128]{2,1,0:T(8,128)(2,1)} %shard_map.75), calls=%async_computation | async-start | bytes 2097152 | tf_op jit(solution)/shard_map/all_to_all | solution.py:307
  10.9 0.0 copy-start.1
  11.0 0.7 copy-done.1
  11.6 0.1 copy.8.b_ref
  11.7 0.0 copy-done
  11.7 0.2 shard_map.76.w_ref
  12.0 25.2 %all-to-all-done.parts_ref = bf16[32,128,128]{2,1,0:T(8,128)(2,1)S(1)} async-done(((bf16[32,128,128]{2,1,0:T(8,128)(2,1)}), bf16[32,128,128]{2,1,0:T(8,128)(2,1)S(1)}, u32[]{:S(2)}, u32[]{:S(2)}) %all-to-all-start) | async-done | bytes 1048608 | tf_op jit(solution)/shard_map/all_to_all | solution.py:307
  37.2 4.7 %shard_map.77 = (bf16[32,128,128]{2,1,0:T(8,128)(2,1)}, bf16[8,64,512]{2,1,0:T(8,128)(2,1)S(1)}, f32[192,192]{1,0:T(8,128)S(1)}, f32[16,64]{1,0:T(8,128)S(1)}) custom-call(bf16[32,128,128]{2,1,0:T(8,128)(2,1)S(1)} %all-to-all-done.parts_ref, bf16[4,192,192]{2,1,0:T(8,128)(2,1)S(1)} %shard_map.76.w_ref, f32[2,64,1]{2,1,0:T(8,128)S(1)} %copy.8.b_ref), custom_call_target="tpu_custom_call" | custom-call | tf_op jit(solution)/shard_map/pallas_call | solution.py:352
  41.9 3.6 %all-to-all-start.1 = ((bf16[32,128,128]{2,1,0:T(8,128)(2,1)}), bf16[32,128,128]{2,1,0:T(8,128)(2,1)S(1)}, u32[]{:S(2)}, u32[]{:S(2)}) async-start(bf16[32,128,128]{2,1,0:T(8,128)(2,1)} %get-tuple-element.20), calls=%async_computation.1 | async-start | bytes 2097152 | tf_op jit(solution)/shard_map/all_to_all | solution.py:307
  45.6 0.8 shard_map.78
  46.4 0.3 collective-permute-start
  46.7 1.0 %collective-permute-done = bf16[320,128]{1,0:T(8,128)(2,1)S(1)} collective-permute-done((bf16[320,128]{1,0:T(8,128)(2,1)S(1)}, bf16[320,128]{1,0:T(8,128)(2,1)S(1)}, u32[]{:S(2)}, u32[]{:S(2)}) %collective-permute-start) | collective-permute-done | bytes 81952 | tf_op jit(solution)/shard_map/ppermute | solution.py:291
  47.7 1.8 %collective-permute-start.1 = (bf16[160,128]{1,0:T(8,128)(2,1)S(1)}, bf16[160,128]{1,0:T(8,128)(2,1)S(1)}, u32[]{:S(2)}, u32[]{:S(2)}) collective-permute-start(bf16[160,128]{1,0:T(8,128)(2,1)S(1)} %slice.15), channel_id=1, source_target_pairs={{0,2},{1,3},{2,0},{3,1},{4,6},{5,7},{6,4},{7,5},{8,10},{9,11},{10,... | collective-permute-start | bytes 122888 | tf_op jit(solution)/shard_map/ppermute | solution.py:291
  49.6 5.9 %collective-permute-done.1 = bf16[160,128]{1,0:T(8,128)(2,1)S(1)} collective-permute-done((bf16[160,128]{1,0:T(8,128)(2,1)S(1)}, bf16[160,128]{1,0:T(8,128)(2,1)S(1)}, u32[]{:S(2)}, u32[]{:S(2)}) %collective-permute-start.1) | collective-permute-done | bytes 40992 | tf_op jit(solution)/shard_map/ppermute | solution.py:291
  55.5 1.5 %collective-permute-start.2 = (bf16[160,128]{1,0:T(8,128)(2,1)S(1)}, bf16[160,128]{1,0:T(8,128)(2,1)S(1)}, u32[]{:S(2)}, u32[]{:S(2)}) collective-permute-start(bf16[160,128]{1,0:T(8,128)(2,1)S(1)} %fusion), channel_id=1, source_target_pairs={{0,4},{1,5},{2,6},{3,7},{4,0},{5,1},{6,2},{7,3},{8,12},{9,13},{10,... | collective-permute-start | bytes 122888 | tf_op jit(solution)/shard_map/ppermute | solution.py:291
  57.1 2.9 %collective-permute-done.2 = bf16[160,128]{1,0:T(8,128)(2,1)S(1)} collective-permute-done((bf16[160,128]{1,0:T(8,128)(2,1)S(1)}, bf16[160,128]{1,0:T(8,128)(2,1)S(1)}, u32[]{:S(2)}, u32[]{:S(2)}) %collective-permute-start.2) | collective-permute-done | bytes 40992 | tf_op jit(solution)/shard_map/ppermute | solution.py:291
  60.0 0.6 collective-permute-start.3
  60.5 5.1 %collective-permute-done.3 = bf16[160,128]{1,0:T(8,128)(2,1)S(1)} collective-permute-done((bf16[160,128]{1,0:T(8,128)(2,1)S(1)}, bf16[160,128]{1,0:T(8,128)(2,1)S(1)}, u32[]{:S(2)}, u32[]{:S(2)}) %collective-permute-start.3) | collective-permute-done | bytes 40992 | tf_op jit(solution)/shard_map/ppermute | solution.py:291
  65.6 3.0 %collective-permute-start.4 = (bf16[160,128]{1,0:T(8,128)(2,1)S(1)}, bf16[160,128]{1,0:T(8,128)(2,1)S(1)}, u32[]{:S(2)}, u32[]{:S(2)}) collective-permute-start(bf16[160,128]{1,0:T(8,128)(2,1)S(1)} %add_convert_fusion.1), channel_id=1, source_target_pairs={{0,16},{1,17},{2,18},{3,19},{4,20},{5,21},{6,22},{7,23},{8,24},{9,... | collective-permute-start | bytes 122888 | tf_op jit(solution)/shard_map/ppermute | solution.py:291
  68.6 4.9 %collective-permute-done.4 = bf16[160,128]{1,0:T(8,128)(2,1)S(1)} collective-permute-done((bf16[160,128]{1,0:T(8,128)(2,1)S(1)}, bf16[160,128]{1,0:T(8,128)(2,1)S(1)}, u32[]{:S(2)}, u32[]{:S(2)}) %collective-permute-start.4) | collective-permute-done | bytes 40992 | tf_op jit(solution)/shard_map/ppermute | solution.py:291
  73.6 0.0 all-to-all-done.1.parts_ref
  73.6 1.5 %collective-permute-start.5 = (bf16[160,128]{1,0:T(8,128)(2,1)S(1)}, bf16[160,128]{1,0:T(8,128)(2,1)S(1)}, u32[]{:S(2)}, u32[]{:S(2)}) collective-permute-start(bf16[160,128]{1,0:T(8,128)(2,1)S(1)} %add_convert_fusion), channel_id=1, source_target_pairs={{0,2},{1,3},{2,0},{3,1},{4,6},{5,7},{6,4},{7,5},{8,10},{9,11},{10,... | collective-permute-start | bytes 122888 | tf_op jit(solution)/shard_map/ppermute | solution.py:291
  75.1 2.5 %collective-permute-done.5 = bf16[160,128]{1,0:T(8,128)(2,1)S(1)} collective-permute-done((bf16[160,128]{1,0:T(8,128)(2,1)S(1)}, bf16[160,128]{1,0:T(8,128)(2,1)S(1)}, u32[]{:S(2)}, u32[]{:S(2)}) %collective-permute-start.5) | collective-permute-done | bytes 40992 | tf_op jit(solution)/shard_map/ppermute | solution.py:291
  77.7 0.1 collective-permute-start.6
  77.7 1.6 %shard_map.79 = (bf16[64,16,256]{2,1,0:T(8,128)(2,1)}, bf16[64,16,256]{2,1,0:T(8,128)(2,1)}) custom-call(bf16[32,128,128]{2,1,0:T(8,128)(2,1)S(1)} %all-to-all-done.1.parts_ref), custom_call_target="tpu_custom_call" | custom-call | flops 268435456 | bytes 2097152 | tf_op jit(solution)/shard_map/pallas_call | solution.py:390
  79.4 0.0 collective-permute-done.6.other_ref
  79.4 1.0 %shard_map.80 = (f32[2,3,3,64,64]{4,3,2,1,0:T(8,128)}, f32[2,64]{1,0:T(2,128)}) custom-call(bf16[320,128]{1,0:T(8,128)(2,1)S(1)} %constant_dynamic-update-slice_fusion.pair_ref, bf16[320,128]{1,0:T(8,128)(2,1)S(1)} %collective-permute-done.6.other_ref), custom_call_target="tpu_custom_call" | custom-call | tf_op jit(solution)/shard_map/pallas_call | solution.py:403
  (8 shorter events, 0.1 us)
Async XLA Ops:
  3.6 8.1 %copy-start = (bf16[2,3,3,64,64]{4,3,2,1,0:T(8,128)(2,1)S(1)}, bf16[2,3,3,64,64]{4,3,2,1,0:T(8,128)(2,1)}, u32[]{:S(2)}) copy-start(bf16[2,3,3,64,64]{4,3,2,1,0:T(8,128)(2,1)} %w_ref) | copy-start | bytes 442372
  3.6 33.5 %all-to-all-start = ((bf16[32,128,128]{2,1,0:T(8,128)(2,1)}), bf16[32,128,128]{2,1,0:T(8,128)(2,1)S(1)}, u32[]{:S(2)}, u32[]{:S(2)}) async-start(bf16[32,128,128]{2,1,0:T(8,128)(2,1)} %shard_map.75), calls=%async_computation | async-start | bytes 2097152 | tf_op jit(solution)/shard_map/all_to_all | solution.py:307
  10.9 0.7 copy-start.1
  41.9 31.7 %all-to-all-start.1 = ((bf16[32,128,128]{2,1,0:T(8,128)(2,1)}), bf16[32,128,128]{2,1,0:T(8,128)(2,1)S(1)}, u32[]{:S(2)}, u32[]{:S(2)}) async-start(bf16[32,128,128]{2,1,0:T(8,128)(2,1)} %get-tuple-element.20), calls=%async_computation.1 | async-start | bytes 2097152 | tf_op jit(solution)/shard_map/all_to_all | solution.py:307
  46.4 1.3 %collective-permute-start = (bf16[320,128]{1,0:T(8,128)(2,1)S(1)}, bf16[320,128]{1,0:T(8,128)(2,1)S(1)}, u32[]{:S(2)}, u32[]{:S(2)}) collective-permute-start(bf16[320,128]{1,0:T(8,128)(2,1)S(1)} %get-tuple-element.25), channel_id=1, source_target_pairs={{0,1},{1,0},{2,3},{3,2},{4,5},{5,4},{6,7},{7,6},{8,9},{9,8},{10,11... | collective-permute-start | bytes 245768 | tf_op jit(solution)/shard_map/ppermute | solution.py:291
  47.7 7.8 %collective-permute-start.1 = (bf16[160,128]{1,0:T(8,128)(2,1)S(1)}, bf16[160,128]{1,0:T(8,128)(2,1)S(1)}, u32[]{:S(2)}, u32[]{:S(2)}) collective-permute-start(bf16[160,128]{1,0:T(8,128)(2,1)S(1)} %slice.15), channel_id=1, source_target_pairs={{0,2},{1,3},{2,0},{3,1},{4,6},{5,7},{6,4},{7,5},{8,10},{9,11},{10,... | collective-permute-start | bytes 122888 | tf_op jit(solution)/shard_map/ppermute | solution.py:291
  55.5 4.4 %collective-permute-start.2 = (bf16[160,128]{1,0:T(8,128)(2,1)S(1)}, bf16[160,128]{1,0:T(8,128)(2,1)S(1)}, u32[]{:S(2)}, u32[]{:S(2)}) collective-permute-start(bf16[160,128]{1,0:T(8,128)(2,1)S(1)} %fusion), channel_id=1, source_target_pairs={{0,4},{1,5},{2,6},{3,7},{4,0},{5,1},{6,2},{7,3},{8,12},{9,13},{10,... | collective-permute-start | bytes 122888 | tf_op jit(solution)/shard_map/ppermute | solution.py:291
  60.0 5.7 %collective-permute-start.3 = (bf16[160,128]{1,0:T(8,128)(2,1)S(1)}, bf16[160,128]{1,0:T(8,128)(2,1)S(1)}, u32[]{:S(2)}, u32[]{:S(2)}) collective-permute-start(bf16[160,128]{1,0:T(8,128)(2,1)S(1)} %add_convert_fusion.2), channel_id=1, source_target_pairs={{0,8},{1,9},{2,10},{3,11},{4,12},{5,13},{6,14},{7,15},{8,0},{9,1},... | collective-permute-start | bytes 122888 | tf_op jit(solution)/shard_map/ppermute | solution.py:291
  65.6 7.9 %collective-permute-start.4 = (bf16[160,128]{1,0:T(8,128)(2,1)S(1)}, bf16[160,128]{1,0:T(8,128)(2,1)S(1)}, u32[]{:S(2)}, u32[]{:S(2)}) collective-permute-start(bf16[160,128]{1,0:T(8,128)(2,1)S(1)} %add_convert_fusion.1), channel_id=1, source_target_pairs={{0,16},{1,17},{2,18},{3,19},{4,20},{5,21},{6,22},{7,23},{8,24},{9,... | collective-permute-start | bytes 122888 | tf_op jit(solution)/shard_map/ppermute | solution.py:291
  73.6 4.1 %collective-permute-start.5 = (bf16[160,128]{1,0:T(8,128)(2,1)S(1)}, bf16[160,128]{1,0:T(8,128)(2,1)S(1)}, u32[]{:S(2)}, u32[]{:S(2)}) collective-permute-start(bf16[160,128]{1,0:T(8,128)(2,1)S(1)} %add_convert_fusion), channel_id=1, source_target_pairs={{0,2},{1,3},{2,0},{3,1},{4,6},{5,7},{6,4},{7,5},{8,10},{9,11},{10,... | collective-permute-start | bytes 122888 | tf_op jit(solution)/shard_map/ppermute | solution.py:291
  77.7 1.7 %collective-permute-start.6 = (bf16[320,128]{1,0:T(8,128)(2,1)S(1)}, bf16[320,128]{1,0:T(8,128)(2,1)S(1)}, u32[]{:S(2)}, u32[]{:S(2)}) collective-permute-start(bf16[320,128]{1,0:T(8,128)(2,1)S(1)} %constant_dynamic-update-slice_fusion.pair_ref), channel_id=1, source_target_pairs={{0,1},{1,0},{2,3},{3,2},{4,5},{5,4},{6,7},{7,6},{8,9},{9,8},{10,11... | collective-permute-start | bytes 245768 | tf_op jit(solution)/shard_map/ppermute | solution.py:291

commit v4 on v2

--- a/solution.py
+++ b/solution.py
@@ -180,12 +180,12 @@
         for i in range(count):
             line = line_of(parts_ref, count, channels, 0, i) if layer == 0 else h_ref[i]
             stack = jnp.concatenate(taps(line, hops * share), axis=0)
-            y_ref[i] = product(kernel, stack)
+            y_ref[i] = product(kernel, stack).astype(BF16)
         bias = b_ref[layer]
         for i in range(count):
-            pre = bias + y_ref[i, channels : 2 * channels]
-            pre = pre + y_ref[(i - hops) % count, :channels]
-            pre = pre + y_ref[(i + hops) % count, 2 * channels :]
+            pre = bias + y_ref[i, channels : 2 * channels].astype(F32)
+            pre = pre + y_ref[(i - hops) % count, :channels].astype(F32)
+            pre = pre + y_ref[(i + hops) % count, 2 * channels :].astype(F32)
             sigma = 0.5 * jnp.tanh(0.5 * pre) + 0.5
             state = pre * sigma
             slope = sigma + state * (1.0 - sigma)
@@ -208,15 +208,15 @@
             else:
                 gated = gz_ref[i]
             stack = back_taps(gated, hops * share)
-            y_ref[i] = product(kernel, stack)
+            y_ref[i] = product(kernel, stack).astype(BF16)
             if layer == 1:
                 around = [h_ref[(i + (a - 1) * hops) % count] for a in range(3)]
                 term, bias_term = weight_product(gated, stack, around)
                 total, bias = total + term, bias + bias_term
         for i in range(count):
-            g = y_ref[i, channels : 2 * channels]
-            g = g + y_ref[(i + hops) % count, :channels]
-            g = g + y_ref[(i - hops) % count, 2 * channels :]
+            g = y_ref[i, channels : 2 * channels].astype(F32)
+            g = g + y_ref[(i + hops) % count, :channels].astype(F32)
+            g = g + y_ref[(i - hops) % count, 2 * channels :].astype(F32)
             g = g.astype(BF16)
             if layer == 1:
                 gz_ref[i] = (g.astype(F32) * s0_ref[i]).astype(BF16)
@@ -282,8 +282,7 @@
 
 def added(keep, send, devices):
     total = keep + partnered(send, devices, 1).astype(F32)
-    bits = [4 << k for k in range((devices // 4).bit_length() - 1)] + [2]
-    for bit in bits:
+    for bit in [2 << k for k in range((devices // 2).bit_length() - 1)]:
         rounded = total.astype(BF16)
         total = rounded.astype(F32) + partnered(rounded, devices, bit).astype(F32)
     return total.astype(BF16)
@@ -348,7 +347,7 @@
             pltpu.VMEM(cells, BF16),
             pltpu.VMEM(cells, F32),
             pltpu.VMEM(cells, F32),
-            pltpu.VMEM((lons, 3 * channels, span), F32),
+            pltpu.VMEM((lons, 3 * channels, span), BF16),
             pltpu.VMEM(parts.shape, BF16),
             pltpu.SemaphoreType.DMA((lons + 1,)),
         ],

time: 82.7 us -> 78 us (0.943)
  waiting for transfers between devices: 49.4 us -> 46.2 us
  starting transfers between devices: 19.9 us -> 18.6 us
    ppermute x6, waiting for transfers between devices: 24.2 us -> 21 us  [partnered(): return lax.ppermute(block, AXES, [(i, i ^ bit) for i in range(devices)])]
    ppermute x6, starting transfers between devices: 9.02 us -> 7.7 us  [partnered(): return lax.ppermute(block, AXES, [(i, i ^ bit) for i in range(devices)])]
where the time goes in v4:
time: 78 us; the launch traced here: 77.7 us
  waiting for transfers between devices  46.2 us (59%)
  starting transfers between devices  18.6 us (24%)
  Pallas kernels  11.2 us (14%)
  local copies, waits for them, and re-layouts  0.78 us (1%)
    all_to_all x2, waiting for transfers between devices, exchanged(): return lax.all_to_all(parts, AXES, 0, 0, tiled=True)  25.2 us
    ppermute x6, waiting for transfers between devices, partnered(): return lax.ppermute(block, AXES, [(i, i ^ bit) for i in range(devices)])  21 us
    all_to_all x2, starting transfers between devices, exchanged(): return lax.all_to_all(parts, AXES, 0, 0, tiled=True)  10.9 us
    ppermute x6, starting transfers between devices, partnered(): return lax.ppermute(block, AXES, [(i, i ^ bit) for i in range(devices)])  7.7 us
    pallas_call x1, Pallas kernels, local(): pl.pallas_call(functools.partial(stack_kernel, share), out_shape=[shape(p...  4.52 us
    pallas_call x1, Pallas kernels, local(): pl.pallas_call(functools.partial(pack_kernel, share), out_shape=shape(fie...  2.97 us
    pallas_call x1, Pallas kernels, local(): pl.pallas_call(functools.partial(unpack_kernel, share), out_shape=[shape(...  1.62 us
  transfers between devices with their start and end apart: 8, of which 6 were waited for; matrix products, arithmetic and copies ran while one was open for 0% of the time, Pallas kernels for 3%

profile of v4, /device:TPU:0, one launch (start us, length us, event | category | flops | bytes accessed | tf_op | source)
XLA Modules:
  0.0 77.7 jit_solution(222199906916870781)
XLA Ops:
  0.6 3.0 %shard_map.75 = bf16[32,128,128]{2,1,0:T(8,128)(2,1)} custom-call(bf16[64,16,256]{2,1,0:T(8,128)(2,1)} %x_ref.1, bf16[64,16,256]{2,1,0:T(8,128)(2,1)} %cot_ref.1), custom_call_target="tpu_custom_call" | custom-call | tf_op jit(solution)/shard_map/pallas_call | solution.py:311
  3.6 0.0 copy-start
  3.6 7.3 %all-to-all-start = ((bf16[32,128,128]{2,1,0:T(8,128)(2,1)}), bf16[32,128,128]{2,1,0:T(8,128)(2,1)S(1)}, u32[]{:S(2)}, u32[]{:S(2)}) async-start(bf16[32,128,128]{2,1,0:T(8,128)(2,1)} %shard_map.75), calls=%async_computation | async-start | bytes 2097152 | tf_op jit(solution)/shard_map/all_to_all | solution.py:292
  10.9 0.0 copy-start.1
  10.9 0.7 copy-done.1
  11.6 0.1 copy.8.b_ref
  11.7 0.0 copy-done
  11.7 0.2 shard_map.76.w_ref
  12.0 25.2 %all-to-all-done.parts_ref = bf16[32,128,128]{2,1,0:T(8,128)(2,1)S(1)} async-done(((bf16[32,128,128]{2,1,0:T(8,128)(2,1)}), bf16[32,128,128]{2,1,0:T(8,128)(2,1)S(1)}, u32[]{:S(2)}, u32[]{:S(2)}) %all-to-all-start) | async-done | bytes 1048608 | tf_op jit(solution)/shard_map/all_to_all | solution.py:292
  37.2 4.5 %shard_map.77 = (bf16[32,128,128]{2,1,0:T(8,128)(2,1)}, bf16[8,64,512]{2,1,0:T(8,128)(2,1)S(1)}, f32[192,192]{1,0:T(8,128)S(1)}, f32[16,64]{1,0:T(8,128)S(1)}) custom-call(bf16[32,128,128]{2,1,0:T(8,128)(2,1)S(1)} %all-to-all-done.parts_ref, bf16[4,192,192]{2,1,0:T(8,128)(2,1)S(1)} %shard_map.76.w_ref, f32[2,64,1]{2,1,0:T(8,128)S(1)} %copy.8.b_ref), custom_call_target="tpu_custom_call" | custom-call | tf_op jit(solution)/shard_map/pallas_call | solution.py:337
  41.7 3.6 %all-to-all-start.1 = ((bf16[32,128,128]{2,1,0:T(8,128)(2,1)}), bf16[32,128,128]{2,1,0:T(8,128)(2,1)S(1)}, u32[]{:S(2)}, u32[]{:S(2)}) async-start(bf16[32,128,128]{2,1,0:T(8,128)(2,1)} %get-tuple-element.20), calls=%async_computation.1 | async-start | bytes 2097152 | tf_op jit(solution)/shard_map/all_to_all | solution.py:292
  45.3 0.8 %shard_map.78 = (f32[304,128]{1,0:T(8,128)S(1)}, bf16[304,128]{1,0:T(8,128)(2,1)S(1)}) custom-call(bf16[32,128,128]{2,1,0:T(8,128)(2,1)S(1)} %all-to-all-done.parts_ref, bf16[8,64,512]{2,1,0:T(8,128)(2,1)S(1)} %get-tuple-element.21.gz_ref, f32[192,192]{1,0:T(8,128)S(1)} %get-tuple-element.22.total_ref, f32[16,64]{1,0:T(8,128)S(1)} %get-tuple-element.23.bias_ref), custom_call_target="tpu_custom_call" | custom-call | flops 301989888 | bytes 1572864 | tf_op jit(solution)/shard_map/pallas_call | solution.py:364
  46.1 0.3 collective-permute-start
  46.5 1.0 %collective-permute-done = bf16[304,128]{1,0:T(8,128)(2,1)S(1)} collective-permute-done((bf16[304,128]{1,0:T(8,128)(2,1)S(1)}, bf16[304,128]{1,0:T(8,128)(2,1)S(1)}, u32[]{:S(2)}, u32[]{:S(2)}) %collective-permute-start) | collective-permute-done | bytes 77856 | tf_op jit(solution)/shard_map/ppermute | solution.py:280
  47.5 1.8 %collective-permute-start.1 = (bf16[304,128]{1,0:T(8,128)(2,1)S(1)}, bf16[304,128]{1,0:T(8,128)(2,1)S(1)}, u32[]{:S(2)}, u32[]{:S(2)}) collective-permute-start(bf16[304,128]{1,0:T(8,128)(2,1)S(1)} %add_convert_fusion.4), channel_id=1, source_target_pairs={{0,2},{1,3},{2,0},{3,1},{4,6},{5,7},{6,4},{7,5},{8,10},{9,11},{10,... | collective-permute-start | bytes 233480 | tf_op jit(solution)/shard_map/ppermute | solution.py:280
  49.3 7.2 %collective-permute-done.1 = bf16[304,128]{1,0:T(8,128)(2,1)S(1)} collective-permute-done((bf16[304,128]{1,0:T(8,128)(2,1)S(1)}, bf16[304,128]{1,0:T(8,128)(2,1)S(1)}, u32[]{:S(2)}, u32[]{:S(2)}) %collective-permute-start.1) | collective-permute-done | bytes 77856 | tf_op jit(solution)/shard_map/ppermute | solution.py:280
  56.6 2.0 %collective-permute-start.2 = (bf16[304,128]{1,0:T(8,128)(2,1)S(1)}, bf16[304,128]{1,0:T(8,128)(2,1)S(1)}, u32[]{:S(2)}, u32[]{:S(2)}) collective-permute-start(bf16[304,128]{1,0:T(8,128)(2,1)S(1)} %add_convert_fusion.3), channel_id=1, source_target_pairs={{0,4},{1,5},{2,6},{3,7},{4,0},{5,1},{6,2},{7,3},{8,12},{9,13},{10,... | collective-permute-start | bytes 233480 | tf_op jit(solution)/shard_map/ppermute | solution.py:280
  58.6 3.0 %collective-permute-done.2 = bf16[304,128]{1,0:T(8,128)(2,1)S(1)} collective-permute-done((bf16[304,128]{1,0:T(8,128)(2,1)S(1)}, bf16[304,128]{1,0:T(8,128)(2,1)S(1)}, u32[]{:S(2)}, u32[]{:S(2)}) %collective-permute-start.2) | collective-permute-done | bytes 77856 | tf_op jit(solution)/shard_map/ppermute | solution.py:280
  61.6 1.4 %collective-permute-start.3 = (bf16[304,128]{1,0:T(8,128)(2,1)S(1)}, bf16[304,128]{1,0:T(8,128)(2,1)S(1)}, u32[]{:S(2)}, u32[]{:S(2)}) collective-permute-start(bf16[304,128]{1,0:T(8,128)(2,1)S(1)} %add_convert_fusion.2), channel_id=1, source_target_pairs={{0,8},{1,9},{2,10},{3,11},{4,12},{5,13},{6,14},{7,15},{8,0},{9,1},... | collective-permute-start | bytes 233480 | tf_op jit(solution)/shard_map/ppermute | solution.py:280
  62.9 4.1 %collective-permute-done.3 = bf16[304,128]{1,0:T(8,128)(2,1)S(1)} collective-permute-done((bf16[304,128]{1,0:T(8,128)(2,1)S(1)}, bf16[304,128]{1,0:T(8,128)(2,1)S(1)}, u32[]{:S(2)}, u32[]{:S(2)}) %collective-permute-start.3) | collective-permute-done | bytes 77856 | tf_op jit(solution)/shard_map/ppermute | solution.py:280
  67.1 2.1 %collective-permute-start.4 = (bf16[304,128]{1,0:T(8,128)(2,1)S(1)}, bf16[304,128]{1,0:T(8,128)(2,1)S(1)}, u32[]{:S(2)}, u32[]{:S(2)}) collective-permute-start(bf16[304,128]{1,0:T(8,128)(2,1)S(1)} %add_convert_fusion.1), channel_id=1, source_target_pairs={{0,16},{1,17},{2,18},{3,19},{4,20},{5,21},{6,22},{7,23},{8,24},{9,... | collective-permute-start | bytes 233480 | tf_op jit(solution)/shard_map/ppermute | solution.py:280
  69.2 5.7 %collective-permute-done.4 = bf16[304,128]{1,0:T(8,128)(2,1)S(1)} collective-permute-done((bf16[304,128]{1,0:T(8,128)(2,1)S(1)}, bf16[304,128]{1,0:T(8,128)(2,1)S(1)}, u32[]{:S(2)}, u32[]{:S(2)}) %collective-permute-start.4) | collective-permute-done | bytes 77856 | tf_op jit(solution)/shard_map/ppermute | solution.py:280
  74.9 0.0 all-to-all-done.1.parts_ref
  74.9 0.1 collective-permute-start.5
  75.0 1.6 %shard_map.79 = (bf16[64,16,256]{2,1,0:T(8,128)(2,1)}, bf16[64,16,256]{2,1,0:T(8,128)(2,1)}) custom-call(bf16[32,128,128]{2,1,0:T(8,128)(2,1)S(1)} %all-to-all-done.1.parts_ref), custom_call_target="tpu_custom_call" | custom-call | flops 268435456 | bytes 2097152 | tf_op jit(solution)/shard_map/pallas_call | solution.py:374
  76.6 0.0 collective-permute-done.5.other_ref
  76.7 1.0 %shard_map.80 = (f32[2,3,3,64,64]{4,3,2,1,0:T(8,128)}, f32[2,64]{1,0:T(2,128)}) custom-call(bf16[304,128]{1,0:T(8,128)(2,1)S(1)} %add_convert_fusion.mine_ref, bf16[304,128]{1,0:T(8,128)(2,1)S(1)} %collective-permute-done.5.other_ref), custom_call_target="tpu_custom_call" | custom-call | tf_op jit(solution)/shard_map/pallas_call | solution.py:387
  (5 shorter events, 0.1 us)
Async XLA Ops:
  3.6 8.1 %copy-start = (bf16[2,3,3,64,64]{4,3,2,1,0:T(8,128)(2,1)S(1)}, bf16[2,3,3,64,64]{4,3,2,1,0:T(8,128)(2,1)}, u32[]{:S(2)}) copy-start(bf16[2,3,3,64,64]{4,3,2,1,0:T(8,128)(2,1)} %w_ref) | copy-start | bytes 442372
  3.6 33.5 %all-to-all-start = ((bf16[32,128,128]{2,1,0:T(8,128)(2,1)}), bf16[32,128,128]{2,1,0:T(8,128)(2,1)S(1)}, u32[]{:S(2)}, u32[]{:S(2)}) async-start(bf16[32,128,128]{2,1,0:T(8,128)(2,1)} %shard_map.75), calls=%async_computation | async-start | bytes 2097152 | tf_op jit(solution)/shard_map/all_to_all | solution.py:292
  10.9 0.7 copy-start.1
  41.7 33.2 %all-to-all-start.1 = ((bf16[32,128,128]{2,1,0:T(8,128)(2,1)}), bf16[32,128,128]{2,1,0:T(8,128)(2,1)S(1)}, u32[]{:S(2)}, u32[]{:S(2)}) async-start(bf16[32,128,128]{2,1,0:T(8,128)(2,1)} %get-tuple-element.20), calls=%async_computation.1 | async-start | bytes 2097152 | tf_op jit(solution)/shard_map/all_to_all | solution.py:292
  46.1 1.3 %collective-permute-start = (bf16[304,128]{1,0:T(8,128)(2,1)S(1)}, bf16[304,128]{1,0:T(8,128)(2,1)S(1)}, u32[]{:S(2)}, u32[]{:S(2)}) collective-permute-start(bf16[304,128]{1,0:T(8,128)(2,1)S(1)} %get-tuple-element.25), channel_id=1, source_target_pairs={{0,1},{1,0},{2,3},{3,2},{4,5},{5,4},{6,7},{7,6},{8,9},{9,8},{10,11... | collective-permute-start | bytes 233480 | tf_op jit(solution)/shard_map/ppermute | solution.py:280
  47.5 9.1 %collective-permute-start.1 = (bf16[304,128]{1,0:T(8,128)(2,1)S(1)}, bf16[304,128]{1,0:T(8,128)(2,1)S(1)}, u32[]{:S(2)}, u32[]{:S(2)}) collective-permute-start(bf16[304,128]{1,0:T(8,128)(2,1)S(1)} %add_convert_fusion.4), channel_id=1, source_target_pairs={{0,2},{1,3},{2,0},{3,1},{4,6},{5,7},{6,4},{7,5},{8,10},{9,11},{10,... | collective-permute-start | bytes 233480 | tf_op jit(solution)/shard_map/ppermute | solution.py:280
  56.6 5.0 %collective-permute-start.2 = (bf16[304,128]{1,0:T(8,128)(2,1)S(1)}, bf16[304,128]{1,0:T(8,128)(2,1)S(1)}, u32[]{:S(2)}, u32[]{:S(2)}) collective-permute-start(bf16[304,128]{1,0:T(8,128)(2,1)S(1)} %add_convert_fusion.3), channel_id=1, source_target_pairs={{0,4},{1,5},{2,6},{3,7},{4,0},{5,1},{6,2},{7,3},{8,12},{9,13},{10,... | collective-permute-start | bytes 233480 | tf_op jit(solution)/shard_map/ppermute | solution.py:280
  61.6 5.5 %collective-permute-start.3 = (bf16[304,128]{1,0:T(8,128)(2,1)S(1)}, bf16[304,128]{1,0:T(8,128)(2,1)S(1)}, u32[]{:S(2)}, u32[]{:S(2)}) collective-permute-start(bf16[304,128]{1,0:T(8,128)(2,1)S(1)} %add_convert_fusion.2), channel_id=1, source_target_pairs={{0,8},{1,9},{2,10},{3,11},{4,12},{5,13},{6,14},{7,15},{8,0},{9,1},... | collective-permute-start | bytes 233480 | tf_op jit(solution)/shard_map/ppermute | solution.py:280
  67.1 7.8 %collective-permute-start.4 = (bf16[304,128]{1,0:T(8,128)(2,1)S(1)}, bf16[304,128]{1,0:T(8,128)(2,1)S(1)}, u32[]{:S(2)}, u32[]{:S(2)}) collective-permute-start(bf16[304,128]{1,0:T(8,128)(2,1)S(1)} %add_convert_fusion.1), channel_id=1, source_target_pairs={{0,16},{1,17},{2,18},{3,19},{4,20},{5,21},{6,22},{7,23},{8,24},{9,... | collective-permute-start | bytes 233480 | tf_op jit(solution)/shard_map/ppermute | solution.py:280
  74.9 1.7 %collective-permute-start.5 = (bf16[304,128]{1,0:T(8,128)(2,1)S(1)}, bf16[304,128]{1,0:T(8,128)(2,1)S(1)}, u32[]{:S(2)}, u32[]{:S(2)}) collective-permute-start(bf16[304,128]{1,0:T(8,128)(2,1)S(1)} %add_convert_fusion.mine_ref), channel_id=1, source_target_pairs={{0,1},{1,0},{2,3},{3,2},{4,5},{5,4},{6,7},{7,6},{8,9},{9,8},{10,11... | collective-permute-start | bytes 233480 | tf_op jit(solution)/shard_map/ppermute | solution.py:280

commit v5 on v4

--- a/solution.py
+++ b/solution.py
@@ -141,6 +141,16 @@
     return jnp.concatenate([after, here, before], axis=0)
 
 
+def interleaved(count, hops, produce, consume):
+    waiting = list(range(count))
+    for i in range(count):
+        produce(i)
+        for j in list(waiting):
+            if max((j - hops) % count, j, (j + hops) % count) <= i:
+                waiting.remove(j)
+                consume(j)
+
+
 def stack_kernel(
     share,
     parts_ref,
@@ -174,58 +184,64 @@
         )
         copies[-1].start()
 
+    def multiply(layer, i):
+        line = line_of(parts_ref, count, channels, 0, i) if layer == 0 else h_ref[i]
+        stack = jnp.concatenate(taps(line, 2**layer * share), axis=0)
+        y_ref[i] = product(w_ref[2 * layer], stack)
+
+    def activate(layer, i):
+        hops = 2**layer
+        pre = b_ref[layer] + y_ref[i, channels : 2 * channels]
+        pre = pre + y_ref[(i - hops) % count, :channels]
+        pre = pre + y_ref[(i + hops) % count, 2 * channels :]
+        sigma = 0.5 * jnp.tanh(0.5 * pre) + 0.5
+        state = pre * sigma
+        slope = sigma + state * (1.0 - sigma)
+        if layer == 0:
+            h_ref[i] = state.astype(BF16)
+            s0_ref[i] = slope
+        else:
+            s1_ref[i] = slope
+            put(0, i, state.astype(BF16))
+
+    def multiply_back(layer, i):
+        hops = 2**layer
+        if layer == 1:
+            gated = line_of(parts_ref, count, channels, 1, i).astype(F32) * s1_ref[i]
+            gated = gated.astype(BF16)
+        else:
+            gated = gz_ref[i]
+        stack = back_taps(gated, hops * share)
+        y_ref[i] = product(w_ref[2 * layer + 1], stack)
+        if layer == 1:
+            around = [h_ref[(i + (a - 1) * hops) % count] for a in range(3)]
+            term, bias_term = weight_product(gated, stack, around)
+            sums[0], sums[1] = sums[0] + term, sums[1] + bias_term
+
+    def pass_back(layer, i):
+        hops = 2**layer
+        g = y_ref[i, channels : 2 * channels]
+        g = g + y_ref[(i + hops) % count, :channels]
+        g = g + y_ref[(i - hops) % count, 2 * channels :]
+        g = g.astype(BF16)
+        if layer == 1:
+            gz_ref[i] = (g.astype(F32) * s0_ref[i]).astype(BF16)
+        else:
+            put(1, i, g)
+            send(1, i, 1)
+
+    sums = [0.0, 0.0]
     for layer in range(2):
-        hops = 2**layer
-        kernel = w_ref[2 * layer]
-        for i in range(count):
-            line = line_of(parts_ref, count, channels, 0, i) if layer == 0 else h_ref[i]
-            stack = jnp.concatenate(taps(line, hops * share), axis=0)
-            y_ref[i] = product(kernel, stack).astype(BF16)
-        bias = b_ref[layer]
-        for i in range(count):
-            pre = bias + y_ref[i, channels : 2 * channels].astype(F32)
-            pre = pre + y_ref[(i - hops) % count, :channels].astype(F32)
-            pre = pre + y_ref[(i + hops) % count, 2 * channels :].astype(F32)
-            sigma = 0.5 * jnp.tanh(0.5 * pre) + 0.5
-            state = pre * sigma
-            slope = sigma + state * (1.0 - sigma)
-            if layer == 0:
-                h_ref[i] = state.astype(BF16)
-                s0_ref[i] = slope
-            else:
-                s1_ref[i] = slope
-                put(0, i, state.astype(BF16))
+        interleaved(count, 2**layer, functools.partial(multiply, layer), functools.partial(activate, layer))
     send(0, 0, count)
-
-    total, bias = 0.0, 0.0
     for layer in (1, 0):
-        hops = 2**layer
-        kernel = w_ref[2 * layer + 1]
-        for i in range(count):
-            if layer == 1:
-                gated = line_of(parts_ref, count, channels, 1, i).astype(F32) * s1_ref[i]
-                gated = gated.astype(BF16)
-            else:
-                gated = gz_ref[i]
-            stack = back_taps(gated, hops * share)
-            y_ref[i] = product(kernel, stack).astype(BF16)
-            if layer == 1:
-                around = [h_ref[(i + (a - 1) * hops) % count] for a in range(3)]
-                term, bias_term = weight_product(gated, stack, around)
-                total, bias = total + term, bias + bias_term
-        for i in range(count):
-            g = y_ref[i, channels : 2 * channels].astype(F32)
-            g = g + y_ref[(i + hops) % count, :channels].astype(F32)
-            g = g + y_ref[(i - hops) % count, 2 * channels :].astype(F32)
-            g = g.astype(BF16)
-            if layer == 1:
-                gz_ref[i] = (g.astype(F32) * s0_ref[i]).astype(BF16)
-            else:
-                put(1, i, g)
-                send(1, i, 1)
-        if layer == 1:
-            total_ref[...] = total
-            bias_ref[...] = bias
+        interleaved(
+            count,
+            2**layer,
+            functools.partial(multiply_back, layer),
+            functools.partial(pass_back, layer),
+        )
+    total_ref[...], bias_ref[...] = sums
     for started in copies:
         started.wait()
 
@@ -347,7 +363,7 @@
             pltpu.VMEM(cells, BF16),
             pltpu.VMEM(cells, F32),
             pltpu.VMEM(cells, F32),
-            pltpu.VMEM((lons, 3 * channels, span), BF16),
+            pltpu.VMEM((lons, 3 * channels, span), F32),
             pltpu.VMEM(parts.shape, BF16),
             pltpu.SemaphoreType.DMA((lons + 1,)),
         ],

time: 78 us -> 78.4 us (level)
  no operation moved by 1% of the time
where the time goes in v5:
time: 78.4 us; the launch traced here: 78.1 us
  waiting for transfers between devices  46.2 us (59%)
  starting transfers between devices  18.6 us (24%)
  Pallas kernels  11.6 us (15%)
    all_to_all x2, waiting for transfers between devices, exchanged(): return lax.all_to_all(parts, AXES, 0, 0, tiled=True)  25.2 us
    ppermute x6, waiting for transfers between devices, partnered(): return lax.ppermute(block, AXES, [(i, i ^ bit) for i in range(devices)])  21 us
    all_to_all x2, starting transfers between devices, exchanged(): return lax.all_to_all(parts, AXES, 0, 0, tiled=True)  10.9 us
    ppermute x6, starting transfers between devices, partnered(): return lax.ppermute(block, AXES, [(i, i ^ bit) for i in range(devices)])  7.7 us
    pallas_call x1, Pallas kernels, local(): pl.pallas_call(functools.partial(stack_kernel, share), out_shape=[shape(p...  4.89 us
    pallas_call x1, Pallas kernels, local(): pl.pallas_call(functools.partial(pack_kernel, share), out_shape=shape(fie...  2.97 us
    pallas_call x1, Pallas kernels, local(): pl.pallas_call(functools.partial(unpack_kernel, share), out_shape=[shape(...  1.62 us
  transfers between devices with their start and end apart: 8, of which 6 were waited for; matrix products, arithmetic and copies ran while one was open for 0% of the time, Pallas kernels for 3%

profile of v5, /device:TPU:0, one launch (start us, length us, event | category | flops | bytes accessed | tf_op | source)
XLA Modules:
  0.0 78.1 jit_solution(1466588347030923139)
XLA Ops:
  0.6 3.0 %shard_map.75 = bf16[32,128,128]{2,1,0:T(8,128)(2,1)} custom-call(bf16[64,16,256]{2,1,0:T(8,128)(2,1)} %x_ref.1, bf16[64,16,256]{2,1,0:T(8,128)(2,1)} %cot_ref.1), custom_call_target="tpu_custom_call" | custom-call | tf_op jit(solution)/shard_map/pallas_call | solution.py:327
  3.6 0.0 copy-start
  3.6 7.3 %all-to-all-start = ((bf16[32,128,128]{2,1,0:T(8,128)(2,1)}), bf16[32,128,128]{2,1,0:T(8,128)(2,1)S(1)}, u32[]{:S(2)}, u32[]{:S(2)}) async-start(bf16[32,128,128]{2,1,0:T(8,128)(2,1)} %shard_map.75), calls=%async_computation | async-start | bytes 2097152 | tf_op jit(solution)/shard_map/all_to_all | solution.py:308
  10.9 0.0 copy-start.1
  10.9 0.7 copy-done.1
  11.6 0.1 copy.8.b_ref
  11.7 0.0 copy-done
  11.7 0.2 shard_map.76.w_ref
  12.0 25.2 %all-to-all-done.parts_ref = bf16[32,128,128]{2,1,0:T(8,128)(2,1)S(1)} async-done(((bf16[32,128,128]{2,1,0:T(8,128)(2,1)}), bf16[32,128,128]{2,1,0:T(8,128)(2,1)S(1)}, u32[]{:S(2)}, u32[]{:S(2)}) %all-to-all-start) | async-done | bytes 1048608 | tf_op jit(solution)/shard_map/all_to_all | solution.py:308
  37.2 4.9 %shard_map.77 = (bf16[32,128,128]{2,1,0:T(8,128)(2,1)}, bf16[8,64,512]{2,1,0:T(8,128)(2,1)S(1)}, f32[192,192]{1,0:T(8,128)S(1)}, f32[16,64]{1,0:T(8,128)S(1)}) custom-call(bf16[32,128,128]{2,1,0:T(8,128)(2,1)S(1)} %all-to-all-done.parts_ref, bf16[4,192,192]{2,1,0:T(8,128)(2,1)S(1)} %shard_map.76.w_ref, f32[2,64,1]{2,1,0:T(8,128)S(1)} %copy.8.b_ref), custom_call_target="tpu_custom_call" | custom-call | tf_op jit(solution)/shard_map/pallas_call | solution.py:353
  42.1 3.6 %all-to-all-start.1 = ((bf16[32,128,128]{2,1,0:T(8,128)(2,1)}), bf16[32,128,128]{2,1,0:T(8,128)(2,1)S(1)}, u32[]{:S(2)}, u32[]{:S(2)}) async-start(bf16[32,128,128]{2,1,0:T(8,128)(2,1)} %get-tuple-element.20), calls=%async_computation.1 | async-start | bytes 2097152 | tf_op jit(solution)/shard_map/all_to_all | solution.py:308
  45.7 0.8 %shard_map.78 = (f32[304,128]{1,0:T(8,128)S(1)}, bf16[304,128]{1,0:T(8,128)(2,1)S(1)}) custom-call(bf16[32,128,128]{2,1,0:T(8,128)(2,1)S(1)} %all-to-all-done.parts_ref, bf16[8,64,512]{2,1,0:T(8,128)(2,1)S(1)} %get-tuple-element.21.gz_ref, f32[192,192]{1,0:T(8,128)S(1)} %get-tuple-element.22.total_ref, f32[16,64]{1,0:T(8,128)S(1)} %get-tuple-element.23.bias_ref), custom_call_target="tpu_custom_call" | custom-call | flops 301989888 | bytes 1572864 | tf_op jit(solution)/shard_map/pallas_call | solution.py:380
  46.5 0.3 collective-permute-start
  46.8 1.0 %collective-permute-done = bf16[304,128]{1,0:T(8,128)(2,1)S(1)} collective-permute-done((bf16[304,128]{1,0:T(8,128)(2,1)S(1)}, bf16[304,128]{1,0:T(8,128)(2,1)S(1)}, u32[]{:S(2)}, u32[]{:S(2)}) %collective-permute-start) | collective-permute-done | bytes 77856 | tf_op jit(solution)/shard_map/ppermute | solution.py:296
  47.9 1.8 %collective-permute-start.1 = (bf16[304,128]{1,0:T(8,128)(2,1)S(1)}, bf16[304,128]{1,0:T(8,128)(2,1)S(1)}, u32[]{:S(2)}, u32[]{:S(2)}) collective-permute-start(bf16[304,128]{1,0:T(8,128)(2,1)S(1)} %add_convert_fusion.4), channel_id=1, source_target_pairs={{0,2},{1,3},{2,0},{3,1},{4,6},{5,7},{6,4},{7,5},{8,10},{9,11},{10,... | collective-permute-start | bytes 233480 | tf_op jit(solution)/shard_map/ppermute | solution.py:296
  49.7 7.2 %collective-permute-done.1 = bf16[304,128]{1,0:T(8,128)(2,1)S(1)} collective-permute-done((bf16[304,128]{1,0:T(8,128)(2,1)S(1)}, bf16[304,128]{1,0:T(8,128)(2,1)S(1)}, u32[]{:S(2)}, u32[]{:S(2)}) %collective-permute-start.1) | collective-permute-done | bytes 77856 | tf_op jit(solution)/shard_map/ppermute | solution.py:296
  57.0 2.0 %collective-permute-start.2 = (bf16[304,128]{1,0:T(8,128)(2,1)S(1)}, bf16[304,128]{1,0:T(8,128)(2,1)S(1)}, u32[]{:S(2)}, u32[]{:S(2)}) collective-permute-start(bf16[304,128]{1,0:T(8,128)(2,1)S(1)} %add_convert_fusion.3), channel_id=1, source_target_pairs={{0,4},{1,5},{2,6},{3,7},{4,0},{5,1},{6,2},{7,3},{8,12},{9,13},{10,... | collective-permute-start | bytes 233480 | tf_op jit(solution)/shard_map/ppermute | solution.py:296
  59.0 3.0 %collective-permute-done.2 = bf16[304,128]{1,0:T(8,128)(2,1)S(1)} collective-permute-done((bf16[304,128]{1,0:T(8,128)(2,1)S(1)}, bf16[304,128]{1,0:T(8,128)(2,1)S(1)}, u32[]{:S(2)}, u32[]{:S(2)}) %collective-permute-start.2) | collective-permute-done | bytes 77856 | tf_op jit(solution)/shard_map/ppermute | solution.py:296
  62.0 1.4 %collective-permute-start.3 = (bf16[304,128]{1,0:T(8,128)(2,1)S(1)}, bf16[304,128]{1,0:T(8,128)(2,1)S(1)}, u32[]{:S(2)}, u32[]{:S(2)}) collective-permute-start(bf16[304,128]{1,0:T(8,128)(2,1)S(1)} %add_convert_fusion.2), channel_id=1, source_target_pairs={{0,8},{1,9},{2,10},{3,11},{4,12},{5,13},{6,14},{7,15},{8,0},{9,1},... | collective-permute-start | bytes 233480 | tf_op jit(solution)/shard_map/ppermute | solution.py:296
  63.3 4.1 %collective-permute-done.3 = bf16[304,128]{1,0:T(8,128)(2,1)S(1)} collective-permute-done((bf16[304,128]{1,0:T(8,128)(2,1)S(1)}, bf16[304,128]{1,0:T(8,128)(2,1)S(1)}, u32[]{:S(2)}, u32[]{:S(2)}) %collective-permute-start.3) | collective-permute-done | bytes 77856 | tf_op jit(solution)/shard_map/ppermute | solution.py:296
  67.5 2.1 %collective-permute-start.4 = (bf16[304,128]{1,0:T(8,128)(2,1)S(1)}, bf16[304,128]{1,0:T(8,128)(2,1)S(1)}, u32[]{:S(2)}, u32[]{:S(2)}) collective-permute-start(bf16[304,128]{1,0:T(8,128)(2,1)S(1)} %add_convert_fusion.1), channel_id=1, source_target_pairs={{0,16},{1,17},{2,18},{3,19},{4,20},{5,21},{6,22},{7,23},{8,24},{9,... | collective-permute-start | bytes 233480 | tf_op jit(solution)/shard_map/ppermute | solution.py:296
  69.6 5.7 %collective-permute-done.4 = bf16[304,128]{1,0:T(8,128)(2,1)S(1)} collective-permute-done((bf16[304,128]{1,0:T(8,128)(2,1)S(1)}, bf16[304,128]{1,0:T(8,128)(2,1)S(1)}, u32[]{:S(2)}, u32[]{:S(2)}) %collective-permute-start.4) | collective-permute-done | bytes 77856 | tf_op jit(solution)/shard_map/ppermute | solution.py:296
  75.3 0.0 all-to-all-done.1.parts_ref
  75.3 0.1 collective-permute-start.5
  75.4 1.6 %shard_map.79 = (bf16[64,16,256]{2,1,0:T(8,128)(2,1)}, bf16[64,16,256]{2,1,0:T(8,128)(2,1)}) custom-call(bf16[32,128,128]{2,1,0:T(8,128)(2,1)S(1)} %all-to-all-done.1.parts_ref), custom_call_target="tpu_custom_call" | custom-call | flops 268435456 | bytes 2097152 | tf_op jit(solution)/shard_map/pallas_call | solution.py:390
  77.0 0.0 collective-permute-done.5.other_ref
  77.0 1.0 %shard_map.80 = (f32[2,3,3,64,64]{4,3,2,1,0:T(8,128)}, f32[2,64]{1,0:T(2,128)}) custom-call(bf16[304,128]{1,0:T(8,128)(2,1)S(1)} %add_convert_fusion.mine_ref, bf16[304,128]{1,0:T(8,128)(2,1)S(1)} %collective-permute-done.5.other_ref), custom_call_target="tpu_custom_call" | custom-call | tf_op jit(solution)/shard_map/pallas_call | solution.py:403
  (5 shorter events, 0.1 us)
Async XLA Ops:
  3.6 8.1 %copy-start = (bf16[2,3,3,64,64]{4,3,2,1,0:T(8,128)(2,1)S(1)}, bf16[2,3,3,64,64]{4,3,2,1,0:T(8,128)(2,1)}, u32[]{:S(2)}) copy-start(bf16[2,3,3,64,64]{4,3,2,1,0:T(8,128)(2,1)} %w_ref) | copy-start | bytes 442372
  3.6 33.5 %all-to-all-start = ((bf16[32,128,128]{2,1,0:T(8,128)(2,1)}), bf16[32,128,128]{2,1,0:T(8,128)(2,1)S(1)}, u32[]{:S(2)}, u32[]{:S(2)}) async-start(bf16[32,128,128]{2,1,0:T(8,128)(2,1)} %shard_map.75), calls=%async_computation | async-start | bytes 2097152 | tf_op jit(solution)/shard_map/all_to_all | solution.py:308
  10.9 0.7 copy-start.1
  42.1 33.2 %all-to-all-start.1 = ((bf16[32,128,128]{2,1,0:T(8,128)(2,1)}), bf16[32,128,128]{2,1,0:T(8,128)(2,1)S(1)}, u32[]{:S(2)}, u32[]{:S(2)}) async-start(bf16[32,128,128]{2,1,0:T(8,128)(2,1)} %get-tuple-element.20), calls=%async_computation.1 | async-start | bytes 2097152 | tf_op jit(solution)/shard_map/all_to_all | solution.py:308
  46.5 1.3 %collective-permute-start = (bf16[304,128]{1,0:T(8,128)(2,1)S(1)}, bf16[304,128]{1,0:T(8,128)(2,1)S(1)}, u32[]{:S(2)}, u32[]{:S(2)}) collective-permute-start(bf16[304,128]{1,0:T(8,128)(2,1)S(1)} %get-tuple-element.25), channel_id=1, source_target_pairs={{0,1},{1,0},{2,3},{3,2},{4,5},{5,4},{6,7},{7,6},{8,9},{9,8},{10,11... | collective-permute-start | bytes 233480 | tf_op jit(solution)/shard_map/ppermute | solution.py:296
  47.9 9.1 %collective-permute-start.1 = (bf16[304,128]{1,0:T(8,128)(2,1)S(1)}, bf16[304,128]{1,0:T(8,128)(2,1)S(1)}, u32[]{:S(2)}, u32[]{:S(2)}) collective-permute-start(bf16[304,128]{1,0:T(8,128)(2,1)S(1)} %add_convert_fusion.4), channel_id=1, source_target_pairs={{0,2},{1,3},{2,0},{3,1},{4,6},{5,7},{6,4},{7,5},{8,10},{9,11},{10,... | collective-permute-start | bytes 233480 | tf_op jit(solution)/shard_map/ppermute | solution.py:296
  57.0 5.0 %collective-permute-start.2 = (bf16[304,128]{1,0:T(8,128)(2,1)S(1)}, bf16[304,128]{1,0:T(8,128)(2,1)S(1)}, u32[]{:S(2)}, u32[]{:S(2)}) collective-permute-start(bf16[304,128]{1,0:T(8,128)(2,1)S(1)} %add_convert_fusion.3), channel_id=1, source_target_pairs={{0,4},{1,5},{2,6},{3,7},{4,0},{5,1},{6,2},{7,3},{8,12},{9,13},{10,... | collective-permute-start | bytes 233480 | tf_op jit(solution)/shard_map/ppermute | solution.py:296
  62.0 5.5 %collective-permute-start.3 = (bf16[304,128]{1,0:T(8,128)(2,1)S(1)}, bf16[304,128]{1,0:T(8,128)(2,1)S(1)}, u32[]{:S(2)}, u32[]{:S(2)}) collective-permute-start(bf16[304,128]{1,0:T(8,128)(2,1)S(1)} %add_convert_fusion.2), channel_id=1, source_target_pairs={{0,8},{1,9},{2,10},{3,11},{4,12},{5,13},{6,14},{7,15},{8,0},{9,1},... | collective-permute-start | bytes 233480 | tf_op jit(solution)/shard_map/ppermute | solution.py:296
  67.5 7.8 %collective-permute-start.4 = (bf16[304,128]{1,0:T(8,128)(2,1)S(1)}, bf16[304,128]{1,0:T(8,128)(2,1)S(1)}, u32[]{:S(2)}, u32[]{:S(2)}) collective-permute-start(bf16[304,128]{1,0:T(8,128)(2,1)S(1)} %add_convert_fusion.1), channel_id=1, source_target_pairs={{0,16},{1,17},{2,18},{3,19},{4,20},{5,21},{6,22},{7,23},{8,24},{9,... | collective-permute-start | bytes 233480 | tf_op jit(solution)/shard_map/ppermute | solution.py:296
  75.3 1.7 %collective-permute-start.5 = (bf16[304,128]{1,0:T(8,128)(2,1)S(1)}, bf16[304,128]{1,0:T(8,128)(2,1)S(1)}, u32[]{:S(2)}, u32[]{:S(2)}) collective-permute-start(bf16[304,128]{1,0:T(8,128)(2,1)S(1)} %add_convert_fusion.mine_ref), channel_id=1, source_target_pairs={{0,1},{1,0},{2,3},{3,2},{4,5},{5,4},{6,7},{7,6},{8,9},{9,8},{10,11... | collective-permute-start | bytes 233480 | tf_op jit(solution)/shard_map/ppermute | solution.py:296

commit v6 on v2

--- a/solution.py
+++ b/solution.py
@@ -141,15 +141,29 @@
     return jnp.concatenate([after, here, before], axis=0)
 
 
+def forward_layer(layer, share, lines, w_ref, b_ref, y_ref, give):
+    count, channels = y_ref.shape[0], y_ref.shape[1] // 3
+    hops = 2**layer
+    kernel = w_ref[2 * layer]
+    for i in range(count):
+        stack = jnp.concatenate(taps(lines(i), hops * share), axis=0)
+        y_ref[i] = product(kernel, stack)
+    bias = b_ref[layer]
+    for i in range(count):
+        pre = bias + y_ref[i, channels : 2 * channels]
+        pre = pre + y_ref[(i - hops) % count, :channels]
+        pre = pre + y_ref[(i + hops) % count, 2 * channels :]
+        give(i, pre, 0.5 * jnp.tanh(0.5 * pre) + 0.5)
+
+
 def stack_kernel(
     share,
     parts_ref,
     w_ref,
     b_ref,
     out_ref,
-    gz_ref,
-    total_ref,
-    bias_ref,
+    gz0_ref,
+    gz1_ref,
     h_ref,
     s0_ref,
     s1_ref,
@@ -174,30 +188,23 @@
         )
         copies[-1].start()
 
-    for layer in range(2):
-        hops = 2**layer
-        kernel = w_ref[2 * layer]
-        for i in range(count):
-            line = line_of(parts_ref, count, channels, 0, i) if layer == 0 else h_ref[i]
-            stack = jnp.concatenate(taps(line, hops * share), axis=0)
-            y_ref[i] = product(kernel, stack)
-        bias = b_ref[layer]
-        for i in range(count):
-            pre = bias + y_ref[i, channels : 2 * channels]
-            pre = pre + y_ref[(i - hops) % count, :channels]
-            pre = pre + y_ref[(i + hops) % count, 2 * channels :]
-            sigma = 0.5 * jnp.tanh(0.5 * pre) + 0.5
-            state = pre * sigma
-            slope = sigma + state * (1.0 - sigma)
-            if layer == 0:
-                h_ref[i] = state.astype(BF16)
-                s0_ref[i] = slope
-            else:
-                s1_ref[i] = slope
-                put(0, i, state.astype(BF16))
+    def give_hidden(i, pre, sigma):
+        state = pre * sigma
+        h_ref[i] = state.astype(BF16)
+        s0_ref[i] = sigma + state * (1.0 - sigma)
+
+    def give_features(i, pre, sigma):
+        state = pre * sigma
+        s1_ref[i] = sigma + state * (1.0 - sigma)
+        put(0, i, state.astype(BF16))
+
+    def line(i):
+        return line_of(parts_ref, count, channels, 0, i)
+
+    forward_layer(0, share, line, w_ref, b_ref, y_ref, give_hidden)
+    forward_layer(1, share, lambda i: h_ref[i], w_ref, b_ref, y_ref, give_features)
     send(0, 0, count)
 
-    total, bias = 0.0, 0.0
     for layer in (1, 0):
         hops = 2**layer
         kernel = w_ref[2 * layer + 1]
@@ -205,48 +212,52 @@
             if layer == 1:
                 gated = line_of(parts_ref, count, channels, 1, i).astype(F32) * s1_ref[i]
                 gated = gated.astype(BF16)
+                gz1_ref[i] = gated
             else:
-                gated = gz_ref[i]
-            stack = back_taps(gated, hops * share)
-            y_ref[i] = product(kernel, stack)
-            if layer == 1:
-                around = [h_ref[(i + (a - 1) * hops) % count] for a in range(3)]
-                term, bias_term = weight_product(gated, stack, around)
-                total, bias = total + term, bias + bias_term
+                gated = gz0_ref[i]
+            y_ref[i] = product(kernel, back_taps(gated, hops * share))
         for i in range(count):
             g = y_ref[i, channels : 2 * channels]
             g = g + y_ref[(i + hops) % count, :channels]
             g = g + y_ref[(i - hops) % count, 2 * channels :]
             g = g.astype(BF16)
             if layer == 1:
-                gz_ref[i] = (g.astype(F32) * s0_ref[i]).astype(BF16)
+                gz0_ref[i] = (g.astype(F32) * s0_ref[i]).astype(BF16)
             else:
                 put(1, i, g)
                 send(1, i, 1)
-        if layer == 1:
-            total_ref[...] = total
-            bias_ref[...] = bias
     for started in copies:
         started.wait()
 
 
-def sums_kernel(share, parts_ref, gz_ref, total_ref, bias_ref, keep_ref, send_ref, rows_ref):
-    count, channels, _ = gz_ref.shape
+def sums_kernel(
+    share, parts_ref, w_ref, b_ref, gz0_ref, gz1_ref, keep_ref, send_ref, rows_ref, h_ref, y_ref
+):
+    count, channels, _ = gz0_ref.shape
     high = 3 * channels
-    total, bias = 0.0, 0.0
-    for i in range(count):
-        gated = gz_ref[i]
-        around = [
-            line_of(parts_ref, count, channels, 0, (i + a - 1) % count) for a in range(3)
-        ]
-        term, bias_term = weight_product(gated, back_taps(gated, share), around)
-        total, bias = total + term, bias + bias_term
-    for layer, sums in enumerate((total, total_ref[...])):
-        rows_ref[layer * high : (layer + 1) * high, :] = sums[:, : 2 * channels]
-        rows_ref[2 * high : 3 * high, layer * channels : (layer + 1) * channels] = sums[
+
+    def line(i):
+        return line_of(parts_ref, count, channels, 0, i)
+
+    def give_hidden(i, pre, sigma):
+        h_ref[i] = (pre * sigma).astype(BF16)
+
+    forward_layer(0, share, line, w_ref, b_ref, y_ref, give_hidden)
+    biases = []
+    for layer, gz_ref, lines in ((0, gz0_ref, line), (1, gz1_ref, lambda i: h_ref[i])):
+        hops = 2**layer
+        total, bias = 0.0, 0.0
+        for i in range(count):
+            gated = gz_ref[i]
+            around = [lines((i + (a - 1) * hops) % count) for a in range(3)]
+            term, bias_term = weight_product(gated, back_taps(gated, hops * share), around)
+            total, bias = total + term, bias + bias_term
+        rows_ref[layer * high : (layer + 1) * high, :] = total[:, : 2 * channels]
+        rows_ref[2 * high : 3 * high, layer * channels : (layer + 1) * channels] = total[
             :, 2 * channels :
         ]
-    bias = jnp.concatenate([bias[:1], bias_ref[:1]], axis=1)
+        biases.append(bias[:1])
+    bias = jnp.concatenate(biases, axis=1)
     row = lax.broadcasted_iota(jnp.int32, (TAIL, 2 * channels), 0)
     rows_ref[3 * high :, :] = jnp.where(row == 0, bias, 0.0)
     half = keep_ref.shape[0]
@@ -282,8 +293,7 @@
 
 def added(keep, send, devices):
     total = keep + partnered(send, devices, 1).astype(F32)
-    bits = [4 << k for k in range((devices // 4).bit_length() - 1)] + [2]
-    for bit in bits:
+    for bit in [2 << k for k in range((devices // 2).bit_length() - 1)]:
         rounded = total.astype(BF16)
         total = rounded.astype(F32) + partnered(rounded, devices, bit).astype(F32)
     return total.astype(BF16)
@@ -334,16 +344,11 @@
         parts = parts.reshape(lons, 2 * channels, span)
 
     cells = (lons, channels, span)
-    high = 3 * channels
-    fields, gated, total, bias_sums = pl.pallas_call(
+    column = biases[:, :, None]
+    fields, gated0, gated1 = pl.pallas_call(
         functools.partial(stack_kernel, share),
-        out_shape=[
-            shape(parts.shape, BF16),
-            shape(cells, BF16),
-            shape((high, high), F32),
-            shape((16, channels), F32),
-        ],
-        out_specs=[hbm, vmem, vmem, vmem],
+        out_shape=[shape(parts.shape, BF16), shape(cells, BF16), shape(cells, BF16)],
+        out_specs=[hbm, vmem, vmem],
         scratch_shapes=[
             pltpu.VMEM(cells, BF16),
             pltpu.VMEM(cells, F32),
@@ -353,7 +358,7 @@
             pltpu.SemaphoreType.DMA((lons + 1,)),
         ],
         compiler_params=PARAMS,
-    )(parts, kernels, biases[:, :, None])
+    )(parts, kernels, column)
     if blocks == 1:
         fields = fields.reshape(lons, 2 * channels, lats, width).transpose(0, 2, 1, 3)
         fields = fields.reshape(fields_shape)
@@ -365,10 +370,14 @@
     keep, send = pl.pallas_call(
         functools.partial(sums_kernel, share),
         out_shape=[shape(half_shape, F32), shape(half_shape, BF16)],
-        scratch_shapes=[pltpu.VMEM((rows, 2 * channels), F32)],
+        scratch_shapes=[
+            pltpu.VMEM((rows, 2 * channels), F32),
+            pltpu.VMEM(cells, BF16),
+            pltpu.VMEM((lons, 3 * channels, span), F32),
+        ],
         compiler_params=PARAMS,
         cost_estimate=pl.CostEstimate(flops=flops, bytes_accessed=3 * parts.size, transcendentals=0),
-    )(parts, gated, total, bias_sums)
+    )(parts, kernels, column, gated0, gated1)
     mine = added(keep, send, devices)
     home, mine = lax.optimization_barrier((home, mine))
     other = partnered(mine, devices, 1)

time: 82.7 us -> 77.8 us (0.941); the launches traced: 82.4 us -> 76.6 us
  waiting for transfers between devices: 49.4 us -> 42.3 us
  local copies, waits for them, and re-layouts: 0.78 us -> 2.61 us
  starting transfers between devices: 19.9 us -> 18.9 us
    ppermute x6, waiting for transfers between devices: 24.2 us -> 17.2 us  [partnered(): return lax.ppermute(block, AXES, [(i, i ^ bit) for i in range(devices)])]
    unnamed x4 -> x8, local copies, waits for them, and re-layouts: 0.68 us -> 2.51 us
    pallas_call x1, Pallas kernels: 0.8 us -> 2.5 us  [local(): pl.pallas_call(functools.partial(sums_kernel, share), out_shape=[shape(ha...]
    pallas_call x1, Pallas kernels: 4.72 us -> 3.53 us  [local(): pl.pallas_call(functools.partial(stack_kernel, share), out_shape=[shape(p...]
    ppermute x6, starting transfers between devices: 9.02 us -> 7.99 us  [partnered(): return lax.ppermute(block, AXES, [(i, i ^ bit) for i in range(devices)])]
  transfers between devices with their start and end apart: 8 -> 8, of which waited for: 6 -> 6; matrix products, arithmetic and copies ran while one was open for 0% -> 0% of each run, Pallas kernels for 3% -> 6%
where the time goes in v6:
time: 77.8 us; the launch traced here: 76.6 us
  waiting for transfers between devices  42.3 us (54%)
  starting transfers between devices  18.9 us (24%)
  Pallas kernels  11.9 us (15%)
  local copies, waits for them, and re-layouts  2.61 us (3%)
  between operations  0.78 us (1%)
    all_to_all x2, waiting for transfers between devices, exchanged(): return lax.all_to_all(parts, AXES, 0, 0, tiled=True)  25.2 us
    ppermute x6, waiting for transfers between devices, partnered(): return lax.ppermute(block, AXES, [(i, i ^ bit) for i in range(devices)])  17.2 us
    all_to_all x2, starting transfers between devices, exchanged(): return lax.all_to_all(parts, AXES, 0, 0, tiled=True)  10.9 us
    ppermute x6, starting transfers between devices, partnered(): return lax.ppermute(block, AXES, [(i, i ^ bit) for i in range(devices)])  7.99 us
    pallas_call x1, Pallas kernels, local(): pl.pallas_call(functools.partial(stack_kernel, share), out_shape=[shape(p...  3.53 us
    pallas_call x1, Pallas kernels, local(): pl.pallas_call(functools.partial(pack_kernel, share), out_shape=shape(fie...  2.96 us
    unnamed x8, local copies, waits for them, and re-layouts  2.51 us
    pallas_call x1, Pallas kernels, local(): pl.pallas_call(functools.partial(sums_kernel, share), out_shape=[shape(ha...  2.5 us
  transfers between devices with their start and end apart: 8, of which 6 were waited for; matrix products, arithmetic and copies ran while one was open for 0% of the time, Pallas kernels for 6%

profile of v6, /device:TPU:0, one launch (start us, length us, event | category | flops | bytes accessed | tf_op | source)
XLA Modules:
  0.0 76.6 jit_solution(10870574648998677283)
XLA Ops:
  0.6 3.0 %shard_map.75 = bf16[32,128,128]{2,1,0:T(8,128)(2,1)} custom-call(bf16[64,16,256]{2,1,0:T(8,128)(2,1)} %x_ref.1, bf16[64,16,256]{2,1,0:T(8,128)(2,1)} %cot_ref.1), custom_call_target="tpu_custom_call" | custom-call | tf_op jit(solution)/shard_map/pallas_call | solution.py:322
  3.6 0.0 copy-start.2
  3.6 7.3 %all-to-all-start = ((bf16[32,128,128]{2,1,0:T(8,128)(2,1)}), bf16[32,128,128]{2,1,0:T(8,128)(2,1)S(1)}, u32[]{:S(2)}, u32[]{:S(2)}) async-start(bf16[32,128,128]{2,1,0:T(8,128)(2,1)} %shard_map.75), calls=%async_computation | async-start | bytes 2097152 | tf_op jit(solution)/shard_map/all_to_all | solution.py:303
  10.9 0.0 copy-start.3
  10.9 0.7 copy-done.3
  11.6 0.1 copy.8.b_ref
  11.7 0.0 copy-done.2
  11.7 0.2 shard_map.76.w_ref
  12.0 25.2 %all-to-all-done.parts_ref = bf16[32,128,128]{2,1,0:T(8,128)(2,1)S(1)} async-done(((bf16[32,128,128]{2,1,0:T(8,128)(2,1)}), bf16[32,128,128]{2,1,0:T(8,128)(2,1)S(1)}, u32[]{:S(2)}, u32[]{:S(2)}) %all-to-all-start) | async-done | bytes 1048608 | tf_op jit(solution)/shard_map/all_to_all | solution.py:303
  37.2 3.5 %shard_map.77 = (bf16[32,128,128]{2,1,0:T(8,128)(2,1)}, bf16[8,64,512]{2,1,0:T(8,128)(2,1)S(1)}, bf16[8,64,512]{2,1,0:T(8,128)(2,1)S(1)}) custom-call(bf16[32,128,128]{2,1,0:T(8,128)(2,1)S(1)} %all-to-all-done.parts_ref, bf16[4,192,192]{2,1,0:T(8,128)(2,1)S(1)} %shard_map.76.w_ref, f32[2,64,1]{2,1,0:T(8,128)S(1)} %copy.8.b_ref), custom_call_target="tpu_custom_call" | custom-call | tf_op jit(solution)/shard_map/pallas_call | solution.py:348
  40.7 0.0 copy-start
  40.7 0.8 %copy-done = bf16[8,64,512]{2,1,0:T(8,128)(2,1)} copy-done((bf16[8,64,512]{2,1,0:T(8,128)(2,1)}, bf16[8,64,512]{2,1,0:T(8,128)(2,1)S(1)}, u32[]{:S(2)}) %copy-start) | copy-done | bytes 524312
  41.5 3.6 %all-to-all-start.1 = ((bf16[32,128,128]{2,1,0:T(8,128)(2,1)}), bf16[32,128,128]{2,1,0:T(8,128)(2,1)S(1)}, u32[]{:S(2)}, u32[]{:S(2)}) async-start(bf16[32,128,128]{2,1,0:T(8,128)(2,1)} %get-tuple-element.19), calls=%async_computation.1 | async-start | bytes 2097152 | tf_op jit(solution)/shard_map/all_to_all | solution.py:303
  45.1 0.0 copy-start.1
  45.1 1.0 %copy-done.1 = bf16[8,64,512]{2,1,0:T(8,128)(2,1)S(1)} copy-done((bf16[8,64,512]{2,1,0:T(8,128)(2,1)S(1)}, bf16[8,64,512]{2,1,0:T(8,128)(2,1)}, u32[]{:S(2)}) %copy-start.1) | copy-done | bytes 524312
  46.2 2.5 %shard_map.78 = (f32[304,128]{1,0:T(8,128)S(1)}, bf16[304,128]{1,0:T(8,128)(2,1)S(1)}) custom-call(bf16[32,128,128]{2,1,0:T(8,128)(2,1)S(1)} %all-to-all-done.parts_ref, bf16[4,192,192]{2,1,0:T(8,128)(2,1)S(1)} %shard_map.76.w_ref, f32[2,64,1]{2,1,0:T(8,128)S(1)} %copy.8.b_ref, bf16[8,64,512]{2,1,0:T(8,128)(2,1)S(1)} %get-tuple-element.20.gz0_ref, ...), custom_call_target="tpu_custom_call" | custom-call | flops 301989888 | bytes 1572864 | tf_op jit(solution)/shard_map/pallas_call | solution.py:370
  48.7 0.3 collective-permute-start
  49.0 1.0 %collective-permute-done = bf16[304,128]{1,0:T(8,128)(2,1)S(1)} collective-permute-done((bf16[304,128]{1,0:T(8,128)(2,1)S(1)}, bf16[304,128]{1,0:T(8,128)(2,1)S(1)}, u32[]{:S(2)}, u32[]{:S(2)}) %collective-permute-start) | collective-permute-done | bytes 77856 | tf_op jit(solution)/shard_map/ppermute | solution.py:291
  50.0 1.8 %collective-permute-start.1 = (bf16[304,128]{1,0:T(8,128)(2,1)S(1)}, bf16[304,128]{1,0:T(8,128)(2,1)S(1)}, u32[]{:S(2)}, u32[]{:S(2)}) collective-permute-start(bf16[304,128]{1,0:T(8,128)(2,1)S(1)} %add_convert_fusion.4), channel_id=1, source_target_pairs={{0,2},{1,3},{2,0},{3,1},{4,6},{5,7},{6,4},{7,5},{8,10},{9,11},{10,... | collective-permute-start | bytes 233480 | tf_op jit(solution)/shard_map/ppermute | solution.py:291
  51.9 5.5 %collective-permute-done.1 = bf16[304,128]{1,0:T(8,128)(2,1)S(1)} collective-permute-done((bf16[304,128]{1,0:T(8,128)(2,1)S(1)}, bf16[304,128]{1,0:T(8,128)(2,1)S(1)}, u32[]{:S(2)}, u32[]{:S(2)}) %collective-permute-start.1) | collective-permute-done | bytes 77856 | tf_op jit(solution)/shard_map/ppermute | solution.py:291
  57.4 2.6 %collective-permute-start.2 = (bf16[304,128]{1,0:T(8,128)(2,1)S(1)}, bf16[304,128]{1,0:T(8,128)(2,1)S(1)}, u32[]{:S(2)}, u32[]{:S(2)}) collective-permute-start(bf16[304,128]{1,0:T(8,128)(2,1)S(1)} %add_convert_fusion.3), channel_id=1, source_target_pairs={{0,4},{1,5},{2,6},{3,7},{4,0},{5,1},{6,2},{7,3},{8,12},{9,13},{10,... | collective-permute-start | bytes 233480 | tf_op jit(solution)/shard_map/ppermute | solution.py:291
  60.0 3.3 %collective-permute-done.2 = bf16[304,128]{1,0:T(8,128)(2,1)S(1)} collective-permute-done((bf16[304,128]{1,0:T(8,128)(2,1)S(1)}, bf16[304,128]{1,0:T(8,128)(2,1)S(1)}, u32[]{:S(2)}, u32[]{:S(2)}) %collective-permute-start.2) | collective-permute-done | bytes 77856 | tf_op jit(solution)/shard_map/ppermute | solution.py:291
  63.3 0.1 collective-permute-start.3
  63.4 4.6 %collective-permute-done.3 = bf16[304,128]{1,0:T(8,128)(2,1)S(1)} collective-permute-done((bf16[304,128]{1,0:T(8,128)(2,1)S(1)}, bf16[304,128]{1,0:T(8,128)(2,1)S(1)}, u32[]{:S(2)}, u32[]{:S(2)}) %collective-permute-start.3) | collective-permute-done | bytes 77856 | tf_op jit(solution)/shard_map/ppermute | solution.py:291
  68.0 3.1 %collective-permute-start.4 = (bf16[304,128]{1,0:T(8,128)(2,1)S(1)}, bf16[304,128]{1,0:T(8,128)(2,1)S(1)}, u32[]{:S(2)}, u32[]{:S(2)}) collective-permute-start(bf16[304,128]{1,0:T(8,128)(2,1)S(1)} %add_convert_fusion.1), channel_id=1, source_target_pairs={{0,16},{1,17},{2,18},{3,19},{4,20},{5,21},{6,22},{7,23},{8,24},{9,... | collective-permute-start | bytes 233480 | tf_op jit(solution)/shard_map/ppermute | solution.py:291
  71.1 2.7 %collective-permute-done.4 = bf16[304,128]{1,0:T(8,128)(2,1)S(1)} collective-permute-done((bf16[304,128]{1,0:T(8,128)(2,1)S(1)}, bf16[304,128]{1,0:T(8,128)(2,1)S(1)}, u32[]{:S(2)}, u32[]{:S(2)}) %collective-permute-start.4) | collective-permute-done | bytes 77856 | tf_op jit(solution)/shard_map/ppermute | solution.py:291
  73.9 0.0 all-to-all-done.1.parts_ref
  73.9 0.1 collective-permute-start.5
  74.0 1.6 %shard_map.79 = (bf16[64,16,256]{2,1,0:T(8,128)(2,1)}, bf16[64,16,256]{2,1,0:T(8,128)(2,1)}) custom-call(bf16[32,128,128]{2,1,0:T(8,128)(2,1)S(1)} %all-to-all-done.1.parts_ref), custom_call_target="tpu_custom_call" | custom-call | flops 268435456 | bytes 2097152 | tf_op jit(solution)/shard_map/pallas_call | solution.py:384
  75.6 0.0 collective-permute-done.5.other_ref
  75.6 1.0 %shard_map.80 = (f32[2,3,3,64,64]{4,3,2,1,0:T(8,128)}, f32[2,64]{1,0:T(2,128)}) custom-call(bf16[304,128]{1,0:T(8,128)(2,1)S(1)} %add_convert_fusion.mine_ref, bf16[304,128]{1,0:T(8,128)(2,1)S(1)} %collective-permute-done.5.other_ref), custom_call_target="tpu_custom_call" | custom-call | tf_op jit(solution)/shard_map/pallas_call | solution.py:397
  (5 shorter events, 0.1 us)
Async XLA Ops:
  3.6 8.1 %copy-start.2 = (bf16[2,3,3,64,64]{4,3,2,1,0:T(8,128)(2,1)S(1)}, bf16[2,3,3,64,64]{4,3,2,1,0:T(8,128)(2,1)}, u32[]{:S(2)}) copy-start(bf16[2,3,3,64,64]{4,3,2,1,0:T(8,128)(2,1)} %w_ref) | copy-start | bytes 442372
  3.6 33.5 %all-to-all-start = ((bf16[32,128,128]{2,1,0:T(8,128)(2,1)}), bf16[32,128,128]{2,1,0:T(8,128)(2,1)S(1)}, u32[]{:S(2)}, u32[]{:S(2)}) async-start(bf16[32,128,128]{2,1,0:T(8,128)(2,1)} %shard_map.75), calls=%async_computation | async-start | bytes 2097152 | tf_op jit(solution)/shard_map/all_to_all | solution.py:303
  10.9 0.7 copy-start.3
  40.7 0.8 %copy-start = (bf16[8,64,512]{2,1,0:T(8,128)(2,1)}, bf16[8,64,512]{2,1,0:T(8,128)(2,1)S(1)}, u32[]{:S(2)}) copy-start(bf16[8,64,512]{2,1,0:T(8,128)(2,1)S(1)} %get-tuple-element.21.gz1_ref) | copy-start | bytes 1572868
  41.5 32.4 %all-to-all-start.1 = ((bf16[32,128,128]{2,1,0:T(8,128)(2,1)}), bf16[32,128,128]{2,1,0:T(8,128)(2,1)S(1)}, u32[]{:S(2)}, u32[]{:S(2)}) async-start(bf16[32,128,128]{2,1,0:T(8,128)(2,1)} %get-tuple-element.19), calls=%async_computation.1 | async-start | bytes 2097152 | tf_op jit(solution)/shard_map/all_to_all | solution.py:303
  45.1 1.0 %copy-start.1 = (bf16[8,64,512]{2,1,0:T(8,128)(2,1)S(1)}, bf16[8,64,512]{2,1,0:T(8,128)(2,1)}, u32[]{:S(2)}) copy-start(bf16[8,64,512]{2,1,0:T(8,128)(2,1)} %copy-done) | copy-start | bytes 1572868
  48.7 1.3 %collective-permute-start = (bf16[304,128]{1,0:T(8,128)(2,1)S(1)}, bf16[304,128]{1,0:T(8,128)(2,1)S(1)}, u32[]{:S(2)}, u32[]{:S(2)}) collective-permute-start(bf16[304,128]{1,0:T(8,128)(2,1)S(1)} %get-tuple-element.23), channel_id=1, source_target_pairs={{0,1},{1,0},{2,3},{3,2},{4,5},{5,4},{6,7},{7,6},{8,9},{9,8},{10,11... | collective-permute-start | bytes 233480 | tf_op jit(solution)/shard_map/ppermute | solution.py:291
  50.0 7.4 %collective-permute-start.1 = (bf16[304,128]{1,0:T(8,128)(2,1)S(1)}, bf16[304,128]{1,0:T(8,128)(2,1)S(1)}, u32[]{:S(2)}, u32[]{:S(2)}) collective-permute-start(bf16[304,128]{1,0:T(8,128)(2,1)S(1)} %add_convert_fusion.4), channel_id=1, source_target_pairs={{0,2},{1,3},{2,0},{3,1},{4,6},{5,7},{6,4},{7,5},{8,10},{9,11},{10,... | collective-permute-start | bytes 233480 | tf_op jit(solution)/shard_map/ppermute | solution.py:291
  57.4 5.9 %collective-permute-start.2 = (bf16[304,128]{1,0:T(8,128)(2,1)S(1)}, bf16[304,128]{1,0:T(8,128)(2,1)S(1)}, u32[]{:S(2)}, u32[]{:S(2)}) collective-permute-start(bf16[304,128]{1,0:T(8,128)(2,1)S(1)} %add_convert_fusion.3), channel_id=1, source_target_pairs={{0,4},{1,5},{2,6},{3,7},{4,0},{5,1},{6,2},{7,3},{8,12},{9,13},{10,... | collective-permute-start | bytes 233480 | tf_op jit(solution)/shard_map/ppermute | solution.py:291
  63.3 4.6 %collective-permute-start.3 = (bf16[304,128]{1,0:T(8,128)(2,1)S(1)}, bf16[304,128]{1,0:T(8,128)(2,1)S(1)}, u32[]{:S(2)}, u32[]{:S(2)}) collective-permute-start(bf16[304,128]{1,0:T(8,128)(2,1)S(1)} %add_convert_fusion.2), channel_id=1, source_target_pairs={{0,8},{1,9},{2,10},{3,11},{4,12},{5,13},{6,14},{7,15},{8,0},{9,1},... | collective-permute-start | bytes 233480 | tf_op jit(solution)/shard_map/ppermute | solution.py:291
  68.0 5.8 %collective-permute-start.4 = (bf16[304,128]{1,0:T(8,128)(2,1)S(1)}, bf16[304,128]{1,0:T(8,128)(2,1)S(1)}, u32[]{:S(2)}, u32[]{:S(2)}) collective-permute-start(bf16[304,128]{1,0:T(8,128)(2,1)S(1)} %add_convert_fusion.1), channel_id=1, source_target_pairs={{0,16},{1,17},{2,18},{3,19},{4,20},{5,21},{6,22},{7,23},{8,24},{9,... | collective-permute-start | bytes 233480 | tf_op jit(solution)/shard_map/ppermute | solution.py:291
  73.9 1.7 %collective-permute-start.5 = (bf16[304,128]{1,0:T(8,128)(2,1)S(1)}, bf16[304,128]{1,0:T(8,128)(2,1)S(1)}, u32[]{:S(2)}, u32[]{:S(2)}) collective-permute-start(bf16[304,128]{1,0:T(8,128)(2,1)S(1)} %add_convert_fusion.mine_ref), channel_id=1, source_target_pairs={{0,1},{1,0},{2,3},{3,2},{4,5},{5,4},{6,7},{7,6},{8,9},{9,8},{10,11... | collective-permute-start | bytes 233480 | tf_op jit(solution)/shard_map/ppermute | solution.py:291

commit v7 on v6

--- a/solution.py
+++ b/solution.py
@@ -110,7 +110,7 @@
     return before, row, after
 
 
-def kernels_kernel(w_ref, out_ref):
+def kernels_kernel(w_ref, first_ref, rest_ref):
     for layer in range(2):
         for back in range(2):
             rows = []
@@ -119,7 +119,11 @@
                 if back:
                     row = [tap.astype(F32).T.astype(BF16) for tap in row]
                 rows.append(jnp.concatenate(row, axis=1))
-            out_ref[2 * layer + back] = jnp.concatenate(rows, axis=0)
+            rows = jnp.concatenate(rows, axis=0)
+            if layer or back:
+                rest_ref[2 * layer + back - 1] = rows
+            else:
+                first_ref[...] = rows
 
 
 def line_of(parts_ref, count, channels, field, i):
@@ -141,10 +145,9 @@
     return jnp.concatenate([after, here, before], axis=0)
 
 
-def forward_layer(layer, share, lines, w_ref, b_ref, y_ref, give):
+def forward_layer(layer, share, lines, kernel, b_ref, y_ref, give):
     count, channels = y_ref.shape[0], y_ref.shape[1] // 3
     hops = 2**layer
-    kernel = w_ref[2 * layer]
     for i in range(count):
         stack = jnp.concatenate(taps(lines(i), hops * share), axis=0)
         y_ref[i] = product(kernel, stack)
@@ -159,7 +162,8 @@
 def stack_kernel(
     share,
     parts_ref,
-    w_ref,
+    first_ref,
+    rest_ref,
     b_ref,
     out_ref,
     gz0_ref,
@@ -201,13 +205,13 @@
     def line(i):
         return line_of(parts_ref, count, channels, 0, i)
 
-    forward_layer(0, share, line, w_ref, b_ref, y_ref, give_hidden)
-    forward_layer(1, share, lambda i: h_ref[i], w_ref, b_ref, y_ref, give_features)
+    forward_layer(0, share, line, first_ref[...], b_ref, y_ref, give_hidden)
+    forward_layer(1, share, lambda i: h_ref[i], rest_ref[1], b_ref, y_ref, give_features)
     send(0, 0, count)
 
     for layer in (1, 0):
         hops = 2**layer
-        kernel = w_ref[2 * layer + 1]
+        kernel = rest_ref[2 * layer]
         for i in range(count):
             if layer == 1:
                 gated = line_of(parts_ref, count, channels, 1, i).astype(F32) * s1_ref[i]
@@ -231,7 +235,7 @@
 
 
 def sums_kernel(
-    share, parts_ref, w_ref, b_ref, gz0_ref, gz1_ref, keep_ref, send_ref, rows_ref, h_ref, y_ref
+    share, parts_ref, first_ref, b_ref, gz0_ref, gz1_ref, keep_ref, send_ref, rows_ref, h_ref, y_ref
 ):
     count, channels, _ = gz0_ref.shape
     high = 3 * channels
@@ -242,7 +246,7 @@
     def give_hidden(i, pre, sigma):
         h_ref[i] = (pre * sigma).astype(BF16)
 
-    forward_layer(0, share, line, w_ref, b_ref, y_ref, give_hidden)
+    forward_layer(0, share, line, first_ref[...], b_ref, y_ref, give_hidden)
     biases = []
     for layer, gz_ref, lines in ((0, gz0_ref, line), (1, gz1_ref, lambda i: h_ref[i])):
         hops = 2**layer
@@ -333,9 +337,12 @@
         compiler_params=WIDE,
     )(inputs, cotangent)
     packed, weights = lax.optimization_barrier((packed, weights))
-    kernels = pl.pallas_call(
+    first, rest = pl.pallas_call(
         kernels_kernel,
-        out_shape=shape((4, 3 * channels, 3 * channels), BF16),
+        out_shape=[
+            shape((3 * channels, 3 * channels), BF16),
+            shape((3, 3 * channels, 3 * channels), BF16),
+        ],
         compiler_params=PARAMS,
     )(weights)
     parts = exchanged(packed)
@@ -358,7 +365,7 @@
             pltpu.SemaphoreType.DMA((lons + 1,)),
         ],
         compiler_params=PARAMS,
-    )(parts, kernels, column)
+    )(parts, first, rest, column)
     if blocks == 1:
         fields = fields.reshape(lons, 2 * channels, lats, width).transpose(0, 2, 1, 3)
         fields = fields.reshape(fields_shape)
@@ -377,7 +384,7 @@
         ],
         compiler_params=PARAMS,
         cost_estimate=pl.CostEstimate(flops=flops, bytes_accessed=3 * parts.size, transcendentals=0),
-    )(parts, kernels, column, gated0, gated1)
+    )(parts, first, column, gated0, gated1)
     mine = added(keep, send, devices)
     home, mine = lax.optimization_barrier((home, mine))
     other = partnered(mine, devices, 1)

time: 77.8 us -> 77.1 us (level); the launches traced: 76.6 us -> 76.7 us
  waiting for transfers between devices: 42.3 us -> 46 us
  local copies, waits for them, and re-layouts: 2.61 us -> 0.78 us
  starting transfers between devices: 18.9 us -> 17.2 us
    ppermute x6, waiting for transfers between devices: 17.2 us -> 20.8 us  [partnered(): return lax.ppermute(block, AXES, [(i, i ^ bit) for i in range(devices)])]
    unnamed x8 -> x4, local copies, waits for them, and re-layouts: 2.51 us -> 0.68 us
    ppermute x6, starting transfers between devices: 7.99 us -> 6.23 us  [partnered(): return lax.ppermute(block, AXES, [(i, i ^ bit) for i in range(devices)])]
where the time goes in v7:
time: 77.1 us; the launch traced here: 76.7 us
  waiting for transfers between devices  46 us (60%)
  starting transfers between devices  17.2 us (22%)
  Pallas kernels  11.9 us (15%)
  local copies, waits for them, and re-layouts  0.78 us (1%)
    all_to_all x2, waiting for transfers between devices, exchanged(): return lax.all_to_all(parts, AXES, 0, 0, tiled=True)  25.2 us
    ppermute x6, waiting for transfers between devices, partnered(): return lax.ppermute(block, AXES, [(i, i ^ bit) for i in range(devices)])  20.8 us
    all_to_all x2, starting transfers between devices, exchanged(): return lax.all_to_all(parts, AXES, 0, 0, tiled=True)  10.9 us
    ppermute x6, starting transfers between devices, partnered(): return lax.ppermute(block, AXES, [(i, i ^ bit) for i in range(devices)])  6.23 us
    pallas_call x1, Pallas kernels, local(): pl.pallas_call(functools.partial(stack_kernel, share), out_shape=[shape(p...  3.54 us
    pallas_call x1, Pallas kernels, local(): pl.pallas_call(functools.partial(pack_kernel, share), out_shape=shape(fie...  2.99 us
    pallas_call x1, Pallas kernels, local(): pl.pallas_call(functools.partial(sums_kernel, share), out_shape=[shape(ha...  2.48 us
    pallas_call x1, Pallas kernels, local(): pl.pallas_call(functools.partial(unpack_kernel, share), out_shape=[shape(...  1.62 us
  transfers between devices with their start and end apart: 8, of which 6 were waited for; matrix products, arithmetic and copies ran while one was open for 0% of the time, Pallas kernels for 6%

profile of v7, /device:TPU:0, one launch (start us, length us, event | category | flops | bytes accessed | tf_op | source)
XLA Modules:
  0.0 76.7 jit_solution(3020381056178544628)
XLA Ops:
  0.6 3.0 %shard_map.75 = bf16[32,128,128]{2,1,0:T(8,128)(2,1)} custom-call(bf16[64,16,256]{2,1,0:T(8,128)(2,1)} %x_ref.1, bf16[64,16,256]{2,1,0:T(8,128)(2,1)} %cot_ref.1), custom_call_target="tpu_custom_call" | custom-call | tf_op jit(solution)/shard_map/pallas_call | solution.py:326
  3.6 0.0 copy-start
  3.6 7.3 %all-to-all-start = ((bf16[32,128,128]{2,1,0:T(8,128)(2,1)}), bf16[32,128,128]{2,1,0:T(8,128)(2,1)S(1)}, u32[]{:S(2)}, u32[]{:S(2)}) async-start(bf16[32,128,128]{2,1,0:T(8,128)(2,1)} %shard_map.75), calls=%async_computation | async-start | bytes 2097152 | tf_op jit(solution)/shard_map/all_to_all | solution.py:307
  10.9 0.0 copy-start.1
  11.0 0.7 copy-done.1
  11.6 0.1 copy.8.b_ref
  11.7 0.0 copy-done
  11.7 0.2 shard_map.76
  12.0 25.2 %all-to-all-done.parts_ref = bf16[32,128,128]{2,1,0:T(8,128)(2,1)S(1)} async-done(((bf16[32,128,128]{2,1,0:T(8,128)(2,1)}), bf16[32,128,128]{2,1,0:T(8,128)(2,1)S(1)}, u32[]{:S(2)}, u32[]{:S(2)}) %all-to-all-start) | async-done | bytes 1048608 | tf_op jit(solution)/shard_map/all_to_all | solution.py:307
  37.2 3.5 %shard_map.77 = (bf16[32,128,128]{2,1,0:T(8,128)(2,1)}, bf16[8,64,512]{2,1,0:T(8,128)(2,1)S(1)}, bf16[8,64,512]{2,1,0:T(8,128)(2,1)S(1)}) custom-call(bf16[32,128,128]{2,1,0:T(8,128)(2,1)S(1)} %all-to-all-done.parts_ref, bf16[192,192]{1,0:T(8,128)(2,1)S(1)} %get-tuple-element.21.first_ref, bf16[3,192,192]{2,1,0:T(8,128)(2,1)S(1)} %get-tuple-element.22.rest_ref, ...), custom_call_target="tpu_custom_call" | custom-call | tf_op jit(solution)/shard_map/pallas_call | solution.py:355
  40.7 3.6 %all-to-all-start.1 = ((bf16[32,128,128]{2,1,0:T(8,128)(2,1)}), bf16[32,128,128]{2,1,0:T(8,128)(2,1)S(1)}, u32[]{:S(2)}, u32[]{:S(2)}) async-start(bf16[32,128,128]{2,1,0:T(8,128)(2,1)} %get-tuple-element.23), calls=%async_computation.1 | async-start | bytes 2097152 | tf_op jit(solution)/shard_map/all_to_all | solution.py:307
  44.4 2.5 %shard_map.78 = (f32[304,128]{1,0:T(8,128)S(1)}, bf16[304,128]{1,0:T(8,128)(2,1)S(1)}) custom-call(bf16[32,128,128]{2,1,0:T(8,128)(2,1)S(1)} %all-to-all-done.parts_ref, bf16[192,192]{1,0:T(8,128)(2,1)S(1)} %get-tuple-element.21.first_ref, f32[2,64,1]{2,1,0:T(8,128)S(1)} %copy.8.b_ref, bf16[8,64,512]{2,1,0:T(8,128)(2,1)S(1)} %get-tuple-element.24.gz0_ref, ...), custom_call_target="tpu_custom_call" | custom-call | flops 301989888 | bytes 1572864 | tf_op jit(solution)/shard_map/pallas_call | solution.py:377
  46.9 0.3 collective-permute-start
  47.2 1.0 %collective-permute-done = bf16[304,128]{1,0:T(8,128)(2,1)S(1)} collective-permute-done((bf16[304,128]{1,0:T(8,128)(2,1)S(1)}, bf16[304,128]{1,0:T(8,128)(2,1)S(1)}, u32[]{:S(2)}, u32[]{:S(2)}) %collective-permute-start) | collective-permute-done | bytes 77856 | tf_op jit(solution)/shard_map/ppermute | solution.py:295
  48.2 1.8 %collective-permute-start.1 = (bf16[304,128]{1,0:T(8,128)(2,1)S(1)}, bf16[304,128]{1,0:T(8,128)(2,1)S(1)}, u32[]{:S(2)}, u32[]{:S(2)}) collective-permute-start(bf16[304,128]{1,0:T(8,128)(2,1)S(1)} %add_convert_fusion.4), channel_id=1, source_target_pairs={{0,2},{1,3},{2,0},{3,1},{4,6},{5,7},{6,4},{7,5},{8,10},{9,11},{10,... | collective-permute-start | bytes 233480 | tf_op jit(solution)/shard_map/ppermute | solution.py:295
  50.1 6.6 %collective-permute-done.1 = bf16[304,128]{1,0:T(8,128)(2,1)S(1)} collective-permute-done((bf16[304,128]{1,0:T(8,128)(2,1)S(1)}, bf16[304,128]{1,0:T(8,128)(2,1)S(1)}, u32[]{:S(2)}, u32[]{:S(2)}) %collective-permute-start.1) | collective-permute-done | bytes 77856 | tf_op jit(solution)/shard_map/ppermute | solution.py:295
  56.7 2.6 %collective-permute-start.2 = (bf16[304,128]{1,0:T(8,128)(2,1)S(1)}, bf16[304,128]{1,0:T(8,128)(2,1)S(1)}, u32[]{:S(2)}, u32[]{:S(2)}) collective-permute-start(bf16[304,128]{1,0:T(8,128)(2,1)S(1)} %add_convert_fusion.3), channel_id=1, source_target_pairs={{0,4},{1,5},{2,6},{3,7},{4,0},{5,1},{6,2},{7,3},{8,12},{9,13},{10,... | collective-permute-start | bytes 233480 | tf_op jit(solution)/shard_map/ppermute | solution.py:295
  59.3 3.3 %collective-permute-done.2 = bf16[304,128]{1,0:T(8,128)(2,1)S(1)} collective-permute-done((bf16[304,128]{1,0:T(8,128)(2,1)S(1)}, bf16[304,128]{1,0:T(8,128)(2,1)S(1)}, u32[]{:S(2)}, u32[]{:S(2)}) %collective-permute-start.2) | collective-permute-done | bytes 77856 | tf_op jit(solution)/shard_map/ppermute | solution.py:295
  62.6 0.1 collective-permute-start.3
  62.7 4.6 %collective-permute-done.3 = bf16[304,128]{1,0:T(8,128)(2,1)S(1)} collective-permute-done((bf16[304,128]{1,0:T(8,128)(2,1)S(1)}, bf16[304,128]{1,0:T(8,128)(2,1)S(1)}, u32[]{:S(2)}, u32[]{:S(2)}) %collective-permute-start.3) | collective-permute-done | bytes 77856 | tf_op jit(solution)/shard_map/ppermute | solution.py:295
  67.3 1.4 %collective-permute-start.4 = (bf16[304,128]{1,0:T(8,128)(2,1)S(1)}, bf16[304,128]{1,0:T(8,128)(2,1)S(1)}, u32[]{:S(2)}, u32[]{:S(2)}) collective-permute-start(bf16[304,128]{1,0:T(8,128)(2,1)S(1)} %add_convert_fusion.1), channel_id=1, source_target_pairs={{0,16},{1,17},{2,18},{3,19},{4,20},{5,21},{6,22},{7,23},{8,24},{9,... | collective-permute-start | bytes 233480 | tf_op jit(solution)/shard_map/ppermute | solution.py:295
  68.6 5.3 %collective-permute-done.4 = bf16[304,128]{1,0:T(8,128)(2,1)S(1)} collective-permute-done((bf16[304,128]{1,0:T(8,128)(2,1)S(1)}, bf16[304,128]{1,0:T(8,128)(2,1)S(1)}, u32[]{:S(2)}, u32[]{:S(2)}) %collective-permute-start.4) | collective-permute-done | bytes 77856 | tf_op jit(solution)/shard_map/ppermute | solution.py:295
  74.0 0.0 all-to-all-done.1.parts_ref
  74.0 0.1 collective-permute-start.5
  74.1 1.6 %shard_map.79 = (bf16[64,16,256]{2,1,0:T(8,128)(2,1)}, bf16[64,16,256]{2,1,0:T(8,128)(2,1)}) custom-call(bf16[32,128,128]{2,1,0:T(8,128)(2,1)S(1)} %all-to-all-done.1.parts_ref), custom_call_target="tpu_custom_call" | custom-call | flops 268435456 | bytes 2097152 | tf_op jit(solution)/shard_map/pallas_call | solution.py:391
  75.7 0.0 collective-permute-done.5.other_ref
  75.7 1.0 %shard_map.80 = (f32[2,3,3,64,64]{4,3,2,1,0:T(8,128)}, f32[2,64]{1,0:T(2,128)}) custom-call(bf16[304,128]{1,0:T(8,128)(2,1)S(1)} %add_convert_fusion.mine_ref, bf16[304,128]{1,0:T(8,128)(2,1)S(1)} %collective-permute-done.5.other_ref), custom_call_target="tpu_custom_call" | custom-call | tf_op jit(solution)/shard_map/pallas_call | solution.py:404
  (5 shorter events, 0.1 us)
Async XLA Ops:
  3.6 8.1 %copy-start = (bf16[2,3,3,64,64]{4,3,2,1,0:T(8,128)(2,1)S(1)}, bf16[2,3,3,64,64]{4,3,2,1,0:T(8,128)(2,1)}, u32[]{:S(2)}) copy-start(bf16[2,3,3,64,64]{4,3,2,1,0:T(8,128)(2,1)} %w_ref) | copy-start | bytes 442372
  3.6 33.5 %all-to-all-start = ((bf16[32,128,128]{2,1,0:T(8,128)(2,1)}), bf16[32,128,128]{2,1,0:T(8,128)(2,1)S(1)}, u32[]{:S(2)}, u32[]{:S(2)}) async-start(bf16[32,128,128]{2,1,0:T(8,128)(2,1)} %shard_map.75), calls=%async_computation | async-start | bytes 2097152 | tf_op jit(solution)/shard_map/all_to_all | solution.py:307
  10.9 0.7 copy-start.1
  40.7 33.2 %all-to-all-start.1 = ((bf16[32,128,128]{2,1,0:T(8,128)(2,1)}), bf16[32,128,128]{2,1,0:T(8,128)(2,1)S(1)}, u32[]{:S(2)}, u32[]{:S(2)}) async-start(bf16[32,128,128]{2,1,0:T(8,128)(2,1)} %get-tuple-element.23), calls=%async_computation.1 | async-start | bytes 2097152 | tf_op jit(solution)/shard_map/all_to_all | solution.py:307
  46.9 1.3 %collective-permute-start = (bf16[304,128]{1,0:T(8,128)(2,1)S(1)}, bf16[304,128]{1,0:T(8,128)(2,1)S(1)}, u32[]{:S(2)}, u32[]{:S(2)}) collective-permute-start(bf16[304,128]{1,0:T(8,128)(2,1)S(1)} %get-tuple-element.27), channel_id=1, source_target_pairs={{0,1},{1,0},{2,3},{3,2},{4,5},{5,4},{6,7},{7,6},{8,9},{9,8},{10,11... | collective-permute-start | bytes 233480 | tf_op jit(solution)/shard_map/ppermute | solution.py:295
  48.2 8.4 %collective-permute-start.1 = (bf16[304,128]{1,0:T(8,128)(2,1)S(1)}, bf16[304,128]{1,0:T(8,128)(2,1)S(1)}, u32[]{:S(2)}, u32[]{:S(2)}) collective-permute-start(bf16[304,128]{1,0:T(8,128)(2,1)S(1)} %add_convert_fusion.4), channel_id=1, source_target_pairs={{0,2},{1,3},{2,0},{3,1},{4,6},{5,7},{6,4},{7,5},{8,10},{9,11},{10,... | collective-permute-start | bytes 233480 | tf_op jit(solution)/shard_map/ppermute | solution.py:295
  56.7 5.9 %collective-permute-start.2 = (bf16[304,128]{1,0:T(8,128)(2,1)S(1)}, bf16[304,128]{1,0:T(8,128)(2,1)S(1)}, u32[]{:S(2)}, u32[]{:S(2)}) collective-permute-start(bf16[304,128]{1,0:T(8,128)(2,1)S(1)} %add_convert_fusion.3), channel_id=1, source_target_pairs={{0,4},{1,5},{2,6},{3,7},{4,0},{5,1},{6,2},{7,3},{8,12},{9,13},{10,... | collective-permute-start | bytes 233480 | tf_op jit(solution)/shard_map/ppermute | solution.py:295
  62.6 4.6 %collective-permute-start.3 = (bf16[304,128]{1,0:T(8,128)(2,1)S(1)}, bf16[304,128]{1,0:T(8,128)(2,1)S(1)}, u32[]{:S(2)}, u32[]{:S(2)}) collective-permute-start(bf16[304,128]{1,0:T(8,128)(2,1)S(1)} %add_convert_fusion.2), channel_id=1, source_target_pairs={{0,8},{1,9},{2,10},{3,11},{4,12},{5,13},{6,14},{7,15},{8,0},{9,1},... | collective-permute-start | bytes 233480 | tf_op jit(solution)/shard_map/ppermute | solution.py:295
  67.3 6.7 %collective-permute-start.4 = (bf16[304,128]{1,0:T(8,128)(2,1)S(1)}, bf16[304,128]{1,0:T(8,128)(2,1)S(1)}, u32[]{:S(2)}, u32[]{:S(2)}) collective-permute-start(bf16[304,128]{1,0:T(8,128)(2,1)S(1)} %add_convert_fusion.1), channel_id=1, source_target_pairs={{0,16},{1,17},{2,18},{3,19},{4,20},{5,21},{6,22},{7,23},{8,24},{9,... | collective-permute-start | bytes 233480 | tf_op jit(solution)/shard_map/ppermute | solution.py:295
  74.0 1.7 %collective-permute-start.5 = (bf16[304,128]{1,0:T(8,128)(2,1)S(1)}, bf16[304,128]{1,0:T(8,128)(2,1)S(1)}, u32[]{:S(2)}, u32[]{:S(2)}) collective-permute-start(bf16[304,128]{1,0:T(8,128)(2,1)S(1)} %add_convert_fusion.mine_ref), channel_id=1, source_target_pairs={{0,1},{1,0},{2,3},{3,2},{4,5},{5,4},{6,7},{7,6},{8,9},{9,8},{10,11... | collective-permute-start | bytes 233480 | tf_op jit(solution)/shard_map/ppermute | solution.py:295

commit v8 on v7

--- a/solution.py
+++ b/solution.py
@@ -297,10 +297,14 @@
 
 def added(keep, send, devices):
     total = keep + partnered(send, devices, 1).astype(F32)
-    for bit in [2 << k for k in range((devices // 2).bit_length() - 1)]:
+    bit = 2
+    while True:
         rounded = total.astype(BF16)
-        total = rounded.astype(F32) + partnered(rounded, devices, bit).astype(F32)
-    return total.astype(BF16)
+        came = partnered(rounded, devices, bit)
+        bit *= 2
+        if bit >= devices:
+            return rounded, came
+        total = rounded.astype(F32) + came.astype(F32)
 
 
 def exchanged(parts):
@@ -385,9 +389,7 @@
         compiler_params=PARAMS,
         cost_estimate=pl.CostEstimate(flops=flops, bytes_accessed=3 * parts.size, transcendentals=0),
     )(parts, first, column, gated0, gated1)
-    mine = added(keep, send, devices)
-    home, mine = lax.optimization_barrier((home, mine))
-    other = partnered(mine, devices, 1)
+    rounded, came = added(keep, send, devices)
     features_out, grad_input = pl.pallas_call(
         functools.partial(unpack_kernel, share),
         out_shape=[shape(inputs.shape, BF16), shape(inputs.shape, BF16)],
@@ -401,6 +403,9 @@
             flops=4 * inputs.size * lat_rows, bytes_accessed=8 * inputs.size, transcendentals=0
         ),
     )(home)
+    came, grad_input = lax.optimization_barrier((came, grad_input))
+    mine = (rounded.astype(F32) + came.astype(F32)).astype(BF16)
+    other = partnered(mine, devices, 1)
     weight_grads, bias_grads = pl.pallas_call(
         functools.partial(assemble_kernel, scale),
         out_shape=[shape(weights.shape, F32), shape(biases.shape, F32)],

time: 77.1 us -> 77.1 us (level)
    all_to_all x2, waiting for transfers between devices: 25.2 us -> 29.3 us  [exchanged(): return lax.all_to_all(parts, AXES, 0, 0, tiled=True)]
    ppermute x6, waiting for transfers between devices: 20.8 us -> 16.8 us  [partnered(): return lax.ppermute(block, AXES, [(i, i ^ bit) for i in range(devices)])]
  transfers between devices with their start and end apart: 8 -> 8, of which waited for: 6 -> 7; matrix products, arithmetic and copies ran while one was open for 0% -> 0% of each run, Pallas kernels for 6% -> 6%
where the time goes in v8:
time: 77.1 us; the launch traced here: 76.8 us
  waiting for transfers between devices  46.1 us (60%)
  starting transfers between devices  17.2 us (22%)
  Pallas kernels  11.9 us (15%)
  local copies, waits for them, and re-layouts  0.78 us (1%)
    all_to_all x2, waiting for transfers between devices, exchanged(): return lax.all_to_all(parts, AXES, 0, 0, tiled=True)  29.3 us
    ppermute x6, waiting for transfers between devices, partnered(): return lax.ppermute(block, AXES, [(i, i ^ bit) for i in range(devices)])  16.8 us
    all_to_all x2, starting transfers between devices, exchanged(): return lax.all_to_all(parts, AXES, 0, 0, tiled=True)  10.9 us
    ppermute x6, starting transfers between devices, partnered(): return lax.ppermute(block, AXES, [(i, i ^ bit) for i in range(devices)])  6.23 us
    pallas_call x1, Pallas kernels, local(): pl.pallas_call(functools.partial(stack_kernel, share), out_shape=[shape(p...  3.54 us
    pallas_call x1, Pallas kernels, local(): pl.pallas_call(functools.partial(pack_kernel, share), out_shape=shape(fie...  2.99 us
    pallas_call x1, Pallas kernels, local(): pl.pallas_call(functools.partial(sums_kernel, share), out_shape=[shape(ha...  2.48 us
    pallas_call x1, Pallas kernels, local(): pl.pallas_call(functools.partial(unpack_kernel, share), out_shape=[shape(...  1.61 us
  transfers between devices with their start and end apart: 8, of which 7 were waited for; matrix products, arithmetic and copies ran while one was open for 0% of the time, Pallas kernels for 6%

profile of v8, /device:TPU:0, one launch (start us, length us, event | category | flops | bytes accessed | tf_op | source)
XLA Modules:
  0.0 76.8 jit_solution(13389042675355272487)
XLA Ops:
  0.6 3.0 %shard_map.75 = bf16[32,128,128]{2,1,0:T(8,128)(2,1)} custom-call(bf16[64,16,256]{2,1,0:T(8,128)(2,1)} %x_ref.1, bf16[64,16,256]{2,1,0:T(8,128)(2,1)} %cot_ref.1), custom_call_target="tpu_custom_call" | custom-call | tf_op jit(solution)/shard_map/pallas_call | solution.py:330
  3.6 0.0 copy-start
  3.6 7.3 %all-to-all-start = ((bf16[32,128,128]{2,1,0:T(8,128)(2,1)}), bf16[32,128,128]{2,1,0:T(8,128)(2,1)S(1)}, u32[]{:S(2)}, u32[]{:S(2)}) async-start(bf16[32,128,128]{2,1,0:T(8,128)(2,1)} %shard_map.75), calls=%async_computation | async-start | bytes 2097152 | tf_op jit(solution)/shard_map/all_to_all | solution.py:311
  10.9 0.0 copy-start.1
  11.0 0.7 copy-done.1
  11.6 0.1 copy.8.b_ref
  11.7 0.0 copy-done
  11.7 0.2 shard_map.76
  12.0 25.2 %all-to-all-done.parts_ref = bf16[32,128,128]{2,1,0:T(8,128)(2,1)S(1)} async-done(((bf16[32,128,128]{2,1,0:T(8,128)(2,1)}), bf16[32,128,128]{2,1,0:T(8,128)(2,1)S(1)}, u32[]{:S(2)}, u32[]{:S(2)}) %all-to-all-start) | async-done | bytes 1048608 | tf_op jit(solution)/shard_map/all_to_all | solution.py:311
  37.2 3.5 %shard_map.77 = (bf16[32,128,128]{2,1,0:T(8,128)(2,1)}, bf16[8,64,512]{2,1,0:T(8,128)(2,1)S(1)}, bf16[8,64,512]{2,1,0:T(8,128)(2,1)S(1)}) custom-call(bf16[32,128,128]{2,1,0:T(8,128)(2,1)S(1)} %all-to-all-done.parts_ref, bf16[192,192]{1,0:T(8,128)(2,1)S(1)} %get-tuple-element.21.first_ref, bf16[3,192,192]{2,1,0:T(8,128)(2,1)S(1)} %get-tuple-element.22.rest_ref, ...), custom_call_target="tpu_custom_call" | custom-call | tf_op jit(solution)/shard_map/pallas_call | solution.py:359
  40.7 3.6 %all-to-all-start.1 = ((bf16[32,128,128]{2,1,0:T(8,128)(2,1)}), bf16[32,128,128]{2,1,0:T(8,128)(2,1)S(1)}, u32[]{:S(2)}, u32[]{:S(2)}) async-start(bf16[32,128,128]{2,1,0:T(8,128)(2,1)} %get-tuple-element.23), calls=%async_computation.1 | async-start | bytes 2097152 | tf_op jit(solution)/shard_map/all_to_all | solution.py:311
  44.4 2.5 %shard_map.79 = (f32[304,128]{1,0:T(8,128)S(1)}, bf16[304,128]{1,0:T(8,128)(2,1)S(1)}) custom-call(bf16[32,128,128]{2,1,0:T(8,128)(2,1)S(1)} %all-to-all-done.parts_ref, bf16[192,192]{1,0:T(8,128)(2,1)S(1)} %get-tuple-element.21.first_ref, f32[2,64,1]{2,1,0:T(8,128)S(1)} %copy.8.b_ref, bf16[8,64,512]{2,1,0:T(8,128)(2,1)S(1)} %get-tuple-element.25.gz0_ref, ...), custom_call_target="tpu_custom_call" | custom-call | flops 301989888 | bytes 1572864 | tf_op jit(solution)/shard_map/pallas_call | solution.py:381
  46.9 0.3 collective-permute-start
  47.2 1.0 %collective-permute-done = bf16[304,128]{1,0:T(8,128)(2,1)S(1)} collective-permute-done((bf16[304,128]{1,0:T(8,128)(2,1)S(1)}, bf16[304,128]{1,0:T(8,128)(2,1)S(1)}, u32[]{:S(2)}, u32[]{:S(2)}) %collective-permute-start) | collective-permute-done | bytes 77856 | tf_op jit(solution)/shard_map/ppermute | solution.py:295
  48.2 1.8 %collective-permute-start.1 = (bf16[304,128]{1,0:T(8,128)(2,1)S(1)}, bf16[304,128]{1,0:T(8,128)(2,1)S(1)}, u32[]{:S(2)}, u32[]{:S(2)}) collective-permute-start(bf16[304,128]{1,0:T(8,128)(2,1)S(1)} %add_convert_fusion.4), channel_id=1, source_target_pairs={{0,2},{1,3},{2,0},{3,1},{4,6},{5,7},{6,4},{7,5},{8,10},{9,11},{10,... | collective-permute-start | bytes 233480 | tf_op jit(solution)/shard_map/ppermute | solution.py:295
  50.1 6.6 %collective-permute-done.1 = bf16[304,128]{1,0:T(8,128)(2,1)S(1)} collective-permute-done((bf16[304,128]{1,0:T(8,128)(2,1)S(1)}, bf16[304,128]{1,0:T(8,128)(2,1)S(1)}, u32[]{:S(2)}, u32[]{:S(2)}) %collective-permute-start.1) | collective-permute-done | bytes 77856 | tf_op jit(solution)/shard_map/ppermute | solution.py:295
  56.7 2.6 %collective-permute-start.2 = (bf16[304,128]{1,0:T(8,128)(2,1)S(1)}, bf16[304,128]{1,0:T(8,128)(2,1)S(1)}, u32[]{:S(2)}, u32[]{:S(2)}) collective-permute-start(bf16[304,128]{1,0:T(8,128)(2,1)S(1)} %add_convert_fusion.3), channel_id=1, source_target_pairs={{0,4},{1,5},{2,6},{3,7},{4,0},{5,1},{6,2},{7,3},{8,12},{9,13},{10,... | collective-permute-start | bytes 233480 | tf_op jit(solution)/shard_map/ppermute | solution.py:295
  59.3 3.3 %collective-permute-done.2 = bf16[304,128]{1,0:T(8,128)(2,1)S(1)} collective-permute-done((bf16[304,128]{1,0:T(8,128)(2,1)S(1)}, bf16[304,128]{1,0:T(8,128)(2,1)S(1)}, u32[]{:S(2)}, u32[]{:S(2)}) %collective-permute-start.2) | collective-permute-done | bytes 77856 | tf_op jit(solution)/shard_map/ppermute | solution.py:295
  62.6 0.1 collective-permute-start.3
  62.7 4.6 %collective-permute-done.3 = bf16[304,128]{1,0:T(8,128)(2,1)S(1)} collective-permute-done((bf16[304,128]{1,0:T(8,128)(2,1)S(1)}, bf16[304,128]{1,0:T(8,128)(2,1)S(1)}, u32[]{:S(2)}, u32[]{:S(2)}) %collective-permute-start.3) | collective-permute-done | bytes 77856 | tf_op jit(solution)/shard_map/ppermute | solution.py:295
  67.3 1.4 %collective-permute-start.4 = (bf16[304,128]{1,0:T(8,128)(2,1)S(1)}, bf16[304,128]{1,0:T(8,128)(2,1)S(1)}, u32[]{:S(2)}, u32[]{:S(2)}) collective-permute-start(bf16[304,128]{1,0:T(8,128)(2,1)S(1)} %add_convert_fusion.1), channel_id=1, source_target_pairs={{0,16},{1,17},{2,18},{3,19},{4,20},{5,21},{6,22},{7,23},{8,24},{9,... | collective-permute-start | bytes 233480 | tf_op jit(solution)/shard_map/ppermute | solution.py:295
  68.6 4.1 %all-to-all-done.1.parts_ref = bf16[32,128,128]{2,1,0:T(8,128)(2,1)S(1)} async-done(((bf16[32,128,128]{2,1,0:T(8,128)(2,1)}), bf16[32,128,128]{2,1,0:T(8,128)(2,1)S(1)}, u32[]{:S(2)}, u32[]{:S(2)}) %all-to-all-start.1) | async-done | bytes 1048608 | tf_op jit(solution)/shard_map/all_to_all | solution.py:311
  72.7 1.6 %shard_map.78 = (bf16[64,16,256]{2,1,0:T(8,128)(2,1)}, bf16[64,16,256]{2,1,0:T(8,128)(2,1)}) custom-call(bf16[32,128,128]{2,1,0:T(8,128)(2,1)S(1)} %all-to-all-done.1.parts_ref), custom_call_target="tpu_custom_call" | custom-call | flops 268435456 | bytes 2097152 | tf_op jit(solution)/shard_map/pallas_call | solution.py:393
  74.4 0.0 collective-permute-done.4
  74.4 0.1 collective-permute-start.5
  74.5 1.3 %collective-permute-done.5.other_ref = bf16[304,128]{1,0:T(8,128)(2,1)S(1)} collective-permute-done((bf16[304,128]{1,0:T(8,128)(2,1)S(1)}, bf16[304,128]{1,0:T(8,128)(2,1)S(1)}, u32[]{:S(2)}, u32[]{:S(2)}) %collective-permute-start.5) | collective-permute-done | bytes 77856 | tf_op jit(solution)/shard_map/ppermute | solution.py:295
  75.7 1.0 %shard_map.80 = (f32[2,3,3,64,64]{4,3,2,1,0:T(8,128)}, f32[2,64]{1,0:T(2,128)}) custom-call(bf16[304,128]{1,0:T(8,128)(2,1)S(1)} %add_convert_fusion.mine_ref, bf16[304,128]{1,0:T(8,128)(2,1)S(1)} %collective-permute-done.5.other_ref), custom_call_target="tpu_custom_call" | custom-call | tf_op jit(solution)/shard_map/pallas_call | solution.py:409
  (5 shorter events, 0.1 us)
Async XLA Ops:
  3.6 8.1 %copy-start = (bf16[2,3,3,64,64]{4,3,2,1,0:T(8,128)(2,1)S(1)}, bf16[2,3,3,64,64]{4,3,2,1,0:T(8,128)(2,1)}, u32[]{:S(2)}) copy-start(bf16[2,3,3,64,64]{4,3,2,1,0:T(8,128)(2,1)} %w_ref) | copy-start | bytes 442372
  3.6 33.5 %all-to-all-start = ((bf16[32,128,128]{2,1,0:T(8,128)(2,1)}), bf16[32,128,128]{2,1,0:T(8,128)(2,1)S(1)}, u32[]{:S(2)}, u32[]{:S(2)}) async-start(bf16[32,128,128]{2,1,0:T(8,128)(2,1)} %shard_map.75), calls=%async_computation | async-start | bytes 2097152 | tf_op jit(solution)/shard_map/all_to_all | solution.py:311
  10.9 0.7 copy-start.1
  40.7 32.0 %all-to-all-start.1 = ((bf16[32,128,128]{2,1,0:T(8,128)(2,1)}), bf16[32,128,128]{2,1,0:T(8,128)(2,1)S(1)}, u32[]{:S(2)}, u32[]{:S(2)}) async-start(bf16[32,128,128]{2,1,0:T(8,128)(2,1)} %get-tuple-element.23), calls=%async_computation.1 | async-start | bytes 2097152 | tf_op jit(solution)/shard_map/all_to_all | solution.py:311
  46.9 1.3 %collective-permute-start = (bf16[304,128]{1,0:T(8,128)(2,1)S(1)}, bf16[304,128]{1,0:T(8,128)(2,1)S(1)}, u32[]{:S(2)}, u32[]{:S(2)}) collective-permute-start(bf16[304,128]{1,0:T(8,128)(2,1)S(1)} %get-tuple-element.28), channel_id=1, source_target_pairs={{0,1},{1,0},{2,3},{3,2},{4,5},{5,4},{6,7},{7,6},{8,9},{9,8},{10,11... | collective-permute-start | bytes 233480 | tf_op jit(solution)/shard_map/ppermute | solution.py:295
  48.2 8.4 %collective-permute-start.1 = (bf16[304,128]{1,0:T(8,128)(2,1)S(1)}, bf16[304,128]{1,0:T(8,128)(2,1)S(1)}, u32[]{:S(2)}, u32[]{:S(2)}) collective-permute-start(bf16[304,128]{1,0:T(8,128)(2,1)S(1)} %add_convert_fusion.4), channel_id=1, source_target_pairs={{0,2},{1,3},{2,0},{3,1},{4,6},{5,7},{6,4},{7,5},{8,10},{9,11},{10,... | collective-permute-start | bytes 233480 | tf_op jit(solution)/shard_map/ppermute | solution.py:295
  56.7 5.9 %collective-permute-start.2 = (bf16[304,128]{1,0:T(8,128)(2,1)S(1)}, bf16[304,128]{1,0:T(8,128)(2,1)S(1)}, u32[]{:S(2)}, u32[]{:S(2)}) collective-permute-start(bf16[304,128]{1,0:T(8,128)(2,1)S(1)} %add_convert_fusion.3), channel_id=1, source_target_pairs={{0,4},{1,5},{2,6},{3,7},{4,0},{5,1},{6,2},{7,3},{8,12},{9,13},{10,... | collective-permute-start | bytes 233480 | tf_op jit(solution)/shard_map/ppermute | solution.py:295
  62.6 4.6 %collective-permute-start.3 = (bf16[304,128]{1,0:T(8,128)(2,1)S(1)}, bf16[304,128]{1,0:T(8,128)(2,1)S(1)}, u32[]{:S(2)}, u32[]{:S(2)}) collective-permute-start(bf16[304,128]{1,0:T(8,128)(2,1)S(1)} %add_convert_fusion.2), channel_id=1, source_target_pairs={{0,8},{1,9},{2,10},{3,11},{4,12},{5,13},{6,14},{7,15},{8,0},{9,1},... | collective-permute-start | bytes 233480 | tf_op jit(solution)/shard_map/ppermute | solution.py:295
  67.3 7.1 %collective-permute-start.4 = (bf16[304,128]{1,0:T(8,128)(2,1)S(1)}, bf16[304,128]{1,0:T(8,128)(2,1)S(1)}, u32[]{:S(2)}, u32[]{:S(2)}) collective-permute-start(bf16[304,128]{1,0:T(8,128)(2,1)S(1)} %add_convert_fusion.1), channel_id=1, source_target_pairs={{0,16},{1,17},{2,18},{3,19},{4,20},{5,21},{6,22},{7,23},{8,24},{9,... | collective-permute-start | bytes 233480 | tf_op jit(solution)/shard_map/ppermute | solution.py:295
  74.4 1.3 %collective-permute-start.5 = (bf16[304,128]{1,0:T(8,128)(2,1)S(1)}, bf16[304,128]{1,0:T(8,128)(2,1)S(1)}, u32[]{:S(2)}, u32[]{:S(2)}) collective-permute-start(bf16[304,128]{1,0:T(8,128)(2,1)S(1)} %add_convert_fusion.mine_ref), channel_id=1, source_target_pairs={{0,1},{1,0},{2,3},{3,2},{4,5},{5,4},{6,7},{7,6},{8,9},{9,8},{10,11... | collective-permute-start | bytes 233480 | tf_op jit(solution)/shard_map/ppermute | solution.py:295

commit v9 on v8

--- a/solution.py
+++ b/solution.py
@@ -70,35 +70,34 @@
         departure.wait()
 
 
-def unpack_kernel(share, parts_ref, feat_ref, grad_ref, buf, sems):
-    _, channels, cols, lat_rows = buf.shape
+def unpack_kernel(share, field, parts_ref, out_ref, buf, sems):
+    channels, cols, lat_rows = buf.shape
     devices, _, width = parts_ref.shape
     groups = devices // cols
     part = min(channels, 256 // cols)
     lanes = lane_order(cols, lat_rows, share, True)
     order = row_order(cols, part)
     departures = []
-    for at, out_ref in enumerate((feat_ref, grad_ref)):
-        for first in range(0, channels, part):
-            start = at * channels + first
-            rows = [
-                jnp.concatenate(
-                    [
-                        parts_ref[col * groups + group, start : start + part, :]
-                        for group in range(groups)
-                    ],
-                    axis=1,
-                )
-                for col in range(cols)
-            ]
-            rows = product(jnp.concatenate(rows, axis=0), lanes).astype(BF16)
-            rows = product(order, rows).astype(BF16)
-            buf[at, first : first + part] = rows.reshape(part, cols, lat_rows)
-            rows = pl.ds(first, part)
-            departures.append(
-                pltpu.make_async_copy(buf.at[at, rows], out_ref.at[rows], sems.at[len(departures)])
+    for first in range(0, channels, part):
+        start = field * channels + first
+        rows = [
+            jnp.concatenate(
+                [
+                    parts_ref[col * groups + group, start : start + part, :]
+                    for group in range(groups)
+                ],
+                axis=1,
             )
-            departures[-1].start()
+            for col in range(cols)
+        ]
+        rows = product(jnp.concatenate(rows, axis=0), lanes).astype(BF16)
+        rows = product(order, rows).astype(BF16)
+        buf[first : first + part] = rows.reshape(part, cols, lat_rows)
+        rows = pl.ds(first, part)
+        departures.append(
+            pltpu.make_async_copy(buf.at[rows], out_ref.at[rows], sems.at[len(departures)])
+        )
+        departures[-1].start()
     for departure in departures:
         departure.wait()
 
@@ -390,20 +389,24 @@
         cost_estimate=pl.CostEstimate(flops=flops, bytes_accessed=3 * parts.size, transcendentals=0),
     )(parts, first, column, gated0, gated1)
     rounded, came = added(keep, send, devices)
-    features_out, grad_input = pl.pallas_call(
-        functools.partial(unpack_kernel, share),
-        out_shape=[shape(inputs.shape, BF16), shape(inputs.shape, BF16)],
-        out_specs=[hbm, hbm],
-        scratch_shapes=[
-            pltpu.VMEM((2,) + inputs.shape, BF16),
-            pltpu.SemaphoreType.DMA((chunks,)),
-        ],
-        compiler_params=PARAMS,
-        cost_estimate=pl.CostEstimate(
-            flops=4 * inputs.size * lat_rows, bytes_accessed=8 * inputs.size, transcendentals=0
-        ),
-    )(home)
-    came, grad_input = lax.optimization_barrier((came, grad_input))
+    def unpacked(field, parts):
+        return pl.pallas_call(
+            functools.partial(unpack_kernel, share, field),
+            out_shape=shape(inputs.shape, BF16),
+            out_specs=hbm,
+            scratch_shapes=[
+                pltpu.VMEM(inputs.shape, BF16),
+                pltpu.SemaphoreType.DMA((chunks // 2,)),
+            ],
+            compiler_params=PARAMS,
+            cost_estimate=pl.CostEstimate(
+                flops=2 * inputs.size * lat_rows, bytes_accessed=4 * inputs.size, transcendentals=0
+            ),
+        )(parts)
+
+    features_out = unpacked(0, home)
+    came, features_out, home = lax.optimization_barrier((came, features_out, home))
+    grad_input = unpacked(1, home)
     mine = (rounded.astype(F32) + came.astype(F32)).astype(BF16)
     other = partnered(mine, devices, 1)
     weight_grads, bias_grads = pl.pallas_call(

time: 77.1 us -> 76.9 us (level)
  waiting for transfers between devices: 46.1 us -> 44.8 us
  Pallas kernels: 11.9 us -> 12.9 us
    ppermute x6, waiting for transfers between devices: 16.8 us -> 15.5 us  [partnered(): return lax.ppermute(block, AXES, [(i, i ^ bit) for i in range(devices)])]
    pallas_call x1 -> x2, Pallas kernels: 1.61 us -> 2.62 us  [unpacked(): pl.pallas_call(functools.partial(unpack_kernel, share, field), out_shape=...]
  transfers between devices with their start and end apart: 8 -> 8, of which waited for: 7 -> 6; matrix products, arithmetic and copies ran while one was open for 0% -> 0% of each run, Pallas kernels for 6% -> 7%
where the time goes in v9:
time: 76.9 us; the launch traced here: 76.5 us
  waiting for transfers between devices  44.8 us (58%)
  starting transfers between devices  17.2 us (22%)
  Pallas kernels  12.9 us (17%)
  local copies, waits for them, and re-layouts  0.78 us (1%)
  between operations  0.78 us (1%)
    all_to_all x2, waiting for transfers between devices, exchanged(): return lax.all_to_all(parts, AXES, 0, 0, tiled=True)  29.3 us
    ppermute x6, waiting for transfers between devices, partnered(): return lax.ppermute(block, AXES, [(i, i ^ bit) for i in range(devices)])  15.5 us
    all_to_all x2, starting transfers between devices, exchanged(): return lax.all_to_all(parts, AXES, 0, 0, tiled=True)  10.9 us
    ppermute x6, starting transfers between devices, partnered(): return lax.ppermute(block, AXES, [(i, i ^ bit) for i in range(devices)])  6.23 us
    pallas_call x1, Pallas kernels, local(): pl.pallas_call(functools.partial(stack_kernel, share), out_shape=[shape(p...  3.53 us
    pallas_call x1, Pallas kernels, local(): pl.pallas_call(functools.partial(pack_kernel, share), out_shape=shape(fie...  2.97 us
    pallas_call x2, Pallas kernels, unpacked(): pl.pallas_call(functools.partial(unpack_kernel, share, field), out_shape=...  2.62 us
    pallas_call x1, Pallas kernels, local(): pl.pallas_call(functools.partial(sums_kernel, share), out_shape=[shape(ha...  2.49 us
  transfers between devices with their start and end apart: 8, of which 6 were waited for; matrix products, arithmetic and copies ran while one was open for 0% of the time, Pallas kernels for 7%

profile of v9, /device:TPU:0, one launch (start us, length us, event | category | flops | bytes accessed | tf_op | source)
XLA Modules:
  0.0 76.5 jit_solution(3396046722302911328)
XLA Ops:
  0.6 3.0 %shard_map.75 = bf16[32,128,128]{2,1,0:T(8,128)(2,1)} custom-call(bf16[64,16,256]{2,1,0:T(8,128)(2,1)} %x_ref.1, bf16[64,16,256]{2,1,0:T(8,128)(2,1)} %cot_ref.1), custom_call_target="tpu_custom_call" | custom-call | tf_op jit(solution)/shard_map/pallas_call | solution.py:329
  3.6 0.0 copy-start
  3.6 7.3 %all-to-all-start = ((bf16[32,128,128]{2,1,0:T(8,128)(2,1)}), bf16[32,128,128]{2,1,0:T(8,128)(2,1)S(1)}, u32[]{:S(2)}, u32[]{:S(2)}) async-start(bf16[32,128,128]{2,1,0:T(8,128)(2,1)} %shard_map.75), calls=%async_computation | async-start | bytes 2097152 | tf_op jit(solution)/shard_map/all_to_all | solution.py:310
  10.9 0.0 copy-start.1
  10.9 0.7 copy-done.1
  11.6 0.1 copy.9.b_ref
  11.7 0.0 copy-done
  11.7 0.2 shard_map.76
  12.0 25.2 %all-to-all-done.parts_ref = bf16[32,128,128]{2,1,0:T(8,128)(2,1)S(1)} async-done(((bf16[32,128,128]{2,1,0:T(8,128)(2,1)}), bf16[32,128,128]{2,1,0:T(8,128)(2,1)S(1)}, u32[]{:S(2)}, u32[]{:S(2)}) %all-to-all-start) | async-done | bytes 1048608 | tf_op jit(solution)/shard_map/all_to_all | solution.py:310
  37.2 3.5 %shard_map.77 = (bf16[32,128,128]{2,1,0:T(8,128)(2,1)}, bf16[8,64,512]{2,1,0:T(8,128)(2,1)S(1)}, bf16[8,64,512]{2,1,0:T(8,128)(2,1)S(1)}) custom-call(bf16[32,128,128]{2,1,0:T(8,128)(2,1)S(1)} %all-to-all-done.parts_ref, bf16[192,192]{1,0:T(8,128)(2,1)S(1)} %get-tuple-element.20.first_ref, bf16[3,192,192]{2,1,0:T(8,128)(2,1)S(1)} %get-tuple-element.21.rest_ref, ...), custom_call_target="tpu_custom_call" | custom-call | tf_op jit(solution)/shard_map/pallas_call | solution.py:358
  40.7 3.6 %all-to-all-start.1 = ((bf16[32,128,128]{2,1,0:T(8,128)(2,1)}), bf16[32,128,128]{2,1,0:T(8,128)(2,1)S(1)}, u32[]{:S(2)}, u32[]{:S(2)}) async-start(bf16[32,128,128]{2,1,0:T(8,128)(2,1)} %get-tuple-element.26), calls=%async_computation.1 | async-start | bytes 2097152 | tf_op jit(solution)/shard_map/all_to_all | solution.py:310
  44.3 2.5 %shard_map.78 = (f32[304,128]{1,0:T(8,128)S(1)}, bf16[304,128]{1,0:T(8,128)(2,1)S(1)}) custom-call(bf16[32,128,128]{2,1,0:T(8,128)(2,1)S(1)} %all-to-all-done.parts_ref, bf16[192,192]{1,0:T(8,128)(2,1)S(1)} %get-tuple-element.20.first_ref, f32[2,64,1]{2,1,0:T(8,128)S(1)} %copy.9.b_ref, bf16[8,64,512]{2,1,0:T(8,128)(2,1)S(1)} %get-tuple-element.22.gz0_ref, ...), custom_call_target="tpu_custom_call" | custom-call | flops 301989888 | bytes 1572864 | tf_op jit(solution)/shard_map/pallas_call | solution.py:380
  46.8 0.3 collective-permute-start
  47.2 1.0 %collective-permute-done = bf16[304,128]{1,0:T(8,128)(2,1)S(1)} collective-permute-done((bf16[304,128]{1,0:T(8,128)(2,1)S(1)}, bf16[304,128]{1,0:T(8,128)(2,1)S(1)}, u32[]{:S(2)}, u32[]{:S(2)}) %collective-permute-start) | collective-permute-done | bytes 77856 | tf_op jit(solution)/shard_map/ppermute | solution.py:294
  48.2 1.8 %collective-permute-start.1 = (bf16[304,128]{1,0:T(8,128)(2,1)S(1)}, bf16[304,128]{1,0:T(8,128)(2,1)S(1)}, u32[]{:S(2)}, u32[]{:S(2)}) collective-permute-start(bf16[304,128]{1,0:T(8,128)(2,1)S(1)} %add_convert_fusion.4), channel_id=1, source_target_pairs={{0,2},{1,3},{2,0},{3,1},{4,6},{5,7},{6,4},{7,5},{8,10},{9,11},{10,... | collective-permute-start | bytes 233480 | tf_op jit(solution)/shard_map/ppermute | solution.py:294
  50.0 6.6 %collective-permute-done.1 = bf16[304,128]{1,0:T(8,128)(2,1)S(1)} collective-permute-done((bf16[304,128]{1,0:T(8,128)(2,1)S(1)}, bf16[304,128]{1,0:T(8,128)(2,1)S(1)}, u32[]{:S(2)}, u32[]{:S(2)}) %collective-permute-start.1) | collective-permute-done | bytes 77856 | tf_op jit(solution)/shard_map/ppermute | solution.py:294
  56.7 2.6 %collective-permute-start.2 = (bf16[304,128]{1,0:T(8,128)(2,1)S(1)}, bf16[304,128]{1,0:T(8,128)(2,1)S(1)}, u32[]{:S(2)}, u32[]{:S(2)}) collective-permute-start(bf16[304,128]{1,0:T(8,128)(2,1)S(1)} %add_convert_fusion.3), channel_id=1, source_target_pairs={{0,4},{1,5},{2,6},{3,7},{4,0},{5,1},{6,2},{7,3},{8,12},{9,13},{10,... | collective-permute-start | bytes 233480 | tf_op jit(solution)/shard_map/ppermute | solution.py:294
  59.2 3.3 %collective-permute-done.2 = bf16[304,128]{1,0:T(8,128)(2,1)S(1)} collective-permute-done((bf16[304,128]{1,0:T(8,128)(2,1)S(1)}, bf16[304,128]{1,0:T(8,128)(2,1)S(1)}, u32[]{:S(2)}, u32[]{:S(2)}) %collective-permute-start.2) | collective-permute-done | bytes 77856 | tf_op jit(solution)/shard_map/ppermute | solution.py:294
  62.6 0.1 collective-permute-start.3
  62.6 4.6 %collective-permute-done.3 = bf16[304,128]{1,0:T(8,128)(2,1)S(1)} collective-permute-done((bf16[304,128]{1,0:T(8,128)(2,1)S(1)}, bf16[304,128]{1,0:T(8,128)(2,1)S(1)}, u32[]{:S(2)}, u32[]{:S(2)}) %collective-permute-start.3) | collective-permute-done | bytes 77856 | tf_op jit(solution)/shard_map/ppermute | solution.py:294
  67.2 1.4 %collective-permute-start.4 = (bf16[304,128]{1,0:T(8,128)(2,1)S(1)}, bf16[304,128]{1,0:T(8,128)(2,1)S(1)}, u32[]{:S(2)}, u32[]{:S(2)}) collective-permute-start(bf16[304,128]{1,0:T(8,128)(2,1)S(1)} %add_convert_fusion.1), channel_id=1, source_target_pairs={{0,16},{1,17},{2,18},{3,19},{4,20},{5,21},{6,22},{7,23},{8,24},{9,... | collective-permute-start | bytes 233480 | tf_op jit(solution)/shard_map/ppermute | solution.py:294
  68.6 4.1 %all-to-all-done.1.parts_ref = bf16[32,128,128]{2,1,0:T(8,128)(2,1)S(1)} async-done(((bf16[32,128,128]{2,1,0:T(8,128)(2,1)}), bf16[32,128,128]{2,1,0:T(8,128)(2,1)S(1)}, u32[]{:S(2)}, u32[]{:S(2)}) %all-to-all-start.1) | async-done | bytes 1048608 | tf_op jit(solution)/shard_map/all_to_all | solution.py:310
  72.7 1.3 %shard_map.79 = bf16[64,16,256]{2,1,0:T(8,128)(2,1)} custom-call(bf16[32,128,128]{2,1,0:T(8,128)(2,1)S(1)} %all-to-all-done.1.parts_ref), custom_call_target="tpu_custom_call" | custom-call | flops 134217728 | bytes 1048576 | tf_op jit(solution)/shard_map/pallas_call | solution.py:393
  74.0 0.0 collective-permute-done.4
  74.1 0.1 collective-permute-start.5
  74.2 1.3 %shard_map.80 = bf16[64,16,256]{2,1,0:T(8,128)(2,1)} custom-call(bf16[32,128,128]{2,1,0:T(8,128)(2,1)S(1)} %all-to-all-done.1.parts_ref), custom_call_target="tpu_custom_call" | custom-call | flops 134217728 | bytes 1048576 | tf_op jit(solution)/shard_map/pallas_call | solution.py:393
  75.5 0.0 collective-permute-done.5.other_ref
  75.5 1.0 %shard_map.81 = (f32[2,3,3,64,64]{4,3,2,1,0:T(8,128)}, f32[2,64]{1,0:T(2,128)}) custom-call(bf16[304,128]{1,0:T(8,128)(2,1)S(1)} %add_convert_fusion.mine_ref, bf16[304,128]{1,0:T(8,128)(2,1)S(1)} %collective-permute-done.5.other_ref), custom_call_target="tpu_custom_call" | custom-call | tf_op jit(solution)/shard_map/pallas_call | solution.py:412
  (5 shorter events, 0.1 us)
Async XLA Ops:
  3.6 8.1 %copy-start = (bf16[2,3,3,64,64]{4,3,2,1,0:T(8,128)(2,1)S(1)}, bf16[2,3,3,64,64]{4,3,2,1,0:T(8,128)(2,1)}, u32[]{:S(2)}) copy-start(bf16[2,3,3,64,64]{4,3,2,1,0:T(8,128)(2,1)} %w_ref) | copy-start | bytes 442372
  3.6 33.5 %all-to-all-start = ((bf16[32,128,128]{2,1,0:T(8,128)(2,1)}), bf16[32,128,128]{2,1,0:T(8,128)(2,1)S(1)}, u32[]{:S(2)}, u32[]{:S(2)}) async-start(bf16[32,128,128]{2,1,0:T(8,128)(2,1)} %shard_map.75), calls=%async_computation | async-start | bytes 2097152 | tf_op jit(solution)/shard_map/all_to_all | solution.py:310
  10.9 0.7 copy-start.1
  40.7 32.0 %all-to-all-start.1 = ((bf16[32,128,128]{2,1,0:T(8,128)(2,1)}), bf16[32,128,128]{2,1,0:T(8,128)(2,1)S(1)}, u32[]{:S(2)}, u32[]{:S(2)}) async-start(bf16[32,128,128]{2,1,0:T(8,128)(2,1)} %get-tuple-element.26), calls=%async_computation.1 | async-start | bytes 2097152 | tf_op jit(solution)/shard_map/all_to_all | solution.py:310
  46.8 1.3 %collective-permute-start = (bf16[304,128]{1,0:T(8,128)(2,1)S(1)}, bf16[304,128]{1,0:T(8,128)(2,1)S(1)}, u32[]{:S(2)}, u32[]{:S(2)}) collective-permute-start(bf16[304,128]{1,0:T(8,128)(2,1)S(1)} %get-tuple-element.25), channel_id=1, source_target_pairs={{0,1},{1,0},{2,3},{3,2},{4,5},{5,4},{6,7},{7,6},{8,9},{9,8},{10,11... | collective-permute-start | bytes 233480 | tf_op jit(solution)/shard_map/ppermute | solution.py:294
  48.2 8.4 %collective-permute-start.1 = (bf16[304,128]{1,0:T(8,128)(2,1)S(1)}, bf16[304,128]{1,0:T(8,128)(2,1)S(1)}, u32[]{:S(2)}, u32[]{:S(2)}) collective-permute-start(bf16[304,128]{1,0:T(8,128)(2,1)S(1)} %add_convert_fusion.4), channel_id=1, source_target_pairs={{0,2},{1,3},{2,0},{3,1},{4,6},{5,7},{6,4},{7,5},{8,10},{9,11},{10,... | collective-permute-start | bytes 233480 | tf_op jit(solution)/shard_map/ppermute | solution.py:294
  56.7 5.9 %collective-permute-start.2 = (bf16[304,128]{1,0:T(8,128)(2,1)S(1)}, bf16[304,128]{1,0:T(8,128)(2,1)S(1)}, u32[]{:S(2)}, u32[]{:S(2)}) collective-permute-start(bf16[304,128]{1,0:T(8,128)(2,1)S(1)} %add_convert_fusion.3), channel_id=1, source_target_pairs={{0,4},{1,5},{2,6},{3,7},{4,0},{5,1},{6,2},{7,3},{8,12},{9,13},{10,... | collective-permute-start | bytes 233480 | tf_op jit(solution)/shard_map/ppermute | solution.py:294
  62.6 4.6 %collective-permute-start.3 = (bf16[304,128]{1,0:T(8,128)(2,1)S(1)}, bf16[304,128]{1,0:T(8,128)(2,1)S(1)}, u32[]{:S(2)}, u32[]{:S(2)}) collective-permute-start(bf16[304,128]{1,0:T(8,128)(2,1)S(1)} %add_convert_fusion.2), channel_id=1, source_target_pairs={{0,8},{1,9},{2,10},{3,11},{4,12},{5,13},{6,14},{7,15},{8,0},{9,1},... | collective-permute-start | bytes 233480 | tf_op jit(solution)/shard_map/ppermute | solution.py:294
  67.2 6.8 %collective-permute-start.4 = (bf16[304,128]{1,0:T(8,128)(2,1)S(1)}, bf16[304,128]{1,0:T(8,128)(2,1)S(1)}, u32[]{:S(2)}, u32[]{:S(2)}) collective-permute-start(bf16[304,128]{1,0:T(8,128)(2,1)S(1)} %add_convert_fusion.1), channel_id=1, source_target_pairs={{0,16},{1,17},{2,18},{3,19},{4,20},{5,21},{6,22},{7,23},{8,24},{9,... | collective-permute-start | bytes 233480 | tf_op jit(solution)/shard_map/ppermute | solution.py:294
  74.1 1.4 %collective-permute-start.5 = (bf16[304,128]{1,0:T(8,128)(2,1)S(1)}, bf16[304,128]{1,0:T(8,128)(2,1)S(1)}, u32[]{:S(2)}, u32[]{:S(2)}) collective-permute-start(bf16[304,128]{1,0:T(8,128)(2,1)S(1)} %add_convert_fusion.mine_ref), channel_id=1, source_target_pairs={{0,1},{1,0},{2,3},{3,2},{4,5},{5,4},{6,7},{7,6},{8,9},{9,8},{10,11... | collective-permute-start | bytes 233480 | tf_op jit(solution)/shard_map/ppermute | solution.py:294

commit v10 on v9

--- a/solution.py
+++ b/solution.py
@@ -228,7 +228,10 @@
                 gz0_ref[i] = (g.astype(F32) * s0_ref[i]).astype(BF16)
             else:
                 put(1, i, g)
-                send(1, i, 1)
+                if count % 2:
+                    send(1, i, 1)
+                elif i % 2:
+                    send(1, i - 1, 2)
     for started in copies:
         started.wait()
 

time: 76.9 us -> 76.9 us (level)
  no operation moved by 1% of the time
where the time goes in v10:
time: 76.9 us; the launch traced here: 76.5 us
  waiting for transfers between devices  44.8 us (58%)
  starting transfers between devices  17.2 us (22%)
  Pallas kernels  12.9 us (17%)
  local copies, waits for them, and re-layouts  0.78 us (1%)
  between operations  0.78 us (1%)
    all_to_all x2, waiting for transfers between devices, exchanged(): return lax.all_to_all(parts, AXES, 0, 0, tiled=True)  29.3 us
    ppermute x6, waiting for transfers between devices, partnered(): return lax.ppermute(block, AXES, [(i, i ^ bit) for i in range(devices)])  15.5 us
    all_to_all x2, starting transfers between devices, exchanged(): return lax.all_to_all(parts, AXES, 0, 0, tiled=True)  10.9 us
    ppermute x6, starting transfers between devices, partnered(): return lax.ppermute(block, AXES, [(i, i ^ bit) for i in range(devices)])  6.23 us
    pallas_call x1, Pallas kernels, local(): pl.pallas_call(functools.partial(stack_kernel, share), out_shape=[shape(p...  3.53 us
    pallas_call x1, Pallas kernels, local(): pl.pallas_call(functools.partial(pack_kernel, share), out_shape=shape(fie...  2.97 us
    pallas_call x2, Pallas kernels, unpacked(): pl.pallas_call(functools.partial(unpack_kernel, share, field), out_shape=...  2.62 us
    pallas_call x1, Pallas kernels, local(): pl.pallas_call(functools.partial(sums_kernel, share), out_shape=[shape(ha...  2.49 us
  transfers between devices with their start and end apart: 8, of which 6 were waited for; matrix products, arithmetic and copies ran while one was open for 0% of the time, Pallas kernels for 7%

profile of v10, /device:TPU:0, one launch (start us, length us, event | category | flops | bytes accessed | tf_op | source)
XLA Modules:
  0.0 76.5 jit_solution(5720367619799907553)
XLA Ops:
  0.6 3.0 %shard_map.75 = bf16[32,128,128]{2,1,0:T(8,128)(2,1)} custom-call(bf16[64,16,256]{2,1,0:T(8,128)(2,1)} %x_ref.1, bf16[64,16,256]{2,1,0:T(8,128)(2,1)} %cot_ref.1), custom_call_target="tpu_custom_call" | custom-call | tf_op jit(solution)/shard_map/pallas_call | solution.py:332
  3.6 0.0 copy-start
  3.6 7.3 %all-to-all-start = ((bf16[32,128,128]{2,1,0:T(8,128)(2,1)}), bf16[32,128,128]{2,1,0:T(8,128)(2,1)S(1)}, u32[]{:S(2)}, u32[]{:S(2)}) async-start(bf16[32,128,128]{2,1,0:T(8,128)(2,1)} %shard_map.75), calls=%async_computation | async-start | bytes 2097152 | tf_op jit(solution)/shard_map/all_to_all | solution.py:313
  10.9 0.0 copy-start.1
  10.9 0.7 copy-done.1
  11.6 0.1 copy.9.b_ref
  11.7 0.0 copy-done
  11.7 0.2 shard_map.76
  12.0 25.2 %all-to-all-done.parts_ref = bf16[32,128,128]{2,1,0:T(8,128)(2,1)S(1)} async-done(((bf16[32,128,128]{2,1,0:T(8,128)(2,1)}), bf16[32,128,128]{2,1,0:T(8,128)(2,1)S(1)}, u32[]{:S(2)}, u32[]{:S(2)}) %all-to-all-start) | async-done | bytes 1048608 | tf_op jit(solution)/shard_map/all_to_all | solution.py:313
  37.2 3.5 %shard_map.77 = (bf16[32,128,128]{2,1,0:T(8,128)(2,1)}, bf16[8,64,512]{2,1,0:T(8,128)(2,1)S(1)}, bf16[8,64,512]{2,1,0:T(8,128)(2,1)S(1)}) custom-call(bf16[32,128,128]{2,1,0:T(8,128)(2,1)S(1)} %all-to-all-done.parts_ref, bf16[192,192]{1,0:T(8,128)(2,1)S(1)} %get-tuple-element.20.first_ref, bf16[3,192,192]{2,1,0:T(8,128)(2,1)S(1)} %get-tuple-element.21.rest_ref, ...), custom_call_target="tpu_custom_call" | custom-call | tf_op jit(solution)/shard_map/pallas_call | solution.py:361
  40.7 3.6 %all-to-all-start.1 = ((bf16[32,128,128]{2,1,0:T(8,128)(2,1)}), bf16[32,128,128]{2,1,0:T(8,128)(2,1)S(1)}, u32[]{:S(2)}, u32[]{:S(2)}) async-start(bf16[32,128,128]{2,1,0:T(8,128)(2,1)} %get-tuple-element.26), calls=%async_computation.1 | async-start | bytes 2097152 | tf_op jit(solution)/shard_map/all_to_all | solution.py:313
  44.3 2.5 %shard_map.78 = (f32[304,128]{1,0:T(8,128)S(1)}, bf16[304,128]{1,0:T(8,128)(2,1)S(1)}) custom-call(bf16[32,128,128]{2,1,0:T(8,128)(2,1)S(1)} %all-to-all-done.parts_ref, bf16[192,192]{1,0:T(8,128)(2,1)S(1)} %get-tuple-element.20.first_ref, f32[2,64,1]{2,1,0:T(8,128)S(1)} %copy.9.b_ref, bf16[8,64,512]{2,1,0:T(8,128)(2,1)S(1)} %get-tuple-element.22.gz0_ref, ...), custom_call_target="tpu_custom_call" | custom-call | flops 301989888 | bytes 1572864 | tf_op jit(solution)/shard_map/pallas_call | solution.py:383
  46.8 0.3 collective-permute-start
  47.2 1.0 %collective-permute-done = bf16[304,128]{1,0:T(8,128)(2,1)S(1)} collective-permute-done((bf16[304,128]{1,0:T(8,128)(2,1)S(1)}, bf16[304,128]{1,0:T(8,128)(2,1)S(1)}, u32[]{:S(2)}, u32[]{:S(2)}) %collective-permute-start) | collective-permute-done | bytes 77856 | tf_op jit(solution)/shard_map/ppermute | solution.py:297
  48.2 1.8 %collective-permute-start.1 = (bf16[304,128]{1,0:T(8,128)(2,1)S(1)}, bf16[304,128]{1,0:T(8,128)(2,1)S(1)}, u32[]{:S(2)}, u32[]{:S(2)}) collective-permute-start(bf16[304,128]{1,0:T(8,128)(2,1)S(1)} %add_convert_fusion.4), channel_id=1, source_target_pairs={{0,2},{1,3},{2,0},{3,1},{4,6},{5,7},{6,4},{7,5},{8,10},{9,11},{10,... | collective-permute-start | bytes 233480 | tf_op jit(solution)/shard_map/ppermute | solution.py:297
  50.0 6.6 %collective-permute-done.1 = bf16[304,128]{1,0:T(8,128)(2,1)S(1)} collective-permute-done((bf16[304,128]{1,0:T(8,128)(2,1)S(1)}, bf16[304,128]{1,0:T(8,128)(2,1)S(1)}, u32[]{:S(2)}, u32[]{:S(2)}) %collective-permute-start.1) | collective-permute-done | bytes 77856 | tf_op jit(solution)/shard_map/ppermute | solution.py:297
  56.7 2.6 %collective-permute-start.2 = (bf16[304,128]{1,0:T(8,128)(2,1)S(1)}, bf16[304,128]{1,0:T(8,128)(2,1)S(1)}, u32[]{:S(2)}, u32[]{:S(2)}) collective-permute-start(bf16[304,128]{1,0:T(8,128)(2,1)S(1)} %add_convert_fusion.3), channel_id=1, source_target_pairs={{0,4},{1,5},{2,6},{3,7},{4,0},{5,1},{6,2},{7,3},{8,12},{9,13},{10,... | collective-permute-start | bytes 233480 | tf_op jit(solution)/shard_map/ppermute | solution.py:297
  59.2 3.3 %collective-permute-done.2 = bf16[304,128]{1,0:T(8,128)(2,1)S(1)} collective-permute-done((bf16[304,128]{1,0:T(8,128)(2,1)S(1)}, bf16[304,128]{1,0:T(8,128)(2,1)S(1)}, u32[]{:S(2)}, u32[]{:S(2)}) %collective-permute-start.2) | collective-permute-done | bytes 77856 | tf_op jit(solution)/shard_map/ppermute | solution.py:297
  62.6 0.1 collective-permute-start.3
  62.6 4.6 %collective-permute-done.3 = bf16[304,128]{1,0:T(8,128)(2,1)S(1)} collective-permute-done((bf16[304,128]{1,0:T(8,128)(2,1)S(1)}, bf16[304,128]{1,0:T(8,128)(2,1)S(1)}, u32[]{:S(2)}, u32[]{:S(2)}) %collective-permute-start.3) | collective-permute-done | bytes 77856 | tf_op jit(solution)/shard_map/ppermute | solution.py:297
  67.2 1.4 %collective-permute-start.4 = (bf16[304,128]{1,0:T(8,128)(2,1)S(1)}, bf16[304,128]{1,0:T(8,128)(2,1)S(1)}, u32[]{:S(2)}, u32[]{:S(2)}) collective-permute-start(bf16[304,128]{1,0:T(8,128)(2,1)S(1)} %add_convert_fusion.1), channel_id=1, source_target_pairs={{0,16},{1,17},{2,18},{3,19},{4,20},{5,21},{6,22},{7,23},{8,24},{9,... | collective-permute-start | bytes 233480 | tf_op jit(solution)/shard_map/ppermute | solution.py:297
  68.6 4.1 %all-to-all-done.1.parts_ref = bf16[32,128,128]{2,1,0:T(8,128)(2,1)S(1)} async-done(((bf16[32,128,128]{2,1,0:T(8,128)(2,1)}), bf16[32,128,128]{2,1,0:T(8,128)(2,1)S(1)}, u32[]{:S(2)}, u32[]{:S(2)}) %all-to-all-start.1) | async-done | bytes 1048608 | tf_op jit(solution)/shard_map/all_to_all | solution.py:313
  72.7 1.3 %shard_map.79 = bf16[64,16,256]{2,1,0:T(8,128)(2,1)} custom-call(bf16[32,128,128]{2,1,0:T(8,128)(2,1)S(1)} %all-to-all-done.1.parts_ref), custom_call_target="tpu_custom_call" | custom-call | flops 134217728 | bytes 1048576 | tf_op jit(solution)/shard_map/pallas_call | solution.py:396
  74.0 0.0 collective-permute-done.4
  74.1 0.1 collective-permute-start.5
  74.2 1.3 %shard_map.80 = bf16[64,16,256]{2,1,0:T(8,128)(2,1)} custom-call(bf16[32,128,128]{2,1,0:T(8,128)(2,1)S(1)} %all-to-all-done.1.parts_ref), custom_call_target="tpu_custom_call" | custom-call | flops 134217728 | bytes 1048576 | tf_op jit(solution)/shard_map/pallas_call | solution.py:396
  75.5 0.0 collective-permute-done.5.other_ref
  75.5 1.0 %shard_map.81 = (f32[2,3,3,64,64]{4,3,2,1,0:T(8,128)}, f32[2,64]{1,0:T(2,128)}) custom-call(bf16[304,128]{1,0:T(8,128)(2,1)S(1)} %add_convert_fusion.mine_ref, bf16[304,128]{1,0:T(8,128)(2,1)S(1)} %collective-permute-done.5.other_ref), custom_call_target="tpu_custom_call" | custom-call | tf_op jit(solution)/shard_map/pallas_call | solution.py:415
  (5 shorter events, 0.1 us)
Async XLA Ops:
  3.6 8.1 %copy-start = (bf16[2,3,3,64,64]{4,3,2,1,0:T(8,128)(2,1)S(1)}, bf16[2,3,3,64,64]{4,3,2,1,0:T(8,128)(2,1)}, u32[]{:S(2)}) copy-start(bf16[2,3,3,64,64]{4,3,2,1,0:T(8,128)(2,1)} %w_ref) | copy-start | bytes 442372
  3.6 33.5 %all-to-all-start = ((bf16[32,128,128]{2,1,0:T(8,128)(2,1)}), bf16[32,128,128]{2,1,0:T(8,128)(2,1)S(1)}, u32[]{:S(2)}, u32[]{:S(2)}) async-start(bf16[32,128,128]{2,1,0:T(8,128)(2,1)} %shard_map.75), calls=%async_computation | async-start | bytes 2097152 | tf_op jit(solution)/shard_map/all_to_all | solution.py:313
  10.9 0.7 copy-start.1
  40.7 32.0 %all-to-all-start.1 = ((bf16[32,128,128]{2,1,0:T(8,128)(2,1)}), bf16[32,128,128]{2,1,0:T(8,128)(2,1)S(1)}, u32[]{:S(2)}, u32[]{:S(2)}) async-start(bf16[32,128,128]{2,1,0:T(8,128)(2,1)} %get-tuple-element.26), calls=%async_computation.1 | async-start | bytes 2097152 | tf_op jit(solution)/shard_map/all_to_all | solution.py:313
  46.8 1.3 %collective-permute-start = (bf16[304,128]{1,0:T(8,128)(2,1)S(1)}, bf16[304,128]{1,0:T(8,128)(2,1)S(1)}, u32[]{:S(2)}, u32[]{:S(2)}) collective-permute-start(bf16[304,128]{1,0:T(8,128)(2,1)S(1)} %get-tuple-element.25), channel_id=1, source_target_pairs={{0,1},{1,0},{2,3},{3,2},{4,5},{5,4},{6,7},{7,6},{8,9},{9,8},{10,11... | collective-permute-start | bytes 233480 | tf_op jit(solution)/shard_map/ppermute | solution.py:297
  48.2 8.4 %collective-permute-start.1 = (bf16[304,128]{1,0:T(8,128)(2,1)S(1)}, bf16[304,128]{1,0:T(8,128)(2,1)S(1)}, u32[]{:S(2)}, u32[]{:S(2)}) collective-permute-start(bf16[304,128]{1,0:T(8,128)(2,1)S(1)} %add_convert_fusion.4), channel_id=1, source_target_pairs={{0,2},{1,3},{2,0},{3,1},{4,6},{5,7},{6,4},{7,5},{8,10},{9,11},{10,... | collective-permute-start | bytes 233480 | tf_op jit(solution)/shard_map/ppermute | solution.py:297
  56.7 5.9 %collective-permute-start.2 = (bf16[304,128]{1,0:T(8,128)(2,1)S(1)}, bf16[304,128]{1,0:T(8,128)(2,1)S(1)}, u32[]{:S(2)}, u32[]{:S(2)}) collective-permute-start(bf16[304,128]{1,0:T(8,128)(2,1)S(1)} %add_convert_fusion.3), channel_id=1, source_target_pairs={{0,4},{1,5},{2,6},{3,7},{4,0},{5,1},{6,2},{7,3},{8,12},{9,13},{10,... | collective-permute-start | bytes 233480 | tf_op jit(solution)/shard_map/ppermute | solution.py:297
  62.6 4.6 %collective-permute-start.3 = (bf16[304,128]{1,0:T(8,128)(2,1)S(1)}, bf16[304,128]{1,0:T(8,128)(2,1)S(1)}, u32[]{:S(2)}, u32[]{:S(2)}) collective-permute-start(bf16[304,128]{1,0:T(8,128)(2,1)S(1)} %add_convert_fusion.2), channel_id=1, source_target_pairs={{0,8},{1,9},{2,10},{3,11},{4,12},{5,13},{6,14},{7,15},{8,0},{9,1},... | collective-permute-start | bytes 233480 | tf_op jit(solution)/shard_map/ppermute | solution.py:297
  67.2 6.8 %collective-permute-start.4 = (bf16[304,128]{1,0:T(8,128)(2,1)S(1)}, bf16[304,128]{1,0:T(8,128)(2,1)S(1)}, u32[]{:S(2)}, u32[]{:S(2)}) collective-permute-start(bf16[304,128]{1,0:T(8,128)(2,1)S(1)} %add_convert_fusion.1), channel_id=1, source_target_pairs={{0,16},{1,17},{2,18},{3,19},{4,20},{5,21},{6,22},{7,23},{8,24},{9,... | collective-permute-start | bytes 233480 | tf_op jit(solution)/shard_map/ppermute | solution.py:297
  74.1 1.4 %collective-permute-start.5 = (bf16[304,128]{1,0:T(8,128)(2,1)S(1)}, bf16[304,128]{1,0:T(8,128)(2,1)S(1)}, u32[]{:S(2)}, u32[]{:S(2)}) collective-permute-start(bf16[304,128]{1,0:T(8,128)(2,1)S(1)} %add_convert_fusion.mine_ref), channel_id=1, source_target_pairs={{0,1},{1,0},{2,3},{3,2},{4,5},{5,4},{6,7},{7,6},{8,9},{9,8},{10,11... | collective-permute-start | bytes 233480 | tf_op jit(solution)/shard_map/ppermute | solution.py:297
